TPU v7x, 1024 devices: a whole 4x4x32 slice. The times are simulated.
1024 devices in a mesh: dp: 64 (over y, z_lo, core), col: 16 (over x, z_hi).
Axes of the slice: x: 4, y: 4, z: 32 (z_hi: 4, z_lo: 8; z = z_hi * 8 + z_lo), core: 2. Of those that a mesh axis runs over, the one named last changes fastest.
Arguments:
- embedded: bfloat16 [32768, 2048], P('dp', 'col'), may hold values from -6 to 6
- gate: bfloat16 [32768, 2048], P('dp', 'col'), may hold values from -6 to 6
- pre_hidden: bfloat16 [32768, 4096], P('dp', 'col'), may hold values from -6 to 6
- hidden_weight: bfloat16 [2048, 4096], P(None, 'col'), may hold values from -0.125 to 0.125
- cross_weight: bfloat16 [2048, 2048], P('col'), may hold values from -0.125 to 0.125
- out_weight: bfloat16 [4096], P('col'), may hold values from -5 to 5
- upstream: float32 [32768], P('dp'), may hold values from -6 to 6
- hot_rows: int32 [262144, 2], P('dp'), may hold values from 0 to 511
- cold_owner: int32 [262144, 2], P('dp'), may hold values from 0 to 63, as said below
- cold_rows: int32 [262144, 2], P('dp'), may hold values from 0 to 511
- hot_flag: int32 [262144, 2], P('dp'), may hold values from 0 to 1
- bag_sizes: int32 [262144], P('dp'), may hold values from 1 to 2
Outputs:
- hot_grad: float32 [256, 512], P('col', 'dp')
- cold_grad: float32 [256, 32768], P('col', 'dp')
Inputs may be any that keep to these rules, and one draw needn't show every extreme that they name: `cold_owner`: the slots of a bag name different owners; among the slots of one device's 512 samples no owner is named more than 160 times; one owner, the same for every device, is named exactly 160 times by each device's slots, and every slot that names it is live (its bag holds 2 ids) and has hot_flag 0.
All inputs are finite; a program needn't handle non-finite values.
Results may differ from a plain program's by a relative error of at most 0.025.
Values may be sent and summed in bfloat16 or wider, within the bound.
No kernel may reach another device: no remote copies, remote signals or barrier semaphores. Data moves between devices by JAX's collectives and lax.ppermute only.
A program may use at most 128 MiB of HBM per device.

v0:
```python
import jax
import jax.numpy as jnp
from jax import lax
from jax.sharding import PartitionSpec as P

F = 8
HOT = 512
COLD_DEV = 512


def local(
    embedded,
    gate,
    pre_hidden,
    hidden_weight,
    cross_weight,
    out_weight,
    upstream,
    hot_rows,
    cold_owner,
    cold_rows,
    hot_flag,
    bag_sizes,
):
    owners = lax.axis_size("dp")
    sample_rows = embedded.shape[0]
    width_local = embedded.shape[1]
    slope_rows = jnp.where(
        pre_hidden > 0, upstream[:, None] * out_weight.astype(jnp.float32)[None, :], 0.0
    ).astype(jnp.bfloat16)
    back_one = lax.psum_scatter(
        lax.dot_general(
            hidden_weight, slope_rows, (((1,), (1,)), ((), ())), preferred_element_type=jnp.float32
        ).astype(jnp.bfloat16),
        "col",
        scatter_dimension=0,
        tiled=True,
    ).astype(jnp.float32)
    gated_prod = (back_one * embedded.T.astype(jnp.float32)).astype(jnp.bfloat16)
    crossed = lax.psum_scatter(
        lax.dot_general(
            cross_weight, gated_prod, (((0,), (0,)), ((), ())), preferred_element_type=jnp.float32
        ).astype(jnp.bfloat16),
        "col",
        scatter_dimension=0,
        tiled=True,
    ).astype(jnp.float32)
    grad_cols = (back_one * (gate.T.astype(jnp.float32) + 1.0) + crossed).astype(jnp.bfloat16)
    emb_cols = width_local // F
    slot_width = hot_rows.shape[1]
    vectors = (
        grad_cols.reshape(emb_cols, F, sample_rows)
        .transpose(2, 1, 0)
        .reshape(sample_rows * F, 1, emb_cols)
    )
    values = jnp.broadcast_to(vectors, (sample_rows * F, slot_width, emb_cols)).reshape(
        -1, emb_cols
    )
    slot_index = lax.broadcasted_iota(jnp.int32, hot_rows.shape, 1)
    active = slot_index < bag_sizes[:, None]
    is_hot = active & (hot_flag == 1)
    is_cold = active & (hot_flag == 0)
    hot_index = jnp.where(is_hot, hot_rows, HOT).reshape(-1)
    hot_local = jax.ops.segment_sum(values.astype(jnp.float32), hot_index, HOT + 1)[:HOT].T
    summed_hot = lax.psum(hot_local, "dp")
    hot_share = HOT // owners
    hot_grad = lax.dynamic_slice_in_dim(summed_hot, lax.axis_index("dp") * hot_share, hot_share, 1)
    slot_count = values.shape[0]
    capacity = max(2, (5 * slot_count + 4 * owners - 1) // (4 * owners))
    owner_flat = cold_owner.reshape(-1)
    cold_flat = is_cold.reshape(-1)
    owner_ids = lax.broadcasted_iota(jnp.int32, (1, owners), 1)
    owner_match = ((owner_flat[:, None] == owner_ids) & cold_flat[:, None]).astype(jnp.int32)
    earlier = jnp.cumsum(owner_match, axis=0) - owner_match
    position = jnp.sum(earlier * owner_match, axis=1)
    target_slot = jnp.where(cold_flat, owner_flat * capacity + position, owners * capacity)
    send_values = (
        jnp.zeros((owners * capacity + 1, emb_cols), jnp.bfloat16)
        .at[target_slot]
        .set(values)[:-1]
        .reshape(owners, capacity, emb_cols)
    )
    send_rows = (
        jnp.full((owners * capacity + 1,), COLD_DEV, jnp.int32)
        .at[target_slot]
        .set(cold_rows.reshape(-1))[:-1]
        .reshape(owners, capacity)
    )
    got_values, got_rows = (
        lax.all_to_all(send_values, "dp", split_axis=0, concat_axis=0, tiled=True),
        lax.all_to_all(send_rows, "dp", split_axis=0, concat_axis=0, tiled=True),
    )
    cold_grad = jax.ops.segment_sum(
        got_values.reshape(-1, emb_cols).astype(jnp.float32), got_rows.reshape(-1), COLD_DEV + 1
    )[:-1].T
    return (hot_grad, cold_grad)


def solution(mesh):
    in_specs = (
        P("dp", "col"),
        P("dp", "col"),
        P("dp", "col"),
        P(None, "col"),
        P("col", None),
        P("col"),
        P("dp"),
        P("dp", None),
        P("dp", None),
        P("dp", None),
        P("dp", None),
        P("dp"),
    )
    out_specs = (P("col", "dp"), P("col", "dp"))
    return jax.shard_map(local, mesh=mesh, in_specs=in_specs, out_specs=out_specs, check_vma=False)
```

profile of v0, /device:TPU:1, one launch (start us, length us, event | category | flops | bytes accessed | tf_op | source)
XLA Modules:
  0.0 1037.7 jit_solution(15555062581613864968)
XLA Ops:
  8.4 1.7 fusion.2
  10.1 2.5 copy.59
  13.7 224.5 %reduce-scatter.7.cloned.1.call-done = bf16[128,512]{1,0:T(8,128)(2,1)} async-done(((bf16[2048,512]{1,0:T(8,128)(2,1)}), bf16[128,512]{1,0:T(8,128)(2,1)}) %reduce-scatter.7.cloned.1.call-update) | async-done | bytes 131088 | tf_op jit(solution)/shard_map/reduce_scatter | solution.py:31
  238.1 1.8 fusion.3
  240.0 2.5 copy.61
  244.2 1.6 and.30
  245.7 1.6 and.27
  247.3 1.6 reshape.96
  249.5 1.2 eq.45
  250.7 1.2 eq.41
  252.6 1.4 mul.49
  254.1 1.6 fusion.9
  255.6 34.1 %reduce-window.6 = s32[64,64,128]{2,1,0:T(8,128)S(1)} reduce-window(s32[64,64,128]{2,1,0:T(8,128)} %fusion.9, s32[]{:T(128)} %constant.17.clone.1), window={size=1x1x128 pad=0_0x0_0x127_0}, to_apply=%region_4.5 | reduce-window | flops 66584576 | bytes 4194308 | tf_op jit(solution)/shard_map/reduce-window
  289.8 1.7 slice_reduce_fusion
  291.7 2.0 copy.53
  293.7 2.7 reshape.113
  297.2 1.9 fusion.6
  299.2 30.5 %scatter_custom_fusion.1 = s32[10241]{0:T(1024)S(1)} fusion(s32[8192]{0:T(1024)S(1)} %bitcast.57, s32[8192]{0:T(1024)S(1)} %reshape.113, s32[]{:T(128)} %constant.14.clone.1), kind=kCustom, calls=%fused_computation.43 | custom fusion | bytes 40968 | tf_op jit(solution)/shard_map/scatter | solution.py:86
  330.4 10.9 %all-to-all-start = ((s32[64,1,160]{2,1,0:T(1,128)}), s32[64,1,160]{2,1,0:T(1,128)S(1)}, u32[]{:S(2)}, u32[]{:S(2)}) async-start(s32[64,1,160]{2,1,0:T(1,128)} %all_to_all.9), calls=%async_computation | async-start | bytes 131072 | tf_op jit(solution)/shard_map/all_to_all | solution.py:91
  341.5 104.7 %reduce-scatter.9.cloned.1.call-done = bf16[128,512]{1,0:T(8,128)(2,1)} async-done(((bf16[2048,512]{1,0:T(8,128)(2,1)}), bf16[128,512]{1,0:T(8,128)(2,1)}) %reduce-scatter.9.cloned.1.call-update) | async-done | bytes 131088 | tf_op jit(solution)/shard_map/reduce_scatter | solution.py:40
  447.2 1.7 copy.46
  448.9 2.8 broadcast_in_dim.33
  451.7 22.9 %scatter_custom_fusion.2 = bf16[10241,16]{1,0:T(8,128)(2,1)} fusion(s32[8192]{0:T(1024)S(1)} %bitcast.58, bf16[8192,16]{1,0:T(8,128)(2,1)S(1)} %bitcast.50, bf16[]{:T(256)} %constant.15.clone.1), kind=kCustom, calls=%fused_computation.20 | custom fusion | bytes 327714 | tf_op jit(solution)/shard_map/scatter | solution.py:80
  474.6 2.9 slice.28
  477.5 3.2 copy.54
  480.7 11.3 %all-to-all-start.1 = ((bf16[64,160,16]{1,2,0:T(8,128)(2,1)}), bf16[64,160,16]{1,2,0:T(8,128)(2,1)}, u32[]{:S(2)}, u32[]{:S(2)}) async-start(bf16[64,160,16]{1,2,0:T(8,128)(2,1)} %copy.54), calls=%async_computation.1 | async-start | bytes 1048576 | tf_op jit(solution)/shard_map/all_to_all | solution.py:90
  492.1 2.0 copy.41
  494.1 2.7 reshape.103
  497.1 47.6 %scatter_custom_fusion = f32[513,16]{1,0:T(8,128)S(1)} fusion(s32[8192]{0:T(1024)S(1)} %reshape.103, bf16[8192,16]{1,0:T(8,128)(2,1)S(1)} %bitcast.51, f32[]{:T(128)} %constant.12.clone.1), kind=kCustom, calls=%fused_computation.4 | custom fusion | flops 262144 | bytes 2129988 | tf_op jit(solution)/shard_map/scatter-add | solution.py:64
  544.7 418.7 %psum.7 = f32[16,512]{0,1:T(8,128)S(1)} all-reduce(f32[16,512]{0,1:T(8,128)S(1)} %slice_bitcast_fusion.1), channel_id=1, replica_groups=mesh['dp'=64,'col'=16] {'dp'}, use_global_device_ids=true, to_apply=%region_3.4 | all-reduce | flops 8192 | bytes 65536 | tf_op jit(solution)/shard_map/psum | solution.py:65
  964.0 3.7 copy.58
  967.7 62.4 %scatter_custom_fusion.3 = f32[513,16]{1,0:T(8,128)S(1)} fusion(s32[10240]{0:T(1024)S(1)} %reshape.127, f32[10240,16]{1,0:T(8,128)} %bitcast.53, f32[]{:T(128)} %constant.12.clone.1), kind=kCustom, calls=%fused_computation.35 | custom fusion | flops 163840 | bytes 33344 | tf_op jit(solution)/shard_map/scatter-add | solution.py:93
  (45 shorter events, 9.7 us)
Async XLA Ops:
  7.2 1.2 copy-start
  7.2 231.0 %reduce-scatter.7.cloned.1.call-start = ((), (), s32[]{:S(2)}) async-start(), calls=%async_computation.4 | async-start | bytes 2228224 | tf_op jit(solution)/shard_map/reduce_scatter | solution.py:31
  12.6 0.9 copy-start.4
  12.7 433.5 %reduce-scatter.9.cloned.1.call-start = ((), (), s32[]{:S(2)}) async-start(), calls=%async_computation.5 | async-start | bytes 2228224 | tf_op jit(solution)/shard_map/reduce_scatter | solution.py:40
  242.5 0.8 copy-start.3
  242.5 0.8 copy-start.6
  242.5 6.4 copy-start.2
  289.8 2.0 copy-start.7
  297.1 44.2 %copy-start.5 = (bf16[512,128]{1,0:T(8,128)(2,1)S(1)}, bf16[512,128]{1,0:T(8,128)(2,1)}, u32[]{:S(2)}) copy-start(bf16[512,128]{1,0:T(8,128)(2,1)} %param.13) | copy-start | bytes 393220
  297.1 149.0 %copy-start.1 = (bf16[128,512]{1,0:T(8,128)(2,1)S(1)}, bf16[128,512]{1,0:T(8,128)(2,1)}, u32[]{:S(2)}) copy-start(bf16[128,512]{1,0:T(8,128)(2,1)} %reduce-scatter.7.cloned.1.call-done) | copy-start | bytes 393220
  330.4 150.3 %all-to-all-start = ((s32[64,1,160]{2,1,0:T(1,128)}), s32[64,1,160]{2,1,0:T(1,128)S(1)}, u32[]{:S(2)}, u32[]{:S(2)}) async-start(s32[64,1,160]{2,1,0:T(1,128)} %all_to_all.9), calls=%async_computation | async-start | bytes 131072 | tf_op jit(solution)/shard_map/all_to_all | solution.py:91
  477.5 14.5 %copy-start.8 = (s32[4096,2]{0,1:T(2,128)S(1)}, s32[4096,2]{0,1:T(2,128)}, u32[]{:S(2)}) copy-start(s32[4096,2]{0,1:T(2,128)} %param.19) | copy-start | bytes 98308
  480.7 483.3 %all-to-all-start.1 = ((bf16[64,160,16]{1,2,0:T(8,128)(2,1)}), bf16[64,160,16]{1,2,0:T(8,128)(2,1)}, u32[]{:S(2)}, u32[]{:S(2)}) async-start(bf16[64,160,16]{1,2,0:T(8,128)(2,1)} %copy.54), calls=%async_computation.1 | async-start | bytes 1048576 | tf_op jit(solution)/shard_map/all_to_all | solution.py:90
Sparse Core Ops, SparseCore 0:
  13.3 224.7 reduce-scatter.6
  244.3 201.8 reduce-scatter.8
where the time goes:
time: 1050 us; the launch traced here: 1040 us
  blocking collectives  419 us (40%)
  waiting for transfers between devices  329 us (31%)
  other arithmetic  151 us (14%)
  local copies, waits for them, and re-layouts  99.1 us (9%)
  starting transfers between devices  22.3 us (2%)
  between operations  14.3 us (1%)
    psum x1, blocking collectives, local(): summed_hot = lax.psum(hot_local, 'dp')  419 us
    reduce_scatter x1, waiting for transfers between devices, local(): lax.psum_scatter(lax.dot_general(hidden_weight, slope_rows, (((1,), (1,))...  224 us
    reduce_scatter x1, waiting for transfers between devices, local(): lax.psum_scatter(lax.dot_general(cross_weight, gated_prod, (((0,), (0,)),...  105 us
    scatter-add x1, other arithmetic, local(): jax.ops.segment_sum(got_values.reshape(-1, emb_cols).astype(jnp.float32),...  62.4 us
    scatter-add x1, other arithmetic, local(): jax.ops.segment_sum(values.astype(jnp.float32), hot_index, HOT + 1)[:HOT]  47.6 us
    another operation x3, other arithmetic  35 us
    scatter x1, local copies, waits for them, and re-layouts, local(): send_rows = jnp.full((owners * capacity + 1,), COLD_DEV, jnp.int32).at[ta...  30.5 us
    scatter x1, local copies, waits for them, and re-layouts, local(): send_values = jnp.zeros((owners * capacity + 1, emb_cols), jnp.bfloat16)....  22.9 us
  transfers between devices with their start and end apart: 4, of which 2 were waited for; matrix products, arithmetic and copies ran while one was open for 17% of the time, Pallas kernels for 0%

commit v1 on v0

v1 whole, which is shorter than its diff:
```python
import jax
import jax.numpy as jnp
from jax import lax
from jax.experimental import pallas as pl
from jax.experimental.pallas import tpu as pltpu
from jax.sharding import PartitionSpec as P

F = 8
HOT = 512
COLD_DEV = 512
CAP = 160
SIDE = 4
MAIN = 128
TAIL = CAP - MAIN
LANES = 256
MSG_ROWS = 24
F32 = jnp.float32
BF16 = jnp.bfloat16
PIECES = ("far_lo", "far_hi", "up_lo", "up_hi", "down_lo", "down_hi", "own")

NT = (((1,), (1,)), ((), ()))
TN = (((0,), (0,)), ((), ()))
NN = (((1,), (0,)), ((), ()))


def mxu(a, b, dims):
    return lax.dot_general(a, b, dims, preferred_element_type=F32)


def iota(shape, axis):
    return lax.broadcasted_iota(jnp.int32, shape, axis)


def one_hot(match):
    return jnp.where(match, 1.0, 0.0).astype(BF16)


def call(kernel, out_shape, inputs, smem=(), scratch=(), flops=0, moved=0):
    vmem = pl.BlockSpec(memory_space=pltpu.VMEM)
    scalar = pl.BlockSpec(memory_space=pltpu.SMEM)
    return pl.pallas_call(
        kernel,
        out_shape=out_shape,
        in_specs=[scalar] * len(smem) + [vmem] * len(inputs),
        out_specs=jax.tree.map(lambda _: vmem, out_shape),
        scratch_shapes=list(scratch),
        compiler_params=pltpu.CompilerParams(vmem_limit_bytes=40 * 2**20),
        cost_estimate=pl.CostEstimate(flops=flops, bytes_accessed=moved, transcendentals=0),
    )(*smem, *inputs)


def piece_shapes(rows, lanes):
    half = jax.ShapeDtypeStruct((rows // 2, lanes), BF16)
    return [half] * 6 + [jax.ShapeDtypeStruct((rows, lanes), BF16)]


def store_pieces(make, here, refs):
    half = refs[0].shape[0]
    for step, lo, hi in ((2, 0, 1), (1, 2, 3), (3, 4, 5)):
        block = make(lax.rem(here + step, SIDE))
        refs[lo][...] = block[:half].astype(BF16)
        refs[hi][...] = block[half:].astype(BF16)
    refs[6][...] = make(here).astype(BF16)


def hidden_kernel(here, weight, pre_hidden, upstream, out_weight, *refs):
    slope = jnp.where(
        pre_hidden[...] > 0, upstream[...] * out_weight[...].astype(F32), 0.0
    ).astype(BF16)
    rows = refs[6].shape[0]

    def make(block):
        start = pl.multiple_of(block * rows, rows)
        return mxu(weight[pl.ds(start, rows), :], slope, NT)

    store_pieces(make, here[0], refs)


def joined(own, below_lo, below_hi, above_lo, above_hi):
    half = own.shape[0] // 2
    lo = own[:half].astype(F32) + below_lo[...].astype(F32) + above_lo[...].astype(F32)
    hi = own[half:].astype(F32) + below_hi[...].astype(F32) + above_hi[...].astype(F32)
    return lo, hi


def mid_kernel(here, own, below_lo, below_hi, above_lo, above_hi, *refs):
    total = refs[7]
    lo, hi = joined(own, below_lo, below_hi, above_lo, above_hi)
    half = lo.shape[0]
    total[:half, :] = lo.astype(BF16)
    total[half:, :] = hi.astype(BF16)
    rows = refs[6].shape[0]

    def make(block):
        return total[pl.ds(pl.multiple_of(block * rows, rows), rows), :]

    store_pieces(make, here[0], refs[:7])


def cross_kernel(
    here, own, below_lo, below_hi, above_lo, above_hi, embedded, weight, back_one, *refs
):
    lo, hi = joined(own, below_lo, below_hi, above_lo, above_hi)
    total = jnp.concatenate([lo, hi], axis=0)
    back_one[...] = total
    gated = (total * embedded[...].astype(F32).T).astype(BF16)
    rows = refs[6].shape[0]

    def make(block):
        start = pl.multiple_of(block * rows, rows)
        return mxu(weight[:, pl.ds(start, rows)], gated, TN)

    store_pieces(make, here[0], refs)


def plan_kernel(owner, rows, flag, bags, source, target, part_a, part_b, part_c):
    width = 512
    owners = source.shape[0]
    ahead = one_hot(iota((width, width), 0) < iota((width, width), 1))
    owner_ids = iota((owners, width), 0)
    lane_slot = iota((LANES, width), 0)
    slot_ids = jnp.where(lane_slot < MAIN, lane_slot, MAIN + lane_slot % TAIL).astype(F32)
    for part in (part_a, part_b, part_c):
        part[...] = jnp.zeros_like(part)

    def step(chunk, used):
        at = pl.ds(pl.multiple_of(chunk * width, width), width)
        bag = chunk * width + iota((1, width), 1)
        for k in range(owner.shape[0]):
            cold = (bags[:, at] > k) & (flag[k : k + 1, at] == 0)
            hit = (owner_ids == owner[k : k + 1, at]) & cold
            match = one_hot(hit)
            before = mxu(match, ahead, NN) + used
            place = jnp.sum(jnp.where(hit, before, 0.0), axis=0, keepdims=True)
            taken = slot_ids == place
            row = rows[k : k + 1, at]
            for part, value in (
                (part_a, (bag >> 6) + 1),
                (part_b, (bag & 63) * 2 + (row & 1)),
                (part_c, row >> 1),
            ):
                part[...] += mxu(match, jnp.where(taken, value.astype(F32), 0.0).astype(BF16), NT)
            used = used + jnp.sum(jnp.where(hit, 1.0, 0.0), axis=1, keepdims=True)
        return used

    lax.fori_loop(0, owner.shape[1] // width, step, jnp.zeros((owners, 1), F32))
    high = part_a[...].astype(jnp.int32)
    low = part_b[...].astype(jnp.int32)
    top = part_c[...].astype(jnp.int32)
    source[...] = jnp.where(high > 0, (high - 1) * 64 + (low >> 1), -1)
    target[...] = jnp.where(high > 0, top * 2 + (low & 1), COLD_DEV)


def send_kernel(
    own, below_lo, below_hi, above_lo, above_hi, back_one, gate, source, hot_index, out, hot_rows
):
    lo, hi = joined(own, below_lo, below_hi, above_lo, above_hi)
    crossed = jnp.concatenate([lo, hi], axis=0)
    grad = (back_one[...] * (gate[...].astype(F32).T + 1.0) + crossed).astype(BF16)
    cols, samples = grad.shape
    wide = cols // F
    row_id = iota((cols, cols), 0)
    grad = mxu(
        one_hot(iota((cols, cols), 1) == (row_id % wide) * F + row_id // wide), grad, NN
    ).astype(BF16)

    owners = source.shape[0]
    share = HOT // owners
    hot_ids = iota((HOT, samples), 0)
    summed = jnp.zeros((HOT, cols), F32)
    for f in range(F):
        count = jnp.where(hot_ids == hot_index[f : f + 1, :], 1.0, 0.0)
        for k in range(1, hot_index.shape[0] // F):
            count += jnp.where(hot_ids == hot_index[k * F + f : k * F + f + 1, :], 1.0, 0.0)
        copies = jnp.concatenate([grad[f * wide : (f + 1) * wide]] * share, axis=0)
        summed += mxu(count.astype(BF16), copies, NT)
    keep = iota((HOT, cols), 1) // wide == iota((HOT, cols), 0) % share
    hot_rows[...] = jnp.sum(
        jnp.where(keep, summed, 0.0).reshape(owners, share, cols), axis=1
    )

    sample_ids = iota((samples, LANES), 0)
    tail_row = iota((wide, MAIN), 0)
    tail_keep = tail_row // 4 == iota((wide, MAIN), 1) // TAIL
    last_row = iota((8, MAIN), 0)

    def step(o, carry):
        pick = source[pl.ds(o, 1), :]
        found = mxu(grad, one_hot(sample_ids == (pick >> 3)), NN)
        feature = pick & 7
        value = jnp.where(feature == 0, found[:wide], 0.0)
        for f in range(1, F):
            value += jnp.where(feature == f, found[f * wide : (f + 1) * wide], 0.0)
        tail = jnp.where(tail_keep, value[:, MAIN:], 0.0)
        tail = tail[:8] + tail[8:]
        tail = tail + pltpu.roll(tail, 4, 0)
        hot = hot_rows[pl.ds(o, 1), :]
        hot_hi = hot.astype(BF16).astype(F32)
        last = jnp.where(
            last_row < 4,
            tail,
            jnp.where(last_row == 4, hot_hi, jnp.where(last_row == 5, hot - hot_hi, 0.0)),
        )
        out[o] = jnp.concatenate([value[:, :MAIN], last], axis=0).astype(BF16)
        return carry

    lax.fori_loop(0, owners, step, 0, unroll=4)


def gather_kernel(got, target, cold, hot):
    owners = got.shape[0]
    rows = cold.shape[1]
    wide = cold.shape[0]
    row_ids = iota((rows, LANES), 0)
    tail_keep = iota((wide, MAIN), 0) // 4 == iota((wide, MAIN), 1) // TAIL
    low_half = iota((8, MAIN), 0) < 4

    def step(o, carry):
        total, tails = carry
        block = got[o].astype(F32)
        last = block[wide:]
        tail = jnp.where(low_half, last, pltpu.roll(last, 4, 0))
        tail = jnp.where(tail_keep, jnp.concatenate([tail, tail], axis=0), 0.0)
        values = jnp.concatenate([block[:wide], tail], axis=1).astype(BF16)
        total = total + mxu(one_hot(row_ids == target[pl.ds(o, 1), :]), values, NT)
        return total, tails + last

    total, tails = lax.fori_loop(
        0,
        owners,
        step,
        (jnp.zeros((rows, wide), F32), jnp.zeros((8, MAIN), F32)),
        unroll=4,
    )
    cold[...] = total.T
    hot[...] = tails[4:5] + tails[5:6]


def ring_sum(pieces, axis_pairs):
    up, down = axis_pairs
    far_lo, far_hi, up_lo, up_hi, down_lo, down_hi, own = pieces

    def shift(x, pairs):
        return lax.ppermute(x, "col", pairs)

    def add(a, b):
        return (a.astype(F32) + b.astype(F32)).astype(BF16)

    first_up = shift(far_lo, up)
    first_down = shift(far_hi, down)
    below_hi = shift(up_hi, up)
    above_lo = shift(down_lo, down)
    below_lo = shift(add(first_up, up_lo), up)
    above_hi = shift(add(first_down, down_hi), down)
    return own, below_lo, below_hi, above_lo, above_hi


def local(
    embedded,
    gate,
    pre_hidden,
    hidden_weight,
    cross_weight,
    out_weight,
    upstream,
    hot_rows,
    cold_owner,
    cold_rows,
    hot_flag,
    bag_sizes,
):
    owners = lax.axis_size("dp")
    groups = lax.axis_size("col")
    samples, cols = embedded.shape
    inner = groups // SIDE
    total_cols = cross_weight.shape[1]
    wide = cols // F
    slots = hot_rows.shape[1]

    def ring(step_outer, step_inner):
        pairs = []
        for g in range(groups):
            outer, rest = divmod(g, inner)
            pairs.append(
                (g, (outer + step_outer) % SIDE * inner + (rest + step_inner) % inner)
            )
        return pairs

    outer_pairs = ring(1, 0), ring(-1, 0)
    inner_pairs = ring(0, 1), ring(0, -1)
    group = lax.axis_index("col")
    outer_here = (group // inner).reshape(1).astype(jnp.int32)
    inner_here = (group % inner).reshape(1).astype(jnp.int32)

    outer_rows = total_cols // SIDE
    pieces = call(
        hidden_kernel,
        piece_shapes(outer_rows, samples),
        (hidden_weight, pre_hidden, upstream[:, None], out_weight[None, :]),
        smem=(outer_here,),
        flops=2 * total_cols * samples * pre_hidden.shape[1],
        moved=4 * total_cols * samples,
    )

    source, target = call(
        plan_kernel,
        [jax.ShapeDtypeStruct((owners, LANES), jnp.int32)] * 2,
        (cold_owner.T, cold_rows.T, hot_flag.T, bag_sizes[None, :]),
        scratch=[pltpu.VMEM((owners, LANES), F32)] * 3,
        flops=2 * 10**9,
        moved=10**7,
    )
    got_rows = lax.all_to_all(
        target[:, :CAP].reshape(owners, 1, CAP), "dp", split_axis=0, concat_axis=0, tiled=True
    ).reshape(owners, CAP)
    got_rows = jnp.concatenate([got_rows[:, :MAIN]] + [got_rows[:, MAIN:]] * (MAIN // TAIL), axis=1)
    live = lax.broadcasted_iota(jnp.int32, hot_rows.shape, 1) < bag_sizes[:, None]
    hot_index = (
        jnp.where(live & (hot_flag == 1), hot_rows, -1)
        .T.reshape(slots, samples, F)
        .transpose(0, 2, 1)
        .reshape(slots * F, samples)
    )

    def stage_two(pieces):
        return call(
            mid_kernel,
            piece_shapes(cols, samples),
            ring_sum(pieces, outer_pairs),
            smem=(inner_here,),
            scratch=[pltpu.VMEM((outer_rows, samples), BF16)],
            flops=4 * outer_rows * samples,
            moved=10 * outer_rows * samples,
        )

    back = ring_sum(stage_two(pieces), inner_pairs)
    back_one, *pieces = call(
        cross_kernel,
        [jax.ShapeDtypeStruct((cols, samples), F32)] + piece_shapes(outer_rows, samples),
        back + (embedded, cross_weight),
        smem=(outer_here,),
        flops=2 * total_cols * samples * cols,
        moved=4 * total_cols * samples,
    )
    crossed = ring_sum(stage_two(pieces), inner_pairs)
    message = call(
        send_kernel,
        jax.ShapeDtypeStruct((owners, MSG_ROWS, MAIN), BF16),
        crossed + (back_one, gate, source, hot_index),
        scratch=[pltpu.VMEM((owners, cols), F32)],
        flops=2 * 10**9,
        moved=10**7,
    )
    got = lax.all_to_all(message, "dp", split_axis=0, concat_axis=0, tiled=True)
    cold_grad, hot_sum = call(
        gather_kernel,
        [
            jax.ShapeDtypeStruct((wide, COLD_DEV), F32),
            jax.ShapeDtypeStruct((1, MAIN), F32),
        ],
        (got, got_rows),
        flops=2 * 10**9,
        moved=10**7,
    )
    hot_grad = hot_sum.reshape(HOT // owners, wide).T
    return (hot_grad, cold_grad)


def solution(mesh):
    in_specs = (
        P("dp", "col"),
        P("dp", "col"),
        P("dp", "col"),
        P(None, "col"),
        P("col", None),
        P("col"),
        P("dp"),
        P("dp", None),
        P("dp", None),
        P("dp", None),
        P("dp", None),
        P("dp"),
    )
    out_specs = (P("col", "dp"), P("col", "dp"))
    return jax.shard_map(local, mesh=mesh, in_specs=in_specs, out_specs=out_specs, check_vma=False)
```

time: 1050 us -> 259 us (0.25); the launches traced: 1040 us -> 258 us
  blocking collectives: 419 us -> 0 us
  waiting for transfers between devices: 329 us -> 55.6 us
  other arithmetic: 151 us -> 1.14 us
  starting transfers between devices: 22.3 us -> 169 us
  local copies, waits for them, and re-layouts: 99.1 us -> 4.54 us
  Pallas kernels: 0 us -> 26.6 us
  between operations: 14.3 us -> 1.28 us
    psum x1 -> x0, blocking collectives: 419 us -> none  [local(): summed_hot = lax.psum(hot_local, 'dp')]
    reduce_scatter x2 -> x0, waiting for transfers between devices: 329 us -> none  [the longest x1 224 us: local(): lax.psum_scatter(lax.dot_general(hidden_weight, slope_rows, (((1,), (1,))...]
    ppermute x0 -> x24, starting transfers between devices: none -> 133 us  [shift(): return lax.ppermute(x, 'col', pairs)]
    scatter-add x2 -> x0, other arithmetic: 110 us -> none  [the longest x1 62.4 us: local(): jax.ops.segment_sum(got_values.reshape(-1, emb_cols).astype(jnp.float32),...]
    scatter x2 -> x0, local copies, waits for them, and re-layouts: 53.4 us -> none  [the longest x1 30.5 us: local(): send_rows = jnp.full((owners * capacity + 1,), COLD_DEV, jnp.int32).at[ta...]
    another operation x3 -> x0, other arithmetic: 35 us -> none
    ppermute x0 -> x24, waiting for transfers between devices: none -> 31.3 us  [shift(): return lax.ppermute(x, 'col', pairs)]
    pallas_call x0 -> x7, Pallas kernels: none -> 26.6 us  [call(): pl.pallas_call(kernel, out_shape=out_shape, in_specs=[scalar] * len(smem)...]
  transfers between devices with their start and end apart: 4 -> 26, of which waited for: 2 -> 6; matrix products, arithmetic and copies ran while one was open for 17% -> 1% of each run, Pallas kernels for 0% -> 7%
where the time goes in v1:
time: 259 us; the launch traced here: 258 us
  starting transfers between devices  169 us (65%)
  waiting for transfers between devices  55.6 us (21%)
  Pallas kernels  26.6 us (10%)
  local copies, waits for them, and re-layouts  4.54 us (2%)
    ppermute x24, starting transfers between devices, shift(): return lax.ppermute(x, 'col', pairs)  133 us
    ppermute x24, waiting for transfers between devices, shift(): return lax.ppermute(x, 'col', pairs)  31.3 us
    pallas_call x7, Pallas kernels, call(): pl.pallas_call(kernel, out_shape=out_shape, in_specs=[scalar] * len(smem)...  26.6 us
    all_to_all x1, waiting for transfers between devices, local(): got = lax.all_to_all(message, 'dp', split_axis=0, concat_axis=0, tiled=True)  24.3 us
    all_to_all x1, starting transfers between devices, local(): got = lax.all_to_all(message, 'dp', split_axis=0, concat_axis=0, tiled=True)  23.6 us
    all_to_all x1, starting transfers between devices, local(): lax.all_to_all(target[:, :CAP].reshape(owners, 1, CAP), 'dp', split_axis=...  12.4 us
  transfers between devices with their start and end apart: 26, of which 6 were waited for; matrix products, arithmetic and copies ran while one was open for 1% of the time, Pallas kernels for 7%

profile of v1, /device:TPU:1, one launch (start us, length us, event | category | flops | bytes accessed | tf_op | source)
XLA Modules:
  0.0 257.8 jit_solution(7235060031606342040)
XLA Ops:
  3.7 5.2 %collective-permute-start.4 = (bf16[256,512]{1,0:T(8,128)(2,1)S(1)}, bf16[256,512]{1,0:T(8,128)(2,1)S(1)}, u32[]{:S(2)}, u32[]{:S(2)}) collective-permute-start(bf16[256,512]{1,0:T(8,128)(2,1)S(1)} %get-tuple-element.40), channel_id=1, source_target_pairs={{0,12},{1,13},{2,14},{3,15},{4,0},{5,1},{6,2},{7,3},{8,4},{9,5},{1... | collective-permute-start | bytes 786440 | tf_op jit(solution)/shard_map/ppermute | solution.py:244
  8.9 1.9 collective-permute-start
  10.8 2.1 collective-permute-start.2
  12.9 4.4 %collective-permute-start.3 = (bf16[256,512]{1,0:T(8,128)(2,1)S(1)}, bf16[256,512]{1,0:T(8,128)(2,1)S(1)}, u32[]{:S(2)}, u32[]{:S(2)}) collective-permute-start(bf16[256,512]{1,0:T(8,128)(2,1)S(1)} %get-tuple-element.39), channel_id=1, source_target_pairs={{0,12},{1,13},{2,14},{3,15},{4,0},{5,1},{6,2},{7,3},{8,4},{9,5},{1... | collective-permute-start | bytes 786440 | tf_op jit(solution)/shard_map/ppermute | solution.py:244
  17.4 3.4 %collective-permute-start.5 = (bf16[256,512]{1,0:T(8,128)(2,1)S(1)}, bf16[256,512]{1,0:T(8,128)(2,1)S(1)}, u32[]{:S(2)}, u32[]{:S(2)}) collective-permute-start(bf16[256,512]{1,0:T(8,128)(2,1)S(1)} %add_convert_fusion.2), channel_id=1, source_target_pairs={{0,12},{1,13},{2,14},{3,15},{4,0},{5,1},{6,2},{7,3},{8,4},{9,5},{1... | collective-permute-start | bytes 786440 | tf_op jit(solution)/shard_map/ppermute | solution.py:244
  20.9 1.9 collective-permute-start.1
  22.8 4.0 %collective-permute-done.5.above_hi = bf16[256,512]{1,0:T(8,128)(2,1)S(1)} collective-permute-done((bf16[256,512]{1,0:T(8,128)(2,1)S(1)}, bf16[256,512]{1,0:T(8,128)(2,1)S(1)}, u32[]{:S(2)}, u32[]{:S(2)}) %collective-permute-start.5) | collective-permute-done | bytes 262176 | tf_op jit(solution)/shard_map/ppermute | solution.py:244
  26.8 5.5 %collective-permute-done.1.below_lo = bf16[256,512]{1,0:T(8,128)(2,1)S(1)} collective-permute-done((bf16[256,512]{1,0:T(8,128)(2,1)S(1)}, bf16[256,512]{1,0:T(8,128)(2,1)S(1)}, u32[]{:S(2)}, u32[]{:S(2)}) %collective-permute-start.1) | collective-permute-done | bytes 262176 | tf_op jit(solution)/shard_map/ppermute | solution.py:244
  32.6 20.2 %collective-permute-start.10 = (bf16[64,512]{1,0:T(8,128)(2,1)S(1)}, bf16[64,512]{1,0:T(8,128)(2,1)S(1)}, u32[]{:S(2)}, u32[]{:S(2)}) collective-permute-start(bf16[64,512]{1,0:T(8,128)(2,1)S(1)} %get-tuple-element.47), channel_id=1, source_target_pairs={{0,3},{1,0},{2,1},{3,2},{4,7},{5,4},{6,5},{7,6},{8,11},{9,8},{10,9... | collective-permute-start | bytes 196616 | tf_op jit(solution)/shard_map/ppermute | solution.py:244
  52.8 1.9 collective-permute-start.6
  54.7 8.2 %collective-permute-start.8 = (bf16[64,512]{1,0:T(8,128)(2,1)S(1)}, bf16[64,512]{1,0:T(8,128)(2,1)S(1)}, u32[]{:S(2)}, u32[]{:S(2)}) collective-permute-start(bf16[64,512]{1,0:T(8,128)(2,1)S(1)} %get-tuple-element.45), channel_id=1, source_target_pairs={{0,1},{1,2},{2,3},{3,0},{4,5},{5,6},{6,7},{7,4},{8,9},{9,10},{10,1... | collective-permute-start | bytes 196616 | tf_op jit(solution)/shard_map/ppermute | solution.py:244
  62.9 5.8 %collective-permute-start.9 = (bf16[64,512]{1,0:T(8,128)(2,1)S(1)}, bf16[64,512]{1,0:T(8,128)(2,1)S(1)}, u32[]{:S(2)}, u32[]{:S(2)}) collective-permute-start(bf16[64,512]{1,0:T(8,128)(2,1)S(1)} %get-tuple-element.46), channel_id=1, source_target_pairs={{0,3},{1,0},{2,1},{3,2},{4,7},{5,4},{6,5},{7,6},{8,11},{9,8},{10,9... | collective-permute-start | bytes 196616 | tf_op jit(solution)/shard_map/ppermute | solution.py:244
  68.8 12.2 %collective-permute-start.11 = (bf16[64,512]{1,0:T(8,128)(2,1)S(1)}, bf16[64,512]{1,0:T(8,128)(2,1)S(1)}, u32[]{:S(2)}, u32[]{:S(2)}) collective-permute-start(bf16[64,512]{1,0:T(8,128)(2,1)S(1)} %add_convert_fusion.6), channel_id=1, source_target_pairs={{0,3},{1,0},{2,1},{3,2},{4,7},{5,4},{6,5},{7,6},{8,11},{9,8},{10,9... | collective-permute-start | bytes 196616 | tf_op jit(solution)/shard_map/ppermute | solution.py:244
  83.0 14.0 %collective-permute-done.11.above_hi = bf16[64,512]{1,0:T(8,128)(2,1)S(1)} collective-permute-done((bf16[64,512]{1,0:T(8,128)(2,1)S(1)}, bf16[64,512]{1,0:T(8,128)(2,1)S(1)}, u32[]{:S(2)}, u32[]{:S(2)}) %collective-permute-start.11) | collective-permute-done | bytes 65568 | tf_op jit(solution)/shard_map/ppermute | solution.py:244
  97.8 3.2 %collective-permute-start.16 = (bf16[256,512]{1,0:T(8,128)(2,1)S(1)}, bf16[256,512]{1,0:T(8,128)(2,1)S(1)}, u32[]{:S(2)}, u32[]{:S(2)}) collective-permute-start(bf16[256,512]{1,0:T(8,128)(2,1)S(1)} %get-tuple-element.54), channel_id=1, source_target_pairs={{0,12},{1,13},{2,14},{3,15},{4,0},{5,1},{6,2},{7,3},{8,4},{9,5},{1... | collective-permute-start | bytes 786440 | tf_op jit(solution)/shard_map/ppermute | solution.py:244
  101.0 2.1 collective-permute-start.12
  105.0 4.6 %collective-permute-start.15 = (bf16[256,512]{1,0:T(8,128)(2,1)S(1)}, bf16[256,512]{1,0:T(8,128)(2,1)S(1)}, u32[]{:S(2)}, u32[]{:S(2)}) collective-permute-start(bf16[256,512]{1,0:T(8,128)(2,1)S(1)} %get-tuple-element.53), channel_id=1, source_target_pairs={{0,12},{1,13},{2,14},{3,15},{4,0},{5,1},{6,2},{7,3},{8,4},{9,5},{1... | collective-permute-start | bytes 786440 | tf_op jit(solution)/shard_map/ppermute | solution.py:244
  109.7 3.2 %collective-permute-start.17 = (bf16[256,512]{1,0:T(8,128)(2,1)S(1)}, bf16[256,512]{1,0:T(8,128)(2,1)S(1)}, u32[]{:S(2)}, u32[]{:S(2)}) collective-permute-start(bf16[256,512]{1,0:T(8,128)(2,1)S(1)} %add_convert_fusion), channel_id=1, source_target_pairs={{0,12},{1,13},{2,14},{3,15},{4,0},{5,1},{6,2},{7,3},{8,4},{9,5},{1... | collective-permute-start | bytes 786440 | tf_op jit(solution)/shard_map/ppermute | solution.py:244
  113.0 2.1 collective-permute-start.13
  115.2 8.5 %shard_map.135 = (s32[64,256]{1,0:T(8,128)S(1)}, s32[64,256]{1,0:T(8,128)S(1)}) custom-call(s32[2,4096]{1,0:T(2,128)S(1)} %bitcast.20, s32[2,4096]{1,0:T(2,128)S(1)} %bitcast.21, s32[2,4096]{1,0:T(2,128)S(1)} %bitcast.17, s32[1,4096]{1,0:T(1,128)S(1)} %bitcast.19), custom_call_target="tpu_custom_call" | custom-call | flops 2000000000 | bytes 10000000 | tf_op jit(solution)/shard_map/pallas_call | solution.py:41
  124.1 12.9 %collective-permute-start.22 = (bf16[64,512]{1,0:T(8,128)(2,1)S(1)}, bf16[64,512]{1,0:T(8,128)(2,1)S(1)}, u32[]{:S(2)}, u32[]{:S(2)}) collective-permute-start(bf16[64,512]{1,0:T(8,128)(2,1)S(1)} %get-tuple-element.61), channel_id=1, source_target_pairs={{0,3},{1,0},{2,1},{3,2},{4,7},{5,4},{6,5},{7,6},{8,11},{9,8},{10,9... | collective-permute-start | bytes 196616 | tf_op jit(solution)/shard_map/ppermute | solution.py:244
  137.8 12.4 %all-to-all-start.1 = ((s32[64,1,160]{2,1,0:T(1,128)}), s32[64,1,160]{2,1,0:T(1,128)S(1)}, u32[]{:S(2)}, u32[]{:S(2)}) async-start(s32[64,1,160]{2,1,0:T(1,128)} %copy.19), calls=%async_computation.1 | async-start | bytes 131072 | tf_op jit(solution)/shard_map/all_to_all | solution.py:313
  150.2 5.6 %collective-permute-start.18 = (bf16[64,512]{1,0:T(8,128)(2,1)S(1)}, bf16[64,512]{1,0:T(8,128)(2,1)S(1)}, u32[]{:S(2)}, u32[]{:S(2)}) collective-permute-start(bf16[64,512]{1,0:T(8,128)(2,1)S(1)} %get-tuple-element.57), channel_id=1, source_target_pairs={{0,1},{1,2},{2,3},{3,0},{4,5},{5,6},{6,7},{7,4},{8,9},{9,10},{10,1... | collective-permute-start | bytes 196616 | tf_op jit(solution)/shard_map/ppermute | solution.py:244
  155.8 5.5 %collective-permute-start.20 = (bf16[64,512]{1,0:T(8,128)(2,1)S(1)}, bf16[64,512]{1,0:T(8,128)(2,1)S(1)}, u32[]{:S(2)}, u32[]{:S(2)}) collective-permute-start(bf16[64,512]{1,0:T(8,128)(2,1)S(1)} %get-tuple-element.59), channel_id=1, source_target_pairs={{0,1},{1,2},{2,3},{3,0},{4,5},{5,6},{6,7},{7,4},{8,9},{9,10},{10,1... | collective-permute-start | bytes 196616 | tf_op jit(solution)/shard_map/ppermute | solution.py:244
  161.4 8.5 %collective-permute-start.21 = (bf16[64,512]{1,0:T(8,128)(2,1)S(1)}, bf16[64,512]{1,0:T(8,128)(2,1)S(1)}, u32[]{:S(2)}, u32[]{:S(2)}) collective-permute-start(bf16[64,512]{1,0:T(8,128)(2,1)S(1)} %get-tuple-element.60), channel_id=1, source_target_pairs={{0,3},{1,0},{2,1},{3,2},{4,7},{5,4},{6,5},{7,6},{8,11},{9,8},{10,9... | collective-permute-start | bytes 196616 | tf_op jit(solution)/shard_map/ppermute | solution.py:244
  169.9 8.4 %collective-permute-start.23 = (bf16[64,512]{1,0:T(8,128)(2,1)S(1)}, bf16[64,512]{1,0:T(8,128)(2,1)S(1)}, u32[]{:S(2)}, u32[]{:S(2)}) collective-permute-start(bf16[64,512]{1,0:T(8,128)(2,1)S(1)} %add_convert_fusion.4), channel_id=1, source_target_pairs={{0,3},{1,0},{2,1},{3,2},{4,7},{5,4},{6,5},{7,6},{8,11},{9,8},{10,9... | collective-permute-start | bytes 196616 | tf_op jit(solution)/shard_map/ppermute | solution.py:244
  178.3 5.6 %collective-permute-start.19 = (bf16[64,512]{1,0:T(8,128)(2,1)S(1)}, bf16[64,512]{1,0:T(8,128)(2,1)S(1)}, u32[]{:S(2)}, u32[]{:S(2)}) collective-permute-start(bf16[64,512]{1,0:T(8,128)(2,1)S(1)} %add_convert_fusion.5), channel_id=1, source_target_pairs={{0,1},{1,2},{2,3},{3,0},{4,5},{5,6},{6,7},{7,4},{8,9},{9,10},{10,1... | collective-permute-start | bytes 196616 | tf_op jit(solution)/shard_map/ppermute | solution.py:244
  185.2 7.1 %collective-permute-done.19.below_lo = bf16[64,512]{1,0:T(8,128)(2,1)S(1)} collective-permute-done((bf16[64,512]{1,0:T(8,128)(2,1)S(1)}, bf16[64,512]{1,0:T(8,128)(2,1)S(1)}, u32[]{:S(2)}, u32[]{:S(2)}) %collective-permute-start.19) | collective-permute-done | bytes 65568 | tf_op jit(solution)/shard_map/ppermute | solution.py:244
  192.3 8.2 %shard_map.136 = bf16[64,24,128]{2,1,0:T(8,128)(2,1)} custom-call(bf16[128,512]{1,0:T(8,128)(2,1)S(1)} %get-tuple-element.56.own, bf16[64,512]{1,0:T(8,128)(2,1)S(1)} %collective-permute-done.19.below_lo, bf16[64,512]{1,0:T(8,128)(2,1)S(1)} %collective-permute-done.20.below_hi, bf16[64,512]{1,0:T(8,128)(2,1)S(1)} %collective-permute-done.21.above_lo, ...), custom_call_target="tpu_custom_call" | custom-call | flops 2000000000 | bytes 10000000 | tf_op jit(solution)/shard_map/pallas_call | solution.py:41
  200.6 23.6 %all-to-all-start = ((bf16[64,24,128]{2,1,0:T(8,128)(2,1)}), bf16[64,24,128]{2,1,0:T(8,128)(2,1)S(1)}, u32[]{:S(2)}, u32[]{:S(2)}) async-start(bf16[64,24,128]{2,1,0:T(8,128)(2,1)} %shard_map.136), calls=%async_computation | async-start | bytes 786432 | tf_op jit(solution)/shard_map/all_to_all | solution.py:354
  224.2 24.3 %all-to-all-done.got = bf16[64,24,128]{2,1,0:T(8,128)(2,1)S(1)} async-done(((bf16[64,24,128]{2,1,0:T(8,128)(2,1)}), bf16[64,24,128]{2,1,0:T(8,128)(2,1)S(1)}, u32[]{:S(2)}, u32[]{:S(2)}) %all-to-all-start) | async-done | bytes 393248 | tf_op jit(solution)/shard_map/all_to_all | solution.py:354
  248.6 7.4 %shard_map.137 = (f32[16,512]{1,0:T(8,128)}, f32[1,128]{1,0:T(1,128)S(1)}) custom-call(bf16[64,24,128]{2,1,0:T(8,128)(2,1)S(1)} %all-to-all-done.got, s32[64,256]{1,0:T(8,128)S(1)} %pad_add_fusion.target), custom_call_target="tpu_custom_call" | custom-call | flops 2000000000 | bytes 10000000 | tf_op jit(solution)/shard_map/pallas_call | solution.py:41
  (70 shorter events, 12.7 us)
Async XLA Ops:
  3.7 13.7 %collective-permute-start.4 = (bf16[256,512]{1,0:T(8,128)(2,1)S(1)}, bf16[256,512]{1,0:T(8,128)(2,1)S(1)}, u32[]{:S(2)}, u32[]{:S(2)}) collective-permute-start(bf16[256,512]{1,0:T(8,128)(2,1)S(1)} %get-tuple-element.40), channel_id=1, source_target_pairs={{0,12},{1,13},{2,14},{3,15},{4,0},{5,1},{6,2},{7,3},{8,4},{9,5},{1... | collective-permute-start | bytes 786440 | tf_op jit(solution)/shard_map/ppermute | solution.py:244
  8.9 11.9 %collective-permute-start = (bf16[256,512]{1,0:T(8,128)(2,1)S(1)}, bf16[256,512]{1,0:T(8,128)(2,1)S(1)}, u32[]{:S(2)}, u32[]{:S(2)}) collective-permute-start(bf16[256,512]{1,0:T(8,128)(2,1)S(1)} %get-tuple-element.36), channel_id=1, source_target_pairs={{0,4},{1,5},{2,6},{3,7},{4,8},{5,9},{6,10},{7,11},{8,12},{9,13},{1... | collective-permute-start | bytes 786440 | tf_op jit(solution)/shard_map/ppermute | solution.py:244
  10.8 12.0 %collective-permute-start.2 = (bf16[256,512]{1,0:T(8,128)(2,1)S(1)}, bf16[256,512]{1,0:T(8,128)(2,1)S(1)}, u32[]{:S(2)}, u32[]{:S(2)}) collective-permute-start(bf16[256,512]{1,0:T(8,128)(2,1)S(1)} %get-tuple-element.38), channel_id=1, source_target_pairs={{0,4},{1,5},{2,6},{3,7},{4,8},{5,9},{6,10},{7,11},{8,12},{9,13},{1... | collective-permute-start | bytes 786440 | tf_op jit(solution)/shard_map/ppermute | solution.py:244
  12.9 9.9 %collective-permute-start.3 = (bf16[256,512]{1,0:T(8,128)(2,1)S(1)}, bf16[256,512]{1,0:T(8,128)(2,1)S(1)}, u32[]{:S(2)}, u32[]{:S(2)}) collective-permute-start(bf16[256,512]{1,0:T(8,128)(2,1)S(1)} %get-tuple-element.39), channel_id=1, source_target_pairs={{0,12},{1,13},{2,14},{3,15},{4,0},{5,1},{6,2},{7,3},{8,4},{9,5},{1... | collective-permute-start | bytes 786440 | tf_op jit(solution)/shard_map/ppermute | solution.py:244
  17.4 9.4 %collective-permute-start.5 = (bf16[256,512]{1,0:T(8,128)(2,1)S(1)}, bf16[256,512]{1,0:T(8,128)(2,1)S(1)}, u32[]{:S(2)}, u32[]{:S(2)}) collective-permute-start(bf16[256,512]{1,0:T(8,128)(2,1)S(1)} %add_convert_fusion.2), channel_id=1, source_target_pairs={{0,12},{1,13},{2,14},{3,15},{4,0},{5,1},{6,2},{7,3},{8,4},{9,5},{1... | collective-permute-start | bytes 786440 | tf_op jit(solution)/shard_map/ppermute | solution.py:244
  20.9 11.4 %collective-permute-start.1 = (bf16[256,512]{1,0:T(8,128)(2,1)S(1)}, bf16[256,512]{1,0:T(8,128)(2,1)S(1)}, u32[]{:S(2)}, u32[]{:S(2)}) collective-permute-start(bf16[256,512]{1,0:T(8,128)(2,1)S(1)} %add_convert_fusion.3), channel_id=1, source_target_pairs={{0,4},{1,5},{2,6},{3,7},{4,8},{5,9},{6,10},{7,11},{8,12},{9,13},{1... | collective-permute-start | bytes 786440 | tf_op jit(solution)/shard_map/ppermute | solution.py:244
  32.3 64.7 %copy-start = (bf16[128,2048]{1,0:T(8,128)(2,1)S(1)}, bf16[128,2048]{1,0:T(8,128)(2,1)}, u32[]{:S(2)}) copy-start(bf16[128,2048]{1,0:T(8,128)(2,1)} %weight.3) | copy-start | bytes 1572868
  32.6 36.1 %collective-permute-start.10 = (bf16[64,512]{1,0:T(8,128)(2,1)S(1)}, bf16[64,512]{1,0:T(8,128)(2,1)S(1)}, u32[]{:S(2)}, u32[]{:S(2)}) collective-permute-start(bf16[64,512]{1,0:T(8,128)(2,1)S(1)} %get-tuple-element.47), channel_id=1, source_target_pairs={{0,3},{1,0},{2,1},{3,2},{4,7},{5,4},{6,5},{7,6},{8,11},{9,8},{10,9... | collective-permute-start | bytes 196616 | tf_op jit(solution)/shard_map/ppermute | solution.py:244
  52.8 28.2 %collective-permute-start.6 = (bf16[64,512]{1,0:T(8,128)(2,1)S(1)}, bf16[64,512]{1,0:T(8,128)(2,1)S(1)}, u32[]{:S(2)}, u32[]{:S(2)}) collective-permute-start(bf16[64,512]{1,0:T(8,128)(2,1)S(1)} %get-tuple-element.43), channel_id=1, source_target_pairs={{0,1},{1,2},{2,3},{3,0},{4,5},{5,6},{6,7},{7,4},{8,9},{9,10},{10,1... | collective-permute-start | bytes 196616 | tf_op jit(solution)/shard_map/ppermute | solution.py:244
  54.7 28.2 %collective-permute-start.8 = (bf16[64,512]{1,0:T(8,128)(2,1)S(1)}, bf16[64,512]{1,0:T(8,128)(2,1)S(1)}, u32[]{:S(2)}, u32[]{:S(2)}) collective-permute-start(bf16[64,512]{1,0:T(8,128)(2,1)S(1)} %get-tuple-element.45), channel_id=1, source_target_pairs={{0,1},{1,2},{2,3},{3,0},{4,5},{5,6},{6,7},{7,4},{8,9},{9,10},{10,1... | collective-permute-start | bytes 196616 | tf_op jit(solution)/shard_map/ppermute | solution.py:244
  62.9 20.1 %collective-permute-start.9 = (bf16[64,512]{1,0:T(8,128)(2,1)S(1)}, bf16[64,512]{1,0:T(8,128)(2,1)S(1)}, u32[]{:S(2)}, u32[]{:S(2)}) collective-permute-start(bf16[64,512]{1,0:T(8,128)(2,1)S(1)} %get-tuple-element.46), channel_id=1, source_target_pairs={{0,3},{1,0},{2,1},{3,2},{4,7},{5,4},{6,5},{7,6},{8,11},{9,8},{10,9... | collective-permute-start | bytes 196616 | tf_op jit(solution)/shard_map/ppermute | solution.py:244
  68.8 28.2 %copy-start.1 = (bf16[512,128]{1,0:T(8,128)(2,1)S(1)}, bf16[512,128]{1,0:T(8,128)(2,1)}, u32[]{:S(2)}) copy-start(bf16[512,128]{1,0:T(8,128)(2,1)} %embedded.1) | copy-start | bytes 393220
  68.8 28.2 %collective-permute-start.11 = (bf16[64,512]{1,0:T(8,128)(2,1)S(1)}, bf16[64,512]{1,0:T(8,128)(2,1)S(1)}, u32[]{:S(2)}, u32[]{:S(2)}) collective-permute-start(bf16[64,512]{1,0:T(8,128)(2,1)S(1)} %add_convert_fusion.6), channel_id=1, source_target_pairs={{0,3},{1,0},{2,1},{3,2},{4,7},{5,4},{6,5},{7,6},{8,11},{9,8},{10,9... | collective-permute-start | bytes 196616 | tf_op jit(solution)/shard_map/ppermute | solution.py:244
  81.0 16.0 %collective-permute-start.7 = (bf16[64,512]{1,0:T(8,128)(2,1)S(1)}, bf16[64,512]{1,0:T(8,128)(2,1)S(1)}, u32[]{:S(2)}, u32[]{:S(2)}) collective-permute-start(bf16[64,512]{1,0:T(8,128)(2,1)S(1)} %add_convert_fusion.7), channel_id=1, source_target_pairs={{0,1},{1,2},{2,3},{3,0},{4,5},{5,6},{6,7},{7,4},{8,9},{9,10},{10,1... | collective-permute-start | bytes 196616 | tf_op jit(solution)/shard_map/ppermute | solution.py:244
  97.8 11.8 %collective-permute-start.16 = (bf16[256,512]{1,0:T(8,128)(2,1)S(1)}, bf16[256,512]{1,0:T(8,128)(2,1)S(1)}, u32[]{:S(2)}, u32[]{:S(2)}) collective-permute-start(bf16[256,512]{1,0:T(8,128)(2,1)S(1)} %get-tuple-element.54), channel_id=1, source_target_pairs={{0,12},{1,13},{2,14},{3,15},{4,0},{5,1},{6,2},{7,3},{8,4},{9,5},{1... | collective-permute-start | bytes 786440 | tf_op jit(solution)/shard_map/ppermute | solution.py:244
  101.0 11.9 %collective-permute-start.12 = (bf16[256,512]{1,0:T(8,128)(2,1)S(1)}, bf16[256,512]{1,0:T(8,128)(2,1)S(1)}, u32[]{:S(2)}, u32[]{:S(2)}) collective-permute-start(bf16[256,512]{1,0:T(8,128)(2,1)S(1)} %get-tuple-element.50), channel_id=1, source_target_pairs={{0,4},{1,5},{2,6},{3,7},{4,8},{5,9},{6,10},{7,11},{8,12},{9,13},{1... | collective-permute-start | bytes 786440 | tf_op jit(solution)/shard_map/ppermute | solution.py:244
  103.1 20.6 %collective-permute-start.14 = (bf16[256,512]{1,0:T(8,128)(2,1)S(1)}, bf16[256,512]{1,0:T(8,128)(2,1)S(1)}, u32[]{:S(2)}, u32[]{:S(2)}) collective-permute-start(bf16[256,512]{1,0:T(8,128)(2,1)S(1)} %get-tuple-element.52), channel_id=1, source_target_pairs={{0,4},{1,5},{2,6},{3,7},{4,8},{5,9},{6,10},{7,11},{8,12},{9,13},{1... | collective-permute-start | bytes 786440 | tf_op jit(solution)/shard_map/ppermute | solution.py:244
  105.0 18.7 %collective-permute-start.15 = (bf16[256,512]{1,0:T(8,128)(2,1)S(1)}, bf16[256,512]{1,0:T(8,128)(2,1)S(1)}, u32[]{:S(2)}, u32[]{:S(2)}) collective-permute-start(bf16[256,512]{1,0:T(8,128)(2,1)S(1)} %get-tuple-element.53), channel_id=1, source_target_pairs={{0,12},{1,13},{2,14},{3,15},{4,0},{5,1},{6,2},{7,3},{8,4},{9,5},{1... | collective-permute-start | bytes 786440 | tf_op jit(solution)/shard_map/ppermute | solution.py:244
  109.7 14.0 %collective-permute-start.17 = (bf16[256,512]{1,0:T(8,128)(2,1)S(1)}, bf16[256,512]{1,0:T(8,128)(2,1)S(1)}, u32[]{:S(2)}, u32[]{:S(2)}) collective-permute-start(bf16[256,512]{1,0:T(8,128)(2,1)S(1)} %add_convert_fusion), channel_id=1, source_target_pairs={{0,12},{1,13},{2,14},{3,15},{4,0},{5,1},{6,2},{7,3},{8,4},{9,5},{1... | collective-permute-start | bytes 786440 | tf_op jit(solution)/shard_map/ppermute | solution.py:244
  112.9 2.3 copy-start.2
  112.9 2.3 copy-start.3
  113.0 10.8 %collective-permute-start.13 = (bf16[256,512]{1,0:T(8,128)(2,1)S(1)}, bf16[256,512]{1,0:T(8,128)(2,1)S(1)}, u32[]{:S(2)}, u32[]{:S(2)}) collective-permute-start(bf16[256,512]{1,0:T(8,128)(2,1)S(1)} %add_convert_fusion.1), channel_id=1, source_target_pairs={{0,4},{1,5},{2,6},{3,7},{4,8},{5,9},{6,10},{7,11},{8,12},{9,13},{1... | collective-permute-start | bytes 786440 | tf_op jit(solution)/shard_map/ppermute | solution.py:244
  124.1 45.7 %collective-permute-start.22 = (bf16[64,512]{1,0:T(8,128)(2,1)S(1)}, bf16[64,512]{1,0:T(8,128)(2,1)S(1)}, u32[]{:S(2)}, u32[]{:S(2)}) collective-permute-start(bf16[64,512]{1,0:T(8,128)(2,1)S(1)} %get-tuple-element.61), channel_id=1, source_target_pairs={{0,3},{1,0},{2,1},{3,2},{4,7},{5,4},{6,5},{7,6},{8,11},{9,8},{10,9... | collective-permute-start | bytes 196616 | tf_op jit(solution)/shard_map/ppermute | solution.py:244
  137.8 62.8 %all-to-all-start.1 = ((s32[64,1,160]{2,1,0:T(1,128)}), s32[64,1,160]{2,1,0:T(1,128)S(1)}, u32[]{:S(2)}, u32[]{:S(2)}) async-start(s32[64,1,160]{2,1,0:T(1,128)} %copy.19), calls=%async_computation.1 | async-start | bytes 131072 | tf_op jit(solution)/shard_map/all_to_all | solution.py:313
  150.2 28.1 %collective-permute-start.18 = (bf16[64,512]{1,0:T(8,128)(2,1)S(1)}, bf16[64,512]{1,0:T(8,128)(2,1)S(1)}, u32[]{:S(2)}, u32[]{:S(2)}) collective-permute-start(bf16[64,512]{1,0:T(8,128)(2,1)S(1)} %get-tuple-element.57), channel_id=1, source_target_pairs={{0,1},{1,2},{2,3},{3,0},{4,5},{5,6},{6,7},{7,4},{8,9},{9,10},{10,1... | collective-permute-start | bytes 196616 | tf_op jit(solution)/shard_map/ppermute | solution.py:244
  155.8 28.7 %collective-permute-start.20 = (bf16[64,512]{1,0:T(8,128)(2,1)S(1)}, bf16[64,512]{1,0:T(8,128)(2,1)S(1)}, u32[]{:S(2)}, u32[]{:S(2)}) collective-permute-start(bf16[64,512]{1,0:T(8,128)(2,1)S(1)} %get-tuple-element.59), channel_id=1, source_target_pairs={{0,1},{1,2},{2,3},{3,0},{4,5},{5,6},{6,7},{7,4},{8,9},{9,10},{10,1... | collective-permute-start | bytes 196616 | tf_op jit(solution)/shard_map/ppermute | solution.py:244
  161.4 23.1 %collective-permute-start.21 = (bf16[64,512]{1,0:T(8,128)(2,1)S(1)}, bf16[64,512]{1,0:T(8,128)(2,1)S(1)}, u32[]{:S(2)}, u32[]{:S(2)}) collective-permute-start(bf16[64,512]{1,0:T(8,128)(2,1)S(1)} %get-tuple-element.60), channel_id=1, source_target_pairs={{0,3},{1,0},{2,1},{3,2},{4,7},{5,4},{6,5},{7,6},{8,11},{9,8},{10,9... | collective-permute-start | bytes 196616 | tf_op jit(solution)/shard_map/ppermute | solution.py:244
  169.9 15.4 %collective-permute-start.23 = (bf16[64,512]{1,0:T(8,128)(2,1)S(1)}, bf16[64,512]{1,0:T(8,128)(2,1)S(1)}, u32[]{:S(2)}, u32[]{:S(2)}) collective-permute-start(bf16[64,512]{1,0:T(8,128)(2,1)S(1)} %add_convert_fusion.4), channel_id=1, source_target_pairs={{0,3},{1,0},{2,1},{3,2},{4,7},{5,4},{6,5},{7,6},{8,11},{9,8},{10,9... | collective-permute-start | bytes 196616 | tf_op jit(solution)/shard_map/ppermute | solution.py:244
  178.3 5.7 %copy-start.9 = (s32[4096,2]{0,1:T(2,128)S(1)}, s32[4096,2]{0,1:T(2,128)}, u32[]{:S(2)}) copy-start(s32[4096,2]{0,1:T(2,128)} %param.19) | copy-start | bytes 98308
  178.3 14.0 %collective-permute-start.19 = (bf16[64,512]{1,0:T(8,128)(2,1)S(1)}, bf16[64,512]{1,0:T(8,128)(2,1)S(1)}, u32[]{:S(2)}, u32[]{:S(2)}) collective-permute-start(bf16[64,512]{1,0:T(8,128)(2,1)S(1)} %add_convert_fusion.5), channel_id=1, source_target_pairs={{0,1},{1,2},{2,3},{3,0},{4,5},{5,6},{6,7},{7,4},{8,9},{9,10},{10,1... | collective-permute-start | bytes 196616 | tf_op jit(solution)/shard_map/ppermute | solution.py:244
  184.3 8.0 %copy-start.6 = (bf16[512,128]{1,0:T(8,128)(2,1)S(1)}, bf16[512,128]{1,0:T(8,128)(2,1)}, u32[]{:S(2)}) copy-start(bf16[512,128]{1,0:T(8,128)(2,1)} %gate.1) | copy-start | bytes 393220
  200.6 48.0 %all-to-all-start = ((bf16[64,24,128]{2,1,0:T(8,128)(2,1)}), bf16[64,24,128]{2,1,0:T(8,128)(2,1)S(1)}, u32[]{:S(2)}, u32[]{:S(2)}) async-start(bf16[64,24,128]{2,1,0:T(8,128)(2,1)} %shard_map.136), calls=%async_computation | async-start | bytes 786432 | tf_op jit(solution)/shard_map/all_to_all | solution.py:354
  (5 other events, 7.6 us)

commit v2 on v1

v2 whole, which is shorter than its diff:
```python
import jax
import jax.numpy as jnp
from jax import lax
from jax.experimental import pallas as pl
from jax.experimental.pallas import tpu as pltpu
from jax.sharding import PartitionSpec as P

F = 8
HOT = 512
COLD_DEV = 512
CAP = 160
SIDE = 4
MAIN = 128
TAIL = CAP - MAIN
LANES = 256
HALF = 256
MSG_ROWS = 24
F32 = jnp.float32
BF16 = jnp.bfloat16
NT = (((1,), (1,)), ((), ()))
TN = (((0,), (0,)), ((), ()))
NN = (((1,), (0,)), ((), ()))


def mxu(a, b, dims):
    return lax.dot_general(a, b, dims, preferred_element_type=F32)


def iota(shape, axis):
    return lax.broadcasted_iota(jnp.int32, shape, axis)


def one_hot(match):
    return jnp.where(match, 1.0, 0.0).astype(BF16)


def call(kernel, out_shape, inputs, smem=(), scratch=(), flops=0, moved=0):
    vmem = pl.BlockSpec(memory_space=pltpu.VMEM)
    scalar = pl.BlockSpec(memory_space=pltpu.SMEM)
    return pl.pallas_call(
        kernel,
        out_shape=out_shape,
        in_specs=[scalar] * len(smem) + [vmem] * len(inputs),
        out_specs=jax.tree.map(lambda _: vmem, out_shape),
        scratch_shapes=list(scratch),
        compiler_params=pltpu.CompilerParams(vmem_limit_bytes=40 * 2**20),
        cost_estimate=pl.CostEstimate(flops=flops, bytes_accessed=moved, transcendentals=0),
    )(*smem, *inputs)


def blocks_of(rows, lanes):
    return [jax.ShapeDtypeStruct((rows, lanes), BF16)] * 4


def partner(here, flip):
    return jnp.where(flip == 0, here ^ 1, SIDE - 1 - here)


def store_blocks(make, place, diagonal, near, second, own):
    here, side = place[0], place[1]
    for ref, block in (
        (diagonal, (here + 2) % SIDE),
        (near, partner(here, side)),
        (second, partner(here, 1 - side)),
        (own, here),
    ):
        ref[...] = make(block).astype(BF16)


def hidden_kernel(place, weight, pre_hidden, upstream, out_weight, *refs):
    slope = jnp.where(
        pre_hidden[...] > 0, upstream[...] * out_weight[...].astype(F32), 0.0
    ).astype(BF16)
    rows = refs[0].shape[0]

    def make(block):
        start = pl.multiple_of(block * rows, rows)
        return mxu(weight[pl.ds(start, rows), :], slope, NT)

    store_blocks(make, place, *refs)


def joined(terms):
    own, near, far = terms
    return own[...].astype(F32) + near[...].astype(F32) + far[...].astype(F32)


def mid_kernel(place, own, near, far, *refs):
    total = refs[4]
    total[...] = joined((own, near, far)).astype(BF16)
    rows = refs[0].shape[0]

    def make(block):
        return total[pl.ds(pl.multiple_of(block * rows, rows), rows), :]

    store_blocks(make, place, *refs[:4])


def cross_kernel(place, own, near, far, embedded, weight, back_one, *refs):
    total = joined((own, near, far))
    back_one[...] = total
    gated = (total * embedded[...].astype(F32).T).astype(BF16)
    rows = refs[0].shape[0]

    def make(block):
        start = pl.multiple_of(block * rows, rows)
        return mxu(weight[:, pl.ds(start, rows)], gated, TN)

    store_blocks(make, place, *refs)


def row_code(row):
    return ((MAIN + (row & (MAIN - 1))) << (row >> 7)).astype(F32)


def plan_kernel(owner, rows, flag, bags, group, sample, code):
    width = 512
    owners = group.shape[0]
    ahead = one_hot(iota((width, width), 0) < iota((width, width), 1))
    owner_ids = iota((owners, width), 0)
    lane_slot = iota((LANES, width), 0)
    slot_ids = jnp.where(lane_slot < MAIN, lane_slot, MAIN + lane_slot % TAIL).astype(F32)
    for part in (group, sample, code):
        part[...] = jnp.zeros_like(part)

    def step(chunk, used):
        at = pl.ds(pl.multiple_of(chunk * width, width), width)
        bag = chunk * width + iota((1, width), 1)
        group_of = (((bag >> 3) // HALF) * F + (bag & 7) + 1).astype(F32)
        sample_of = ((bag >> 3) % HALF).astype(F32)
        for k in range(owner.shape[0]):
            cold = (bags[:, at] > k) & (flag[k : k + 1, at] == 0)
            hit = (owner_ids == owner[k : k + 1, at]) & cold
            match = one_hot(hit)
            before = mxu(match, ahead, NN) + used
            place = jnp.sum(jnp.where(hit, before, 0.0), axis=0, keepdims=True)
            taken = slot_ids == place
            code_of = row_code(rows[k : k + 1, at])
            for part, value in ((group, group_of), (sample, sample_of), (code, code_of)):
                part[...] += mxu(match, jnp.where(taken, value, 0.0).astype(BF16), NT)
            used = used + jnp.sum(jnp.where(hit, 1.0, 0.0), axis=1, keepdims=True)
        return used

    lax.fori_loop(0, owner.shape[1] // width, step, jnp.zeros((owners, 1), F32))


def send_kernel(
    own, near, far, back_one, gate, group, sample, code, hot_index, out, hot_rows
):
    crossed = joined((own, near, far))
    grad = (back_one[...] * (gate[...].astype(F32).T + 1.0) + crossed).astype(BF16)
    cols, samples = grad.shape
    wide = cols // F
    row_id = iota((cols, cols), 0)
    grad = mxu(
        one_hot(iota((cols, cols), 1) == (row_id % wide) * F + row_id // wide), grad, NN
    ).astype(BF16)

    owners = group.shape[0]
    share = HOT // owners
    owner_ids = iota((owners, samples), 0)
    share_ids = iota((cols, samples), 0) // wide
    summed = jnp.zeros((owners, cols), F32)
    for f in range(F):
        copies = jnp.concatenate([grad[f * wide : (f + 1) * wide]] * share, axis=0).astype(F32)
        for k in range(hot_index.shape[0] // F):
            index = hot_index[k * F + f : k * F + f + 1, :]
            picked = jnp.where(share_ids == (index & (share - 1)), copies, 0.0).astype(BF16)
            summed += mxu(one_hot(owner_ids == (index >> 3)), picked, NT)
    hot_rows[...] = summed

    halves = jnp.concatenate(
        [grad[:, h * HALF : (h + 1) * HALF] for h in range(samples // HALF)], axis=0
    )
    groups = halves.shape[0] // wide
    sample_ids = iota((HALF, LANES), 0).astype(F32)
    tail_keep = iota((wide, MAIN), 0) // 4 == iota((wide, MAIN), 1) // TAIL
    last_row = iota((8, MAIN), 0)

    def step(o, carry):
        at = pl.ds(o, 1)
        found = mxu(halves, one_hot(sample_ids == sample[at, :]), NN)
        which = group[at, :]
        value = jnp.where(which == 1.0, found[:wide], 0.0)
        for g in range(1, groups):
            value = jnp.where(which == g + 1.0, found[g * wide : (g + 1) * wide], value)
        tail = jnp.where(tail_keep, value[:, MAIN:], 0.0)
        tail = tail[:8] + tail[8:]
        tail = tail + pltpu.roll(tail, 4, 0)
        hot = hot_rows[at, :]
        hot_hi = hot.astype(BF16).astype(F32)
        codes = code[at, :]
        last = tail
        for row, line in ((4, hot_hi), (5, hot - hot_hi), (6, codes[:, :MAIN]), (7, codes[:, MAIN:])):
            last = jnp.where(last_row == row, line, last)
        out[o] = jnp.concatenate([value[:, :MAIN], last], axis=0).astype(BF16)
        return carry

    lax.fori_loop(0, owners, step, 0, unroll=4)


def gather_kernel(got, cold, hot):
    owners = got.shape[0]
    wide = cold.shape[0]
    parts = cold.shape[1] // MAIN
    row_ids = (iota((MAIN, LANES), 0) + MAIN).astype(F32)
    part_ids = iota((parts * wide, LANES), 0) // wide
    tail_keep = iota((wide, MAIN), 0) // 4 == iota((wide, MAIN), 1) // TAIL
    low_half = iota((8, MAIN), 0) < 4

    def step(o, carry):
        total, tails = carry
        block = got[o].astype(F32)
        last = block[wide:]
        tail = jnp.where(low_half, last, pltpu.roll(last, 4, 0))
        tail = jnp.where(tail_keep, jnp.concatenate([tail, tail], axis=0), 0.0)
        values = jnp.concatenate([block[:wide], tail], axis=1)
        codes = jnp.concatenate([last[6:7], last[7:8]], axis=1)
        part = jnp.zeros(codes.shape, jnp.int32)
        lead = codes
        for p in range(1, parts):
            above = codes >= float(MAIN << p)
            part = jnp.where(above, p, part)
            lead = jnp.where(above, codes * (0.5**p), lead)
        spread = jnp.where(part_ids == part, jnp.concatenate([values] * parts, axis=0), 0.0)
        total = total + mxu(one_hot(row_ids == lead), spread.astype(BF16), NT)
        return total, tails + last

    total, tails = lax.fori_loop(
        0,
        owners,
        step,
        (jnp.zeros((MAIN, parts * wide), F32), jnp.zeros((8, MAIN), F32)),
        unroll=4,
    )
    total = total.T
    for p in range(parts):
        cold[:, p * MAIN : (p + 1) * MAIN] = total[p * wide : (p + 1) * wide]
    hot[...] = tails[4:5] + tails[5:6]


def local(
    embedded,
    gate,
    pre_hidden,
    hidden_weight,
    cross_weight,
    out_weight,
    upstream,
    hot_rows,
    cold_owner,
    cold_rows,
    hot_flag,
    bag_sizes,
):
    owners = lax.axis_size("dp")
    groups = lax.axis_size("col")
    samples, cols = embedded.shape
    inner = groups // SIDE
    total_cols = cross_weight.shape[1]
    wide = cols // F
    slots = hot_rows.shape[1]
    side = lax.axis_index("dp") % 2
    group = lax.axis_index("col")
    outer_place = jnp.stack([group // inner, side]).astype(jnp.int32)
    inner_place = jnp.stack([group % inner, side]).astype(jnp.int32)

    def shift(x, along_outer, turn):
        pairs = []
        for d in range(owners):
            for g in range(groups):
                outer, rest = divmod(g, inner)
                here = outer if along_outer else rest
                other = here ^ 1 if (d + turn) % 2 == 0 else SIDE - 1 - here
                to = other * inner + rest if along_outer else outer * inner + other
                pairs.append((d * groups + g, d * groups + to))
        return lax.ppermute(x, ("dp", "col"), pairs)

    def exchange(blocks, along_outer, beside=None):
        diagonal, near, second, own = blocks
        extra = None
        if beside is not None:
            held, diagonal = lax.optimization_barrier((beside[1], diagonal))
        first = shift(diagonal, along_outer, 0)
        near = shift(near, along_outer, 0)
        if beside is not None:
            extra = beside[0](*held)
            first, extra = lax.optimization_barrier((first, extra))
        onward = (second.astype(F32) + first.astype(F32)).astype(BF16)
        return (own, near, shift(onward, along_outer, 1)), extra

    def plan(owner, rows, flag, bags):
        return call(
            plan_kernel,
            [jax.ShapeDtypeStruct((owners, LANES), F32)] * 3,
            (owner, rows, flag, bags),
            flops=2 * 10**9,
            moved=10**7,
        )

    live = lax.broadcasted_iota(jnp.int32, hot_rows.shape, 1) < bag_sizes[:, None]
    hot_index = (
        jnp.where(live & (hot_flag == 1), hot_rows, -1)
        .T.reshape(slots, samples, F)
        .transpose(0, 2, 1)
        .reshape(slots * F, samples)
    )
    outer_rows = total_cols // SIDE

    def stage_two(terms):
        return call(
            mid_kernel,
            blocks_of(cols, samples),
            terms,
            smem=(inner_place,),
            scratch=[pltpu.VMEM((outer_rows, samples), BF16)],
            flops=4 * outer_rows * samples,
            moved=10 * outer_rows * samples,
        )

    blocks = call(
        hidden_kernel,
        blocks_of(outer_rows, samples),
        (hidden_weight, pre_hidden, upstream[:, None], out_weight[None, :]),
        smem=(outer_place,),
        flops=2 * total_cols * samples * pre_hidden.shape[1],
        moved=4 * total_cols * samples,
    )
    terms, _ = exchange(blocks, True)
    terms, routes = exchange(
        stage_two(terms), False, (plan, (cold_owner.T, cold_rows.T, hot_flag.T, bag_sizes[None, :]))
    )
    back_one, *blocks = call(
        cross_kernel,
        [jax.ShapeDtypeStruct((cols, samples), F32)] + blocks_of(outer_rows, samples),
        terms + (embedded, cross_weight),
        smem=(outer_place,),
        flops=2 * total_cols * samples * cols,
        moved=4 * total_cols * samples,
    )
    terms, _ = exchange(blocks, True)
    terms, _ = exchange(stage_two(terms), False)
    message = call(
        send_kernel,
        jax.ShapeDtypeStruct((owners, MSG_ROWS, MAIN), BF16),
        terms + (back_one, gate, *routes, hot_index),
        scratch=[pltpu.VMEM((owners, cols), F32)],
        flops=2 * 10**9,
        moved=10**7,
    )
    got = lax.all_to_all(message, "dp", split_axis=0, concat_axis=0, tiled=True)
    cold_grad, hot_sum = call(
        gather_kernel,
        [
            jax.ShapeDtypeStruct((wide, COLD_DEV), F32),
            jax.ShapeDtypeStruct((1, MAIN), F32),
        ],
        (got,),
        flops=2 * 10**9,
        moved=10**7,
    )
    hot_grad = hot_sum.reshape(HOT // owners, wide).T
    return (hot_grad, cold_grad)


def solution(mesh):
    in_specs = (
        P("dp", "col"),
        P("dp", "col"),
        P("dp", "col"),
        P(None, "col"),
        P("col", None),
        P("col"),
        P("dp"),
        P("dp", None),
        P("dp", None),
        P("dp", None),
        P("dp", None),
        P("dp"),
    )
    out_specs = (P("col", "dp"), P("col", "dp"))
    return jax.shard_map(local, mesh=mesh, in_specs=in_specs, out_specs=out_specs, check_vma=False)
```

time: 259 us -> 215 us (0.83)
  starting transfers between devices: 169 us -> 69.5 us
  blocking collectives: 0 us -> 41.7 us
  waiting for transfers between devices: 55.6 us -> 72.2 us
  Pallas kernels: 26.6 us -> 23.5 us
    ppermute x24 -> x12, starting transfers between devices: 133 us -> 69.5 us  [shift(): return lax.ppermute(x, ('dp', 'col'), pairs)]
    all_to_all x0 -> x1, blocking collectives: none -> 41.7 us  [local(): got = lax.all_to_all(message, 'dp', split_axis=0, concat_axis=0, tiled=True)]
    ppermute x24 -> x12, waiting for transfers between devices: 31.3 us -> 72.2 us  [shift(): return lax.ppermute(x, ('dp', 'col'), pairs)]
    all_to_all x2 -> x0, starting transfers between devices: 36 us -> none  [the longest x1 23.6 us: local(): got = lax.all_to_all(message, 'dp', split_axis=0, concat_axis=0, tiled=True)]
    all_to_all x2 -> x0, waiting for transfers between devices: 24.3 us -> none  [the longest x1 24.3 us: local(): got = lax.all_to_all(message, 'dp', split_axis=0, concat_axis=0, tiled=True)]
    pallas_call x7, Pallas kernels: 26.6 us -> 23.5 us  [call(): pl.pallas_call(kernel, out_shape=out_shape, in_specs=[scalar] * len(smem)...]
  transfers between devices with their start and end apart: 26 -> 12, of which waited for: 6 -> 11; matrix products, arithmetic and copies ran while one was open for 1% -> 0% of each run, Pallas kernels for 7% -> 4%
where the time goes in v2:
time: 215 us; the launch traced here: 213 us
  waiting for transfers between devices  72.2 us (34%)
  starting transfers between devices  69.5 us (32%)
  blocking collectives  41.7 us (19%)
  Pallas kernels  23.5 us (11%)
  local copies, waits for them, and re-layouts  3.79 us (2%)
    ppermute x12, waiting for transfers between devices, shift(): return lax.ppermute(x, ('dp', 'col'), pairs)  72.2 us
    ppermute x12, starting transfers between devices, shift(): return lax.ppermute(x, ('dp', 'col'), pairs)  69.5 us
    all_to_all x1, blocking collectives, local(): got = lax.all_to_all(message, 'dp', split_axis=0, concat_axis=0, tiled=True)  41.7 us
    pallas_call x7, Pallas kernels, call(): pl.pallas_call(kernel, out_shape=out_shape, in_specs=[scalar] * len(smem)...  23.5 us
  transfers between devices with their start and end apart: 12, of which 11 were waited for; matrix products, arithmetic and copies ran while one was open for 0% of the time, Pallas kernels for 4%

profile of v2, /device:TPU:1, one launch (start us, length us, event | category | flops | bytes accessed | tf_op | source)
XLA Modules:
  0.0 212.9 jit_solution(8958622696198395850)
XLA Ops:
  1.7 1.2 copy-done.4
  2.9 1.4 shard_map.131
  4.3 5.2 %collective-permute-start.1 = (bf16[512,512]{1,0:T(8,128)(2,1)S(1)}, bf16[512,512]{1,0:T(8,128)(2,1)S(1)}, u32[]{:S(2)}, u32[]{:S(2)}) collective-permute-start(bf16[512,512]{1,0:T(8,128)(2,1)S(1)} %get-tuple-element.36), channel_id=1, source_target_pairs={{0,4},{1,5},{2,6},{3,7},{4,0},{5,1},{6,2},{7,3},{8,12},{9,13},{10,... | collective-permute-start | bytes 1572872 | tf_op jit(solution)/shard_map/ppermute | solution.py:277
  9.5 1.9 collective-permute-start
  11.4 4.6 %collective-permute-done.1 = bf16[512,512]{1,0:T(8,128)(2,1)S(1)} collective-permute-done((bf16[512,512]{1,0:T(8,128)(2,1)S(1)}, bf16[512,512]{1,0:T(8,128)(2,1)S(1)}, u32[]{:S(2)}, u32[]{:S(2)}) %collective-permute-start.1) | collective-permute-done | bytes 524320 | tf_op jit(solution)/shard_map/ppermute | solution.py:277
  16.2 2.1 collective-permute-start.2
  18.4 3.3 %collective-permute-done.near = bf16[512,512]{1,0:T(8,128)(2,1)S(1)} collective-permute-done((bf16[512,512]{1,0:T(8,128)(2,1)S(1)}, bf16[512,512]{1,0:T(8,128)(2,1)S(1)}, u32[]{:S(2)}, u32[]{:S(2)}) %collective-permute-start) | collective-permute-done | bytes 524320 | tf_op jit(solution)/shard_map/ppermute | solution.py:277
  21.7 7.6 %collective-permute-done.2.far = bf16[512,512]{1,0:T(8,128)(2,1)S(1)} collective-permute-done((bf16[512,512]{1,0:T(8,128)(2,1)S(1)}, bf16[512,512]{1,0:T(8,128)(2,1)S(1)}, u32[]{:S(2)}, u32[]{:S(2)}) %collective-permute-start.2) | collective-permute-done | bytes 524320 | tf_op jit(solution)/shard_map/ppermute | solution.py:277
  29.3 0.9 shard_map.132
  30.2 21.1 %collective-permute-start.4 = (bf16[128,512]{1,0:T(8,128)(2,1)S(1)}, bf16[128,512]{1,0:T(8,128)(2,1)S(1)}, u32[]{:S(2)}, u32[]{:S(2)}) collective-permute-start(bf16[128,512]{1,0:T(8,128)(2,1)S(1)} %get-tuple-element.41), channel_id=1, source_target_pairs={{0,1},{1,0},{2,3},{3,2},{4,5},{5,4},{6,7},{7,6},{8,9},{9,8},{10,11... | collective-permute-start | bytes 393224 | tf_op jit(solution)/shard_map/ppermute | solution.py:277
  51.4 2.1 collective-permute-start.3
  53.5 8.5 %shard_map.133 = (f32[64,256]{1,0:T(8,128)S(1)}, f32[64,256]{1,0:T(8,128)S(1)}, f32[64,256]{1,0:T(8,128)S(1)}) custom-call(s32[2,4096]{1,0:T(2,128)S(1)} %bitcast.16, s32[2,4096]{1,0:T(2,128)S(1)} %bitcast.17, s32[2,4096]{1,0:T(2,128)S(1)} %bitcast.13, s32[1,4096]{1,0:T(1,128)S(1)} %bitcast.15), custom_call_target="tpu_custom_call" | custom-call | flops 2000000000 | bytes 10000000 | tf_op jit(solution)/shard_map/pallas_call | solution.py:40
  62.1 9.9 %collective-permute-start.5 = (bf16[128,512]{1,0:T(8,128)(2,1)S(1)}, bf16[128,512]{1,0:T(8,128)(2,1)S(1)}, u32[]{:S(2)}, u32[]{:S(2)}) collective-permute-start(bf16[128,512]{1,0:T(8,128)(2,1)S(1)} %add_convert_fusion.3), channel_id=1, source_target_pairs={{0,3},{1,2},{2,1},{3,0},{4,7},{5,6},{6,5},{7,4},{8,11},{9,10},{10,... | collective-permute-start | bytes 393224 | tf_op jit(solution)/shard_map/ppermute | solution.py:277
  71.9 1.3 collective-permute-done.3.near
  73.2 13.6 %collective-permute-done.5.far = bf16[128,512]{1,0:T(8,128)(2,1)S(1)} collective-permute-done((bf16[128,512]{1,0:T(8,128)(2,1)S(1)}, bf16[128,512]{1,0:T(8,128)(2,1)S(1)}, u32[]{:S(2)}, u32[]{:S(2)}) %collective-permute-start.5) | collective-permute-done | bytes 131104 | tf_op jit(solution)/shard_map/ppermute | solution.py:277
  86.9 1.3 shard_map.134
  88.2 4.2 %collective-permute-start.7 = (bf16[512,512]{1,0:T(8,128)(2,1)S(1)}, bf16[512,512]{1,0:T(8,128)(2,1)S(1)}, u32[]{:S(2)}, u32[]{:S(2)}) collective-permute-start(bf16[512,512]{1,0:T(8,128)(2,1)S(1)} %get-tuple-element.53), channel_id=1, source_target_pairs={{0,4},{1,5},{2,6},{3,7},{4,0},{5,1},{6,2},{7,3},{8,12},{9,13},{10,... | collective-permute-start | bytes 1572872 | tf_op jit(solution)/shard_map/ppermute | solution.py:277
  92.4 2.3 %collective-permute-start.6 = (bf16[512,512]{1,0:T(8,128)(2,1)S(1)}, bf16[512,512]{1,0:T(8,128)(2,1)S(1)}, u32[]{:S(2)}, u32[]{:S(2)}) collective-permute-start(bf16[512,512]{1,0:T(8,128)(2,1)S(1)} %get-tuple-element.51), channel_id=1, source_target_pairs={{0,4},{1,5},{2,6},{3,7},{4,0},{5,1},{6,2},{7,3},{8,12},{9,13},{10,... | collective-permute-start | bytes 1572872 | tf_op jit(solution)/shard_map/ppermute | solution.py:277
  94.7 4.6 %collective-permute-done.7 = bf16[512,512]{1,0:T(8,128)(2,1)S(1)} collective-permute-done((bf16[512,512]{1,0:T(8,128)(2,1)S(1)}, bf16[512,512]{1,0:T(8,128)(2,1)S(1)}, u32[]{:S(2)}, u32[]{:S(2)}) %collective-permute-start.7) | collective-permute-done | bytes 524320 | tf_op jit(solution)/shard_map/ppermute | solution.py:277
  99.5 3.2 %collective-permute-start.8 = (bf16[512,512]{1,0:T(8,128)(2,1)S(1)}, bf16[512,512]{1,0:T(8,128)(2,1)S(1)}, u32[]{:S(2)}, u32[]{:S(2)}) collective-permute-start(bf16[512,512]{1,0:T(8,128)(2,1)S(1)} %add_convert_fusion), channel_id=1, source_target_pairs={{0,12},{1,13},{2,14},{3,15},{4,8},{5,9},{6,10},{7,11},{8,4},{9,5},... | collective-permute-start | bytes 1572872 | tf_op jit(solution)/shard_map/ppermute | solution.py:277
  102.7 2.3 %collective-permute-done.6.near = bf16[512,512]{1,0:T(8,128)(2,1)S(1)} collective-permute-done((bf16[512,512]{1,0:T(8,128)(2,1)S(1)}, bf16[512,512]{1,0:T(8,128)(2,1)S(1)}, u32[]{:S(2)}, u32[]{:S(2)}) %collective-permute-start.6) | collective-permute-done | bytes 524320 | tf_op jit(solution)/shard_map/ppermute | solution.py:277
  104.9 8.4 %collective-permute-done.8.far = bf16[512,512]{1,0:T(8,128)(2,1)S(1)} collective-permute-done((bf16[512,512]{1,0:T(8,128)(2,1)S(1)}, bf16[512,512]{1,0:T(8,128)(2,1)S(1)}, u32[]{:S(2)}, u32[]{:S(2)}) %collective-permute-start.8) | collective-permute-done | bytes 524320 | tf_op jit(solution)/shard_map/ppermute | solution.py:277
  113.4 1.0 shard_map.135
  114.3 10.6 %collective-permute-start.10 = (bf16[128,512]{1,0:T(8,128)(2,1)S(1)}, bf16[128,512]{1,0:T(8,128)(2,1)S(1)}, u32[]{:S(2)}, u32[]{:S(2)}) collective-permute-start(bf16[128,512]{1,0:T(8,128)(2,1)S(1)} %get-tuple-element.57), channel_id=1, source_target_pairs={{0,1},{1,0},{2,3},{3,2},{4,5},{5,4},{6,7},{7,6},{8,9},{9,8},{10,11... | collective-permute-start | bytes 393224 | tf_op jit(solution)/shard_map/ppermute | solution.py:277
  124.9 3.4 %collective-permute-start.9 = (bf16[128,512]{1,0:T(8,128)(2,1)S(1)}, bf16[128,512]{1,0:T(8,128)(2,1)S(1)}, u32[]{:S(2)}, u32[]{:S(2)}) collective-permute-start(bf16[128,512]{1,0:T(8,128)(2,1)S(1)} %get-tuple-element.55), channel_id=1, source_target_pairs={{0,1},{1,0},{2,3},{3,2},{4,5},{5,4},{6,7},{7,6},{8,9},{9,8},{10,11... | collective-permute-start | bytes 393224 | tf_op jit(solution)/shard_map/ppermute | solution.py:277
  128.3 3.2 %collective-permute-done.10 = bf16[128,512]{1,0:T(8,128)(2,1)S(1)} collective-permute-done((bf16[128,512]{1,0:T(8,128)(2,1)S(1)}, bf16[128,512]{1,0:T(8,128)(2,1)S(1)}, u32[]{:S(2)}, u32[]{:S(2)}) %collective-permute-start.10) | collective-permute-done | bytes 131104 | tf_op jit(solution)/shard_map/ppermute | solution.py:277
  131.6 3.5 %collective-permute-start.11 = (bf16[128,512]{1,0:T(8,128)(2,1)S(1)}, bf16[128,512]{1,0:T(8,128)(2,1)S(1)}, u32[]{:S(2)}, u32[]{:S(2)}) collective-permute-start(bf16[128,512]{1,0:T(8,128)(2,1)S(1)} %add_convert_fusion.2), channel_id=1, source_target_pairs={{0,3},{1,2},{2,1},{3,0},{4,7},{5,6},{6,5},{7,4},{8,11},{9,10},{10,... | collective-permute-start | bytes 393224 | tf_op jit(solution)/shard_map/ppermute | solution.py:277
  135.6 9.0 %collective-permute-done.9.near = bf16[128,512]{1,0:T(8,128)(2,1)S(1)} collective-permute-done((bf16[128,512]{1,0:T(8,128)(2,1)S(1)}, bf16[128,512]{1,0:T(8,128)(2,1)S(1)}, u32[]{:S(2)}, u32[]{:S(2)}) %collective-permute-start.9) | collective-permute-done | bytes 131104 | tf_op jit(solution)/shard_map/ppermute | solution.py:277
  144.6 14.3 %collective-permute-done.11.far = bf16[128,512]{1,0:T(8,128)(2,1)S(1)} collective-permute-done((bf16[128,512]{1,0:T(8,128)(2,1)S(1)}, bf16[128,512]{1,0:T(8,128)(2,1)S(1)}, u32[]{:S(2)}, u32[]{:S(2)}) %collective-permute-start.11) | collective-permute-done | bytes 131104 | tf_op jit(solution)/shard_map/ppermute | solution.py:277
  158.9 5.9 %shard_map.136 = bf16[64,24,128]{2,1,0:T(8,128)(2,1)S(1)} custom-call(bf16[128,512]{1,0:T(8,128)(2,1)S(1)} %get-tuple-element.54.own, bf16[128,512]{1,0:T(8,128)(2,1)S(1)} %collective-permute-done.9.near, bf16[128,512]{1,0:T(8,128)(2,1)S(1)} %collective-permute-done.11.far, f32[128,512]{1,0:T(8,128)S(1)} %get-tuple-element.58.back_one, ...), custom_call_target="tpu_custom_call" | custom-call | flops 2000000000 | bytes 10000000 | tf_op jit(solution)/shard_map/pallas_call | solution.py:40
  164.8 41.7 %all_to_all.5.got = bf16[64,24,128]{2,1,0:T(8,128)(2,1)S(1)} all-to-all(bf16[64,24,128]{2,1,0:T(8,128)(2,1)S(1)} %shard_map.136), channel_id=1, replica_groups=mesh['dp'=64,'col'=16] {'dp'}, dimensions={0} | all-to-all | bytes 786432 | tf_op jit(solution)/shard_map/all_to_all | solution.py:351
  206.6 4.5 %shard_map.137 = (f32[16,512]{1,0:T(8,128)}, f32[1,128]{1,0:T(1,128)S(1)}) custom-call(bf16[64,24,128]{2,1,0:T(8,128)(2,1)S(1)} %all_to_all.5.got), custom_call_target="tpu_custom_call" | custom-call | flops 2000000000 | bytes 10000000 | tf_op jit(solution)/shard_map/pallas_call | solution.py:40
  (36 shorter events, 3.8 us)
Async XLA Ops:
  0.6 1.0 copy-start.5
  0.7 0.9 copy-start.10
  1.7 1.2 copy-start.4
  4.3 11.8 %collective-permute-start.1 = (bf16[512,512]{1,0:T(8,128)(2,1)S(1)}, bf16[512,512]{1,0:T(8,128)(2,1)S(1)}, u32[]{:S(2)}, u32[]{:S(2)}) collective-permute-start(bf16[512,512]{1,0:T(8,128)(2,1)S(1)} %get-tuple-element.36), channel_id=1, source_target_pairs={{0,4},{1,5},{2,6},{3,7},{4,0},{5,1},{6,2},{7,3},{8,12},{9,13},{10,... | collective-permute-start | bytes 1572872 | tf_op jit(solution)/shard_map/ppermute | solution.py:277
  9.5 12.2 %collective-permute-start = (bf16[512,512]{1,0:T(8,128)(2,1)S(1)}, bf16[512,512]{1,0:T(8,128)(2,1)S(1)}, u32[]{:S(2)}, u32[]{:S(2)}) collective-permute-start(bf16[512,512]{1,0:T(8,128)(2,1)S(1)} %get-tuple-element.34), channel_id=1, source_target_pairs={{0,4},{1,5},{2,6},{3,7},{4,0},{5,1},{6,2},{7,3},{8,12},{9,13},{10,... | collective-permute-start | bytes 1572872 | tf_op jit(solution)/shard_map/ppermute | solution.py:277
  16.2 13.1 %collective-permute-start.2 = (bf16[512,512]{1,0:T(8,128)(2,1)S(1)}, bf16[512,512]{1,0:T(8,128)(2,1)S(1)}, u32[]{:S(2)}, u32[]{:S(2)}) collective-permute-start(bf16[512,512]{1,0:T(8,128)(2,1)S(1)} %add_convert_fusion.1), channel_id=1, source_target_pairs={{0,12},{1,13},{2,14},{3,15},{4,8},{5,9},{6,10},{7,11},{8,4},{9,5},... | collective-permute-start | bytes 1572872 | tf_op jit(solution)/shard_map/ppermute | solution.py:277
  29.3 24.2 %copy-start.2 = (s32[4096,2]{0,1:T(2,128)S(1)}, s32[4096,2]{0,1:T(2,128)}, u32[]{:S(2)}) copy-start(s32[4096,2]{0,1:T(2,128)} %param.22) | copy-start | bytes 98308
  29.3 24.2 %copy-start.3 = (s32[4096]{0:T(1024)S(1)}, s32[4096]{0:T(1024)}, u32[]{:S(2)}) copy-start(s32[4096]{0:T(1024)} %param.23) | copy-start | bytes 49156
  29.3 24.2 %copy-start.7 = (s32[4096,2]{0,1:T(2,128)S(1)}, s32[4096,2]{0,1:T(2,128)}, u32[]{:S(2)}) copy-start(s32[4096,2]{0,1:T(2,128)} %param.20) | copy-start | bytes 98308
  29.3 24.2 %copy-start.8 = (s32[4096,2]{0,1:T(2,128)S(1)}, s32[4096,2]{0,1:T(2,128)}, u32[]{:S(2)}) copy-start(s32[4096,2]{0,1:T(2,128)} %param.21) | copy-start | bytes 98308
  30.2 31.8 %collective-permute-start.4 = (bf16[128,512]{1,0:T(8,128)(2,1)S(1)}, bf16[128,512]{1,0:T(8,128)(2,1)S(1)}, u32[]{:S(2)}, u32[]{:S(2)}) collective-permute-start(bf16[128,512]{1,0:T(8,128)(2,1)S(1)} %get-tuple-element.41), channel_id=1, source_target_pairs={{0,1},{1,0},{2,3},{3,2},{4,5},{5,4},{6,7},{7,6},{8,9},{9,8},{10,11... | collective-permute-start | bytes 393224 | tf_op jit(solution)/shard_map/ppermute | solution.py:277
  51.4 35.5 %copy-start = (bf16[128,2048]{1,0:T(8,128)(2,1)S(1)}, bf16[128,2048]{1,0:T(8,128)(2,1)}, u32[]{:S(2)}) copy-start(bf16[128,2048]{1,0:T(8,128)(2,1)} %weight.3) | copy-start | bytes 1572868
  51.4 21.8 %collective-permute-start.3 = (bf16[128,512]{1,0:T(8,128)(2,1)S(1)}, bf16[128,512]{1,0:T(8,128)(2,1)S(1)}, u32[]{:S(2)}, u32[]{:S(2)}) collective-permute-start(bf16[128,512]{1,0:T(8,128)(2,1)S(1)} %get-tuple-element.38), channel_id=1, source_target_pairs={{0,1},{1,0},{2,3},{3,2},{4,5},{5,4},{6,7},{7,6},{8,9},{9,8},{10,11... | collective-permute-start | bytes 393224 | tf_op jit(solution)/shard_map/ppermute | solution.py:277
  62.0 24.8 %copy-start.1 = (bf16[512,128]{1,0:T(8,128)(2,1)S(1)}, bf16[512,128]{1,0:T(8,128)(2,1)}, u32[]{:S(2)}) copy-start(bf16[512,128]{1,0:T(8,128)(2,1)} %embedded.1) | copy-start | bytes 393220
  62.1 24.8 %collective-permute-start.5 = (bf16[128,512]{1,0:T(8,128)(2,1)S(1)}, bf16[128,512]{1,0:T(8,128)(2,1)S(1)}, u32[]{:S(2)}, u32[]{:S(2)}) collective-permute-start(bf16[128,512]{1,0:T(8,128)(2,1)S(1)} %add_convert_fusion.3), channel_id=1, source_target_pairs={{0,3},{1,2},{2,1},{3,0},{4,7},{5,6},{6,5},{7,4},{8,11},{9,10},{10,... | collective-permute-start | bytes 393224 | tf_op jit(solution)/shard_map/ppermute | solution.py:277
  88.2 11.1 %collective-permute-start.7 = (bf16[512,512]{1,0:T(8,128)(2,1)S(1)}, bf16[512,512]{1,0:T(8,128)(2,1)S(1)}, u32[]{:S(2)}, u32[]{:S(2)}) collective-permute-start(bf16[512,512]{1,0:T(8,128)(2,1)S(1)} %get-tuple-element.53), channel_id=1, source_target_pairs={{0,4},{1,5},{2,6},{3,7},{4,0},{5,1},{6,2},{7,3},{8,12},{9,13},{10,... | collective-permute-start | bytes 1572872 | tf_op jit(solution)/shard_map/ppermute | solution.py:277
  92.4 12.6 %collective-permute-start.6 = (bf16[512,512]{1,0:T(8,128)(2,1)S(1)}, bf16[512,512]{1,0:T(8,128)(2,1)S(1)}, u32[]{:S(2)}, u32[]{:S(2)}) collective-permute-start(bf16[512,512]{1,0:T(8,128)(2,1)S(1)} %get-tuple-element.51), channel_id=1, source_target_pairs={{0,4},{1,5},{2,6},{3,7},{4,0},{5,1},{6,2},{7,3},{8,12},{9,13},{10,... | collective-permute-start | bytes 1572872 | tf_op jit(solution)/shard_map/ppermute | solution.py:277
  99.5 13.9 %collective-permute-start.8 = (bf16[512,512]{1,0:T(8,128)(2,1)S(1)}, bf16[512,512]{1,0:T(8,128)(2,1)S(1)}, u32[]{:S(2)}, u32[]{:S(2)}) collective-permute-start(bf16[512,512]{1,0:T(8,128)(2,1)S(1)} %add_convert_fusion), channel_id=1, source_target_pairs={{0,12},{1,13},{2,14},{3,15},{4,8},{5,9},{6,10},{7,11},{8,4},{9,5},... | collective-permute-start | bytes 1572872 | tf_op jit(solution)/shard_map/ppermute | solution.py:277
  114.3 17.2 %collective-permute-start.10 = (bf16[128,512]{1,0:T(8,128)(2,1)S(1)}, bf16[128,512]{1,0:T(8,128)(2,1)S(1)}, u32[]{:S(2)}, u32[]{:S(2)}) collective-permute-start(bf16[128,512]{1,0:T(8,128)(2,1)S(1)} %get-tuple-element.57), channel_id=1, source_target_pairs={{0,1},{1,0},{2,3},{3,2},{4,5},{5,4},{6,7},{7,6},{8,9},{9,8},{10,11... | collective-permute-start | bytes 393224 | tf_op jit(solution)/shard_map/ppermute | solution.py:277
  124.9 19.7 %collective-permute-start.9 = (bf16[128,512]{1,0:T(8,128)(2,1)S(1)}, bf16[128,512]{1,0:T(8,128)(2,1)S(1)}, u32[]{:S(2)}, u32[]{:S(2)}) collective-permute-start(bf16[128,512]{1,0:T(8,128)(2,1)S(1)} %get-tuple-element.55), channel_id=1, source_target_pairs={{0,1},{1,0},{2,3},{3,2},{4,5},{5,4},{6,7},{7,6},{8,9},{9,8},{10,11... | collective-permute-start | bytes 393224 | tf_op jit(solution)/shard_map/ppermute | solution.py:277
  131.5 3.5 %copy-start.9 = (s32[4096,2]{0,1:T(2,128)S(1)}, s32[4096,2]{0,1:T(2,128)}, u32[]{:S(2)}) copy-start(s32[4096,2]{0,1:T(2,128)} %param.19) | copy-start | bytes 98308
  131.6 27.3 %collective-permute-start.11 = (bf16[128,512]{1,0:T(8,128)(2,1)S(1)}, bf16[128,512]{1,0:T(8,128)(2,1)S(1)}, u32[]{:S(2)}, u32[]{:S(2)}) collective-permute-start(bf16[128,512]{1,0:T(8,128)(2,1)S(1)} %add_convert_fusion.2), channel_id=1, source_target_pairs={{0,3},{1,2},{2,1},{3,0},{4,7},{5,6},{6,5},{7,4},{8,11},{9,10},{10,... | collective-permute-start | bytes 393224 | tf_op jit(solution)/shard_map/ppermute | solution.py:277
  135.4 23.5 %copy-start.6 = (bf16[512,128]{1,0:T(8,128)(2,1)S(1)}, bf16[512,128]{1,0:T(8,128)(2,1)}, u32[]{:S(2)}) copy-start(bf16[512,128]{1,0:T(8,128)(2,1)} %gate.1) | copy-start | bytes 393220

commit v3 on v2

--- a/solution.py
+++ b/solution.py
@@ -96,24 +96,37 @@
     store_blocks(make, place, *refs[:4])
 
 
-def cross_kernel(place, own, near, far, embedded, weight, back_one, *refs):
+def gate_kernel(own, near, far, embedded, back_one, gated):
     total = joined((own, near, far))
     back_one[...] = total
-    gated = (total * embedded[...].astype(F32).T).astype(BF16)
+    gated[...] = (total * embedded[...].astype(F32).T).astype(BF16)
+
+
+def cross_kernel(place, w_own, w_near, w_far, w_diag, g_own, g_near, g_far, g_diag, *refs):
+    total = refs[4]
+    product = mxu(w_own[...], g_own[...], TN)
+    for weight, gated in ((w_near, g_near), (w_far, g_far), (w_diag, g_diag)):
+        product += mxu(weight[...], gated[...], TN)
+    total[...] = product.astype(BF16)
     rows = refs[0].shape[0]
 
     def make(block):
-        start = pl.multiple_of(block * rows, rows)
-        return mxu(weight[:, pl.ds(start, rows)], gated, TN)
-
-    store_blocks(make, place, *refs)
+        return total[pl.ds(pl.multiple_of(block * rows, rows), rows), :]
+
+    store_blocks(make, place, *refs[:4])
 
 
 def row_code(row):
     return ((MAIN + (row & (MAIN - 1))) << (row >> 7)).astype(F32)
 
 
-def plan_kernel(owner, rows, flag, bags, group, sample, code):
+def plan_kernel(place, owner, rows, flag, bags, weight, group, sample, code, *blocks):
+    span = blocks[0].shape[1]
+
+    def make(block):
+        return weight[:, pl.ds(pl.multiple_of(block * span, span), span)]
+
+    store_blocks(make, place, *blocks)
     width = 512
     owners = group.shape[0]
     ahead = one_hot(iota((width, width), 0) < iota((width, width), 1))
@@ -265,38 +278,52 @@
     outer_place = jnp.stack([group // inner, side]).astype(jnp.int32)
     inner_place = jnp.stack([group % inner, side]).astype(jnp.int32)
 
+    outer_rows = total_cols // SIDE
+
     def shift(x, along_outer, turn):
         pairs = []
         for d in range(owners):
             for g in range(groups):
                 outer, rest = divmod(g, inner)
                 here = outer if along_outer else rest
-                other = here ^ 1 if (d + turn) % 2 == 0 else SIDE - 1 - here
+                if turn is None:
+                    other = (here + 2) % SIDE
+                else:
+                    other = here ^ 1 if (d + turn) % 2 == 0 else SIDE - 1 - here
                 to = other * inner + rest if along_outer else outer * inner + other
                 pairs.append((d * groups + g, d * groups + to))
         return lax.ppermute(x, ("dp", "col"), pairs)
 
-    def exchange(blocks, along_outer, beside=None):
+    def onward(second, first):
+        return (second.astype(F32) + first.astype(F32)).astype(BF16)
+
+    def exchange(blocks, along_outer):
         diagonal, near, second, own = blocks
-        extra = None
-        if beside is not None:
-            held, diagonal = lax.optimization_barrier((beside[1], diagonal))
         first = shift(diagonal, along_outer, 0)
         near = shift(near, along_outer, 0)
-        if beside is not None:
-            extra = beside[0](*held)
-            first, extra = lax.optimization_barrier((first, extra))
-        onward = (second.astype(F32) + first.astype(F32)).astype(BF16)
-        return (own, near, shift(onward, along_outer, 1)), extra
-
-    def plan(owner, rows, flag, bags):
-        return call(
+        return own, near, shift(onward(second, first), along_outer, 1)
+
+    def exchange_beside(blocks, held):
+        diagonal, near, second, own = blocks
+        held, diagonal = lax.optimization_barrier((held, diagonal))
+        first = shift(diagonal, False, 0)
+        near = shift(near, False, 0)
+        *routes, w_diag, w_near, w_far, w_own = call(
             plan_kernel,
-            [jax.ShapeDtypeStruct((owners, LANES), F32)] * 3,
-            (owner, rows, flag, bags),
+            [jax.ShapeDtypeStruct((owners, LANES), F32)] * 3 + blocks_of(cols, outer_rows),
+            held,
+            smem=(outer_place,),
             flops=2 * 10**9,
             moved=10**7,
         )
+        first, routes, parts = lax.optimization_barrier((first, routes, (w_near, w_far, w_diag)))
+        far = onward(second, first)
+        far, parts = lax.optimization_barrier((far, parts))
+        far = shift(far, False, 1)
+        near, parts = lax.optimization_barrier((near, parts))
+        parts = tuple(shift(part, True, turn) for part, turn in zip(parts, (0, 1, None)))
+        far, parts = lax.optimization_barrier((far, parts))
+        return (own, near, far), routes, (w_own, *parts)
 
     live = lax.broadcasted_iota(jnp.int32, hot_rows.shape, 1) < bag_sizes[:, None]
     hot_index = (
@@ -305,7 +332,6 @@
         .transpose(0, 2, 1)
         .reshape(slots * F, samples)
     )
-    outer_rows = total_cols // SIDE
 
     def stage_two(terms):
         return call(
@@ -326,20 +352,30 @@
         flops=2 * total_cols * samples * pre_hidden.shape[1],
         moved=4 * total_cols * samples,
     )
-    terms, _ = exchange(blocks, True)
-    terms, routes = exchange(
-        stage_two(terms), False, (plan, (cold_owner.T, cold_rows.T, hot_flag.T, bag_sizes[None, :]))
-    )
-    back_one, *blocks = call(
+    terms, routes, weights = exchange_beside(
+        stage_two(exchange(blocks, True)),
+        (cold_owner.T, cold_rows.T, hot_flag.T, bag_sizes[None, :], cross_weight),
+    )
+    back_one, gated = call(
+        gate_kernel,
+        [jax.ShapeDtypeStruct((cols, samples), F32), jax.ShapeDtypeStruct((cols, samples), BF16)],
+        terms + (embedded,),
+        flops=4 * cols * samples,
+        moved=16 * cols * samples,
+    )
+    near = shift(gated, True, 0)
+    far = shift(gated, True, 1)
+    diagonal = shift(near, True, 1)
+    blocks = call(
         cross_kernel,
-        [jax.ShapeDtypeStruct((cols, samples), F32)] + blocks_of(outer_rows, samples),
-        terms + (embedded, cross_weight),
-        smem=(outer_place,),
+        blocks_of(cols, samples),
+        weights + (gated, near, far, diagonal),
+        smem=(inner_place,),
+        scratch=[pltpu.VMEM((outer_rows, samples), BF16)],
         flops=2 * total_cols * samples * cols,
-        moved=4 * total_cols * samples,
-    )
-    terms, _ = exchange(blocks, True)
-    terms, _ = exchange(stage_two(terms), False)
+        moved=4 * outer_rows * samples,
+    )
+    terms = exchange(blocks, False)
     message = call(
         send_kernel,
         jax.ShapeDtypeStruct((owners, MSG_ROWS, MAIN), BF16),

time: 215 us -> 219 us (1.019)
  waiting for transfers between devices: 72.2 us -> 51.3 us
  starting transfers between devices: 69.5 us -> 83.3 us
  blocking collectives: 41.7 us -> 54.6 us
    ppermute x12 -> x15, waiting for transfers between devices: 72.2 us -> 51.3 us  [shift(): return lax.ppermute(x, ('dp', 'col'), pairs)]
    ppermute x12 -> x15, starting transfers between devices: 69.5 us -> 83.3 us  [shift(): return lax.ppermute(x, ('dp', 'col'), pairs)]
    all_to_all x1, blocking collectives: 41.7 us -> 54.6 us  [local(): got = lax.all_to_all(message, 'dp', split_axis=0, concat_axis=0, tiled=True)]
  transfers between devices with their start and end apart: 12 -> 15, of which waited for: 11 -> 11; matrix products, arithmetic and copies ran while one was open for 0% -> 0% of each run, Pallas kernels for 4% -> 4%
where the time goes in v3:
time: 219 us; the launch traced here: 218 us
  starting transfers between devices  83.3 us (38%)
  blocking collectives  54.6 us (25%)
  waiting for transfers between devices  51.3 us (23%)
  Pallas kernels  23.2 us (11%)
  local copies, waits for them, and re-layouts  3.79 us (2%)
    ppermute x15, starting transfers between devices, shift(): return lax.ppermute(x, ('dp', 'col'), pairs)  83.3 us
    all_to_all x1, blocking collectives, local(): got = lax.all_to_all(message, 'dp', split_axis=0, concat_axis=0, tiled=True)  54.6 us
    ppermute x15, waiting for transfers between devices, shift(): return lax.ppermute(x, ('dp', 'col'), pairs)  51.3 us
    pallas_call x7, Pallas kernels, call(): pl.pallas_call(kernel, out_shape=out_shape, in_specs=[scalar] * len(smem)...  23.2 us
  transfers between devices with their start and end apart: 15, of which 11 were waited for; matrix products, arithmetic and copies ran while one was open for 0% of the time, Pallas kernels for 4%

profile of v3, /device:TPU:1, one launch (start us, length us, event | category | flops | bytes accessed | tf_op | source)
XLA Modules:
  0.0 218.3 jit_solution(12456743831659115569)
XLA Ops:
  1.7 1.2 copy-done.3
  2.9 1.4 shard_map.131
  4.3 5.2 %collective-permute-start.1 = (bf16[512,512]{1,0:T(8,128)(2,1)S(1)}, bf16[512,512]{1,0:T(8,128)(2,1)S(1)}, u32[]{:S(2)}, u32[]{:S(2)}) collective-permute-start(bf16[512,512]{1,0:T(8,128)(2,1)S(1)} %get-tuple-element.53), channel_id=1, source_target_pairs={{0,4},{1,5},{2,6},{3,7},{4,0},{5,1},{6,2},{7,3},{8,12},{9,13},{10,... | collective-permute-start | bytes 1572872 | tf_op jit(solution)/shard_map/ppermute | solution.py:295
  9.5 1.9 collective-permute-start
  11.4 4.6 %collective-permute-done.1 = bf16[512,512]{1,0:T(8,128)(2,1)S(1)} collective-permute-done((bf16[512,512]{1,0:T(8,128)(2,1)S(1)}, bf16[512,512]{1,0:T(8,128)(2,1)S(1)}, u32[]{:S(2)}, u32[]{:S(2)}) %collective-permute-start.1) | collective-permute-done | bytes 524320 | tf_op jit(solution)/shard_map/ppermute | solution.py:295
  16.2 2.1 collective-permute-start.2
  18.4 3.3 %collective-permute-done.near = bf16[512,512]{1,0:T(8,128)(2,1)S(1)} collective-permute-done((bf16[512,512]{1,0:T(8,128)(2,1)S(1)}, bf16[512,512]{1,0:T(8,128)(2,1)S(1)}, u32[]{:S(2)}, u32[]{:S(2)}) %collective-permute-start) | collective-permute-done | bytes 524320 | tf_op jit(solution)/shard_map/ppermute | solution.py:295
  21.7 7.6 %collective-permute-done.2.far = bf16[512,512]{1,0:T(8,128)(2,1)S(1)} collective-permute-done((bf16[512,512]{1,0:T(8,128)(2,1)S(1)}, bf16[512,512]{1,0:T(8,128)(2,1)S(1)}, u32[]{:S(2)}, u32[]{:S(2)}) %collective-permute-start.2) | collective-permute-done | bytes 524320 | tf_op jit(solution)/shard_map/ppermute | solution.py:295
  30.2 21.2 %collective-permute-start.3 = (bf16[128,512]{1,0:T(8,128)(2,1)S(1)}, bf16[128,512]{1,0:T(8,128)(2,1)S(1)}, u32[]{:S(2)}, u32[]{:S(2)}) collective-permute-start(bf16[128,512]{1,0:T(8,128)(2,1)S(1)} %get-tuple-element.62), channel_id=1, source_target_pairs={{0,1},{1,0},{2,3},{3,2},{4,5},{5,4},{6,7},{7,6},{8,9},{9,8},{10,11... | collective-permute-start | bytes 393224 | tf_op jit(solution)/shard_map/ppermute | solution.py:295
  51.4 1.9 collective-permute-start.5
  53.4 9.1 %shard_map.133 = (f32[64,256]{1,0:T(8,128)S(1)}, f32[64,256]{1,0:T(8,128)S(1)}, f32[64,256]{1,0:T(8,128)S(1)}, bf16[128,512]{1,0:T(8,128)(2,1)S(1)}, bf16[128,51...) custom-call(s32[2]{0:T(128)S(1)} %pad_add_fusion.1.place, s32[2,4096]{1,0:T(2,128)S(1)} %bitcast.16, ...), custom_call_target="tpu_custom_call" | custom-call | flops 2000000000 | bytes 10000000 | tf_op jit(solution)/shard_map/pallas_call | solution.py:40
  62.5 9.4 %collective-permute-start.4 = (bf16[128,512]{1,0:T(8,128)(2,1)S(1)}, bf16[128,512]{1,0:T(8,128)(2,1)S(1)}, u32[]{:S(2)}, u32[]{:S(2)}) collective-permute-start(bf16[128,512]{1,0:T(8,128)(2,1)S(1)} %add_convert_fusion.2), channel_id=1, source_target_pairs={{0,3},{1,2},{2,1},{3,0},{4,7},{5,6},{6,5},{7,4},{8,11},{9,10},{10,... | collective-permute-start | bytes 393224 | tf_op jit(solution)/shard_map/ppermute | solution.py:295
  72.0 1.2 collective-permute-done.5.near
  73.2 4.5 %collective-permute-start.6 = (bf16[128,512]{1,0:T(8,128)(2,1)S(1)}, bf16[128,512]{1,0:T(8,128)(2,1)S(1)}, u32[]{:S(2)}, u32[]{:S(2)}) collective-permute-start(bf16[128,512]{1,0:T(8,128)(2,1)S(1)} %get-tuple-element.78), channel_id=1, source_target_pairs={{0,4},{1,5},{2,6},{3,7},{4,0},{5,1},{6,2},{7,3},{8,12},{9,13},{10,... | collective-permute-start | bytes 393224 | tf_op jit(solution)/shard_map/ppermute | solution.py:295
  77.7 9.1 %collective-permute-start.7 = (bf16[128,512]{1,0:T(8,128)(2,1)S(1)}, bf16[128,512]{1,0:T(8,128)(2,1)S(1)}, u32[]{:S(2)}, u32[]{:S(2)}) collective-permute-start(bf16[128,512]{1,0:T(8,128)(2,1)S(1)} %get-tuple-element.79), channel_id=1, source_target_pairs={{0,12},{1,13},{2,14},{3,15},{4,8},{5,9},{6,10},{7,11},{8,4},{9,5},... | collective-permute-start | bytes 393224 | tf_op jit(solution)/shard_map/ppermute | solution.py:295
  86.8 2.5 %collective-permute-start.8 = (bf16[128,512]{1,0:T(8,128)(2,1)S(1)}, bf16[128,512]{1,0:T(8,128)(2,1)S(1)}, u32[]{:S(2)}, u32[]{:S(2)}) collective-permute-start(bf16[128,512]{1,0:T(8,128)(2,1)S(1)} %get-tuple-element.80), channel_id=1, source_target_pairs={{0,8},{1,9},{2,10},{3,11},{4,12},{5,13},{6,14},{7,15},{8,0},{9,1},... | collective-permute-start | bytes 393224 | tf_op jit(solution)/shard_map/ppermute | solution.py:295
  90.1 4.0 %collective-permute-done.8.w_diag = bf16[128,512]{1,0:T(8,128)(2,1)S(1)} collective-permute-done((bf16[128,512]{1,0:T(8,128)(2,1)S(1)}, bf16[128,512]{1,0:T(8,128)(2,1)S(1)}, u32[]{:S(2)}, u32[]{:S(2)}) %collective-permute-start.8) | collective-permute-done | bytes 131104 | tf_op jit(solution)/shard_map/ppermute | solution.py:295
  94.2 2.7 %collective-permute-start.9 = (bf16[128,512]{1,0:T(8,128)(2,1)S(1)}, bf16[128,512]{1,0:T(8,128)(2,1)S(1)}, u32[]{:S(2)}, u32[]{:S(2)}) collective-permute-start(bf16[128,512]{1,0:T(8,128)(2,1)S(1)} %get-tuple-element.87.g_own), channel_id=1, source_target_pairs={{0,4},{1,5},{2,6},{3,7},{4,0},{5,1},{6,2},{7,3},{8,12},{9,13},{10,... | collective-permute-start | bytes 393224 | tf_op jit(solution)/shard_map/ppermute | solution.py:295
  97.0 1.9 collective-permute-start.10
  98.9 2.2 %collective-permute-done.9.g_near = bf16[128,512]{1,0:T(8,128)(2,1)S(1)} collective-permute-done((bf16[128,512]{1,0:T(8,128)(2,1)S(1)}, bf16[128,512]{1,0:T(8,128)(2,1)S(1)}, u32[]{:S(2)}, u32[]{:S(2)}) %collective-permute-start.9) | collective-permute-done | bytes 131104 | tf_op jit(solution)/shard_map/ppermute | solution.py:295
  101.2 1.9 collective-permute-start.11
  103.1 3.8 %collective-permute-done.11.g_diag = bf16[128,512]{1,0:T(8,128)(2,1)S(1)} collective-permute-done((bf16[128,512]{1,0:T(8,128)(2,1)S(1)}, bf16[128,512]{1,0:T(8,128)(2,1)S(1)}, u32[]{:S(2)}, u32[]{:S(2)}) %collective-permute-start.11) | collective-permute-done | bytes 131104 | tf_op jit(solution)/shard_map/ppermute | solution.py:295
  106.9 1.3 shard_map.135
  108.2 13.4 %collective-permute-start.13 = (bf16[128,512]{1,0:T(8,128)(2,1)S(1)}, bf16[128,512]{1,0:T(8,128)(2,1)S(1)}, u32[]{:S(2)}, u32[]{:S(2)}) collective-permute-start(bf16[128,512]{1,0:T(8,128)(2,1)S(1)} %get-tuple-element.91), channel_id=1, source_target_pairs={{0,1},{1,0},{2,3},{3,2},{4,5},{5,4},{6,7},{7,6},{8,9},{9,8},{10,11... | collective-permute-start | bytes 393224 | tf_op jit(solution)/shard_map/ppermute | solution.py:295
  121.6 1.9 collective-permute-start.12
  123.6 11.3 %collective-permute-done.13 = bf16[128,512]{1,0:T(8,128)(2,1)S(1)} collective-permute-done((bf16[128,512]{1,0:T(8,128)(2,1)S(1)}, bf16[128,512]{1,0:T(8,128)(2,1)S(1)}, u32[]{:S(2)}, u32[]{:S(2)}) %collective-permute-start.13) | collective-permute-done | bytes 131104 | tf_op jit(solution)/shard_map/ppermute | solution.py:295
  134.9 3.5 %collective-permute-start.14 = (bf16[128,512]{1,0:T(8,128)(2,1)S(1)}, bf16[128,512]{1,0:T(8,128)(2,1)S(1)}, u32[]{:S(2)}, u32[]{:S(2)}) collective-permute-start(bf16[128,512]{1,0:T(8,128)(2,1)S(1)} %add_convert_fusion.1), channel_id=1, source_target_pairs={{0,3},{1,2},{2,1},{3,0},{4,7},{5,6},{6,5},{7,4},{8,11},{9,10},{10,... | collective-permute-start | bytes 393224 | tf_op jit(solution)/shard_map/ppermute | solution.py:295
  138.9 4.8 %collective-permute-done.12.near = bf16[128,512]{1,0:T(8,128)(2,1)S(1)} collective-permute-done((bf16[128,512]{1,0:T(8,128)(2,1)S(1)}, bf16[128,512]{1,0:T(8,128)(2,1)S(1)}, u32[]{:S(2)}, u32[]{:S(2)}) %collective-permute-start.12) | collective-permute-done | bytes 131104 | tf_op jit(solution)/shard_map/ppermute | solution.py:295
  143.8 7.7 %collective-permute-done.14.far = bf16[128,512]{1,0:T(8,128)(2,1)S(1)} collective-permute-done((bf16[128,512]{1,0:T(8,128)(2,1)S(1)}, bf16[128,512]{1,0:T(8,128)(2,1)S(1)}, u32[]{:S(2)}, u32[]{:S(2)}) %collective-permute-start.14) | collective-permute-done | bytes 131104 | tf_op jit(solution)/shard_map/ppermute | solution.py:295
  151.5 5.9 %shard_map.136 = bf16[64,24,128]{2,1,0:T(8,128)(2,1)S(1)} custom-call(bf16[128,512]{1,0:T(8,128)(2,1)S(1)} %get-tuple-element.88.own, bf16[128,512]{1,0:T(8,128)(2,1)S(1)} %collective-permute-done.12.near, bf16[128,512]{1,0:T(8,128)(2,1)S(1)} %collective-permute-done.14.far, f32[128,512]{1,0:T(8,128)S(1)} %get-tuple-element.92.back_one, ...), custom_call_target="tpu_custom_call" | custom-call | flops 2000000000 | bytes 10000000 | tf_op jit(solution)/shard_map/pallas_call | solution.py:40
  157.4 54.6 %all_to_all.5.got = bf16[64,24,128]{2,1,0:T(8,128)(2,1)S(1)} all-to-all(bf16[64,24,128]{2,1,0:T(8,128)(2,1)S(1)} %shard_map.136), channel_id=1, replica_groups=mesh['dp'=64,'col'=16] {'dp'}, dimensions={0} | all-to-all | bytes 786432 | tf_op jit(solution)/shard_map/all_to_all | solution.py:387
  212.0 4.5 %shard_map.137 = (f32[16,512]{1,0:T(8,128)}, f32[1,128]{1,0:T(1,128)S(1)}) custom-call(bf16[64,24,128]{2,1,0:T(8,128)(2,1)S(1)} %all_to_all.5.got), custom_call_target="tpu_custom_call" | custom-call | flops 2000000000 | bytes 10000000 | tf_op jit(solution)/shard_map/pallas_call | solution.py:40
  (41 shorter events, 5.4 us)
Async XLA Ops:
  0.6 1.0 copy-start.5
  0.7 0.9 copy-start.10
  1.7 1.2 copy-start.3
  4.3 11.8 %collective-permute-start.1 = (bf16[512,512]{1,0:T(8,128)(2,1)S(1)}, bf16[512,512]{1,0:T(8,128)(2,1)S(1)}, u32[]{:S(2)}, u32[]{:S(2)}) collective-permute-start(bf16[512,512]{1,0:T(8,128)(2,1)S(1)} %get-tuple-element.53), channel_id=1, source_target_pairs={{0,4},{1,5},{2,6},{3,7},{4,0},{5,1},{6,2},{7,3},{8,12},{9,13},{10,... | collective-permute-start | bytes 1572872 | tf_op jit(solution)/shard_map/ppermute | solution.py:295
  9.5 12.2 %collective-permute-start = (bf16[512,512]{1,0:T(8,128)(2,1)S(1)}, bf16[512,512]{1,0:T(8,128)(2,1)S(1)}, u32[]{:S(2)}, u32[]{:S(2)}) collective-permute-start(bf16[512,512]{1,0:T(8,128)(2,1)S(1)} %get-tuple-element.51), channel_id=1, source_target_pairs={{0,4},{1,5},{2,6},{3,7},{4,0},{5,1},{6,2},{7,3},{8,12},{9,13},{10,... | collective-permute-start | bytes 1572872 | tf_op jit(solution)/shard_map/ppermute | solution.py:295
  16.2 13.1 %collective-permute-start.2 = (bf16[512,512]{1,0:T(8,128)(2,1)S(1)}, bf16[512,512]{1,0:T(8,128)(2,1)S(1)}, u32[]{:S(2)}, u32[]{:S(2)}) collective-permute-start(bf16[512,512]{1,0:T(8,128)(2,1)S(1)} %add_convert_fusion), channel_id=1, source_target_pairs={{0,12},{1,13},{2,14},{3,15},{4,8},{5,9},{6,10},{7,11},{8,4},{9,5},... | collective-permute-start | bytes 1572872 | tf_op jit(solution)/shard_map/ppermute | solution.py:295
  29.2 24.1 %copy-start.1 = (s32[4096,2]{0,1:T(2,128)S(1)}, s32[4096,2]{0,1:T(2,128)}, u32[]{:S(2)}) copy-start(s32[4096,2]{0,1:T(2,128)} %param.22) | copy-start | bytes 98308
  29.2 24.1 %copy-start.2 = (s32[4096]{0:T(1024)S(1)}, s32[4096]{0:T(1024)}, u32[]{:S(2)}) copy-start(s32[4096]{0:T(1024)} %param.23) | copy-start | bytes 49156
  29.3 24.1 %copy-start.4 = (bf16[128,2048]{1,0:T(8,128)(2,1)S(1)}, bf16[128,2048]{1,0:T(8,128)(2,1)}, u32[]{:S(2)}) copy-start(bf16[128,2048]{1,0:T(8,128)(2,1)} %weight.2) | copy-start | bytes 1572868
  29.3 24.1 %copy-start.7 = (s32[4096,2]{0,1:T(2,128)S(1)}, s32[4096,2]{0,1:T(2,128)}, u32[]{:S(2)}) copy-start(s32[4096,2]{0,1:T(2,128)} %param.20) | copy-start | bytes 98308
  29.3 24.1 %copy-start.8 = (s32[4096,2]{0,1:T(2,128)S(1)}, s32[4096,2]{0,1:T(2,128)}, u32[]{:S(2)}) copy-start(s32[4096,2]{0,1:T(2,128)} %param.21) | copy-start | bytes 98308
  30.2 32.2 %collective-permute-start.3 = (bf16[128,512]{1,0:T(8,128)(2,1)S(1)}, bf16[128,512]{1,0:T(8,128)(2,1)S(1)}, u32[]{:S(2)}, u32[]{:S(2)}) collective-permute-start(bf16[128,512]{1,0:T(8,128)(2,1)S(1)} %get-tuple-element.62), channel_id=1, source_target_pairs={{0,1},{1,0},{2,3},{3,2},{4,5},{5,4},{6,7},{7,6},{8,9},{9,8},{10,11... | collective-permute-start | bytes 393224 | tf_op jit(solution)/shard_map/ppermute | solution.py:295
  51.4 21.8 %collective-permute-start.5 = (bf16[128,512]{1,0:T(8,128)(2,1)S(1)}, bf16[128,512]{1,0:T(8,128)(2,1)S(1)}, u32[]{:S(2)}, u32[]{:S(2)}) collective-permute-start(bf16[128,512]{1,0:T(8,128)(2,1)S(1)} %get-tuple-element.74), channel_id=1, source_target_pairs={{0,1},{1,0},{2,3},{3,2},{4,5},{5,4},{6,7},{7,6},{8,9},{9,8},{10,11... | collective-permute-start | bytes 393224 | tf_op jit(solution)/shard_map/ppermute | solution.py:295
  62.5 31.7 %copy-start = (bf16[512,128]{1,0:T(8,128)(2,1)S(1)}, bf16[512,128]{1,0:T(8,128)(2,1)}, u32[]{:S(2)}) copy-start(bf16[512,128]{1,0:T(8,128)(2,1)} %embedded.1) | copy-start | bytes 393220
  62.5 26.8 %collective-permute-start.4 = (bf16[128,512]{1,0:T(8,128)(2,1)S(1)}, bf16[128,512]{1,0:T(8,128)(2,1)S(1)}, u32[]{:S(2)}, u32[]{:S(2)}) collective-permute-start(bf16[128,512]{1,0:T(8,128)(2,1)S(1)} %add_convert_fusion.2), channel_id=1, source_target_pairs={{0,3},{1,2},{2,1},{3,0},{4,7},{5,6},{6,5},{7,4},{8,11},{9,10},{10,... | collective-permute-start | bytes 393224 | tf_op jit(solution)/shard_map/ppermute | solution.py:295
  73.2 16.2 %collective-permute-start.6 = (bf16[128,512]{1,0:T(8,128)(2,1)S(1)}, bf16[128,512]{1,0:T(8,128)(2,1)S(1)}, u32[]{:S(2)}, u32[]{:S(2)}) collective-permute-start(bf16[128,512]{1,0:T(8,128)(2,1)S(1)} %get-tuple-element.78), channel_id=1, source_target_pairs={{0,4},{1,5},{2,6},{3,7},{4,0},{5,1},{6,2},{7,3},{8,12},{9,13},{10,... | collective-permute-start | bytes 393224 | tf_op jit(solution)/shard_map/ppermute | solution.py:295
  77.7 12.4 %collective-permute-start.7 = (bf16[128,512]{1,0:T(8,128)(2,1)S(1)}, bf16[128,512]{1,0:T(8,128)(2,1)S(1)}, u32[]{:S(2)}, u32[]{:S(2)}) collective-permute-start(bf16[128,512]{1,0:T(8,128)(2,1)S(1)} %get-tuple-element.79), channel_id=1, source_target_pairs={{0,12},{1,13},{2,14},{3,15},{4,8},{5,9},{6,10},{7,11},{8,4},{9,5},... | collective-permute-start | bytes 393224 | tf_op jit(solution)/shard_map/ppermute | solution.py:295
  86.8 7.3 %collective-permute-start.8 = (bf16[128,512]{1,0:T(8,128)(2,1)S(1)}, bf16[128,512]{1,0:T(8,128)(2,1)S(1)}, u32[]{:S(2)}, u32[]{:S(2)}) collective-permute-start(bf16[128,512]{1,0:T(8,128)(2,1)S(1)} %get-tuple-element.80), channel_id=1, source_target_pairs={{0,8},{1,9},{2,10},{3,11},{4,12},{5,13},{6,14},{7,15},{8,0},{9,1},... | collective-permute-start | bytes 393224 | tf_op jit(solution)/shard_map/ppermute | solution.py:295
  94.2 6.9 %collective-permute-start.9 = (bf16[128,512]{1,0:T(8,128)(2,1)S(1)}, bf16[128,512]{1,0:T(8,128)(2,1)S(1)}, u32[]{:S(2)}, u32[]{:S(2)}) collective-permute-start(bf16[128,512]{1,0:T(8,128)(2,1)S(1)} %get-tuple-element.87.g_own), channel_id=1, source_target_pairs={{0,4},{1,5},{2,6},{3,7},{4,0},{5,1},{6,2},{7,3},{8,12},{9,13},{10,... | collective-permute-start | bytes 393224 | tf_op jit(solution)/shard_map/ppermute | solution.py:295
  97.0 6.1 %collective-permute-start.10 = (bf16[128,512]{1,0:T(8,128)(2,1)S(1)}, bf16[128,512]{1,0:T(8,128)(2,1)S(1)}, u32[]{:S(2)}, u32[]{:S(2)}) collective-permute-start(bf16[128,512]{1,0:T(8,128)(2,1)S(1)} %get-tuple-element.87.g_own), channel_id=1, source_target_pairs={{0,12},{1,13},{2,14},{3,15},{4,8},{5,9},{6,10},{7,11},{8,4},{9,5},... | collective-permute-start | bytes 393224 | tf_op jit(solution)/shard_map/ppermute | solution.py:295
  101.2 5.7 %collective-permute-start.11 = (bf16[128,512]{1,0:T(8,128)(2,1)S(1)}, bf16[128,512]{1,0:T(8,128)(2,1)S(1)}, u32[]{:S(2)}, u32[]{:S(2)}) collective-permute-start(bf16[128,512]{1,0:T(8,128)(2,1)S(1)} %collective-permute-done.9.g_near), channel_id=1, source_target_pairs={{0,12},{1,13},{2,14},{3,15},{4,8},{5,9},{6,10},{7,11},{8,4},{9,5},... | collective-permute-start | bytes 393224 | tf_op jit(solution)/shard_map/ppermute | solution.py:295
  108.2 26.7 %collective-permute-start.13 = (bf16[128,512]{1,0:T(8,128)(2,1)S(1)}, bf16[128,512]{1,0:T(8,128)(2,1)S(1)}, u32[]{:S(2)}, u32[]{:S(2)}) collective-permute-start(bf16[128,512]{1,0:T(8,128)(2,1)S(1)} %get-tuple-element.91), channel_id=1, source_target_pairs={{0,1},{1,0},{2,3},{3,2},{4,5},{5,4},{6,7},{7,6},{8,9},{9,8},{10,11... | collective-permute-start | bytes 393224 | tf_op jit(solution)/shard_map/ppermute | solution.py:295
  121.6 22.2 %collective-permute-start.12 = (bf16[128,512]{1,0:T(8,128)(2,1)S(1)}, bf16[128,512]{1,0:T(8,128)(2,1)S(1)}, u32[]{:S(2)}, u32[]{:S(2)}) collective-permute-start(bf16[128,512]{1,0:T(8,128)(2,1)S(1)} %get-tuple-element.89), channel_id=1, source_target_pairs={{0,1},{1,0},{2,3},{3,2},{4,5},{5,4},{6,7},{7,6},{8,9},{9,8},{10,11... | collective-permute-start | bytes 393224 | tf_op jit(solution)/shard_map/ppermute | solution.py:295
  134.8 3.6 %copy-start.9 = (s32[4096,2]{0,1:T(2,128)S(1)}, s32[4096,2]{0,1:T(2,128)}, u32[]{:S(2)}) copy-start(s32[4096,2]{0,1:T(2,128)} %param.19) | copy-start | bytes 98308
  134.9 16.6 %collective-permute-start.14 = (bf16[128,512]{1,0:T(8,128)(2,1)S(1)}, bf16[128,512]{1,0:T(8,128)(2,1)S(1)}, u32[]{:S(2)}, u32[]{:S(2)}) collective-permute-start(bf16[128,512]{1,0:T(8,128)(2,1)S(1)} %add_convert_fusion.1), channel_id=1, source_target_pairs={{0,3},{1,2},{2,1},{3,0},{4,7},{5,6},{6,5},{7,4},{8,11},{9,10},{10,... | collective-permute-start | bytes 393224 | tf_op jit(solution)/shard_map/ppermute | solution.py:295
  138.8 12.7 %copy-start.6 = (bf16[512,128]{1,0:T(8,128)(2,1)S(1)}, bf16[512,128]{1,0:T(8,128)(2,1)}, u32[]{:S(2)}) copy-start(bf16[512,128]{1,0:T(8,128)(2,1)} %gate.1) | copy-start | bytes 393220

commit v4 on v3

--- a/solution.py
+++ b/solution.py
@@ -1,3 +1,5 @@
+import functools
+
 import jax
 import jax.numpy as jnp
 from jax import lax
@@ -68,8 +70,9 @@
 
 
 def hidden_kernel(place, weight, pre_hidden, upstream, out_weight, *refs):
+    scale = jnp.broadcast_to(upstream[...], (8, upstream.shape[1])).T[:, :1]
     slope = jnp.where(
-        pre_hidden[...] > 0, upstream[...] * out_weight[...].astype(F32), 0.0
+        pre_hidden[...] > 0, scale * out_weight[...].astype(F32), 0.0
     ).astype(BF16)
     rows = refs[0].shape[0]
 
@@ -85,8 +88,8 @@
     return own[...].astype(F32) + near[...].astype(F32) + far[...].astype(F32)
 
 
-def mid_kernel(place, own, near, far, *refs):
-    total = refs[4]
+def mid_kernel(place, outer_place, own, near, far, weight, *refs):
+    total = refs[8]
     total[...] = joined((own, near, far)).astype(BF16)
     rows = refs[0].shape[0]
 
@@ -94,6 +97,12 @@
         return total[pl.ds(pl.multiple_of(block * rows, rows), rows), :]
 
     store_blocks(make, place, *refs[:4])
+    span = refs[4].shape[1]
+
+    def weight_block(block):
+        return weight[:, pl.ds(pl.multiple_of(block * span, span), span)]
+
+    store_blocks(weight_block, outer_place, *refs[4:8])
 
 
 def gate_kernel(own, near, far, embedded, back_one, gated):
@@ -120,21 +129,15 @@
     return ((MAIN + (row & (MAIN - 1))) << (row >> 7)).astype(F32)
 
 
-def plan_kernel(place, owner, rows, flag, bags, weight, group, sample, code, *blocks):
-    span = blocks[0].shape[1]
-
-    def make(block):
-        return weight[:, pl.ds(pl.multiple_of(block * span, span), span)]
-
-    store_blocks(make, place, *blocks)
+def plan_kernel(begin, end, owner, rows, flag, bags, *refs):
     width = 512
-    owners = group.shape[0]
+    before_parts, outs, parts = (refs[:4], refs[4:7], refs[7:]) if begin else ((), (), refs)
+    owners = parts[0].shape[0]
     ahead = one_hot(iota((width, width), 0) < iota((width, width), 1))
     owner_ids = iota((owners, width), 0)
-    lane_slot = iota((LANES, width), 0)
-    slot_ids = jnp.where(lane_slot < MAIN, lane_slot, MAIN + lane_slot % TAIL).astype(F32)
-    for part in (group, sample, code):
-        part[...] = jnp.zeros_like(part)
+    slot_ids = iota((CAP, width), 0).astype(F32)
+    for i, part in enumerate(parts):
+        part[...] = before_parts[i][...] if begin else jnp.zeros_like(part)
 
     def step(chunk, used):
         at = pl.ds(pl.multiple_of(chunk * width, width), width)
@@ -149,12 +152,16 @@
             place = jnp.sum(jnp.where(hit, before, 0.0), axis=0, keepdims=True)
             taken = slot_ids == place
             code_of = row_code(rows[k : k + 1, at])
-            for part, value in ((group, group_of), (sample, sample_of), (code, code_of)):
+            for part, value in zip(parts, (group_of, sample_of, code_of)):
                 part[...] += mxu(match, jnp.where(taken, value, 0.0).astype(BF16), NT)
             used = used + jnp.sum(jnp.where(hit, 1.0, 0.0), axis=1, keepdims=True)
         return used
 
-    lax.fori_loop(0, owner.shape[1] // width, step, jnp.zeros((owners, 1), F32))
+    used = lax.fori_loop(begin, end, step, parts[3][:, :1])
+    parts[3][...] = jnp.broadcast_to(used, parts[3].shape)
+    for out, part in zip(outs, parts):
+        out[:, :MAIN] = part[:, :MAIN]
+        out[:, MAIN:] = jnp.concatenate([part[:, MAIN:]] * (MAIN // TAIL), axis=1)
 
 
 def send_kernel(
@@ -297,34 +304,35 @@
     def onward(second, first):
         return (second.astype(F32) + first.astype(F32)).astype(BF16)
 
-    def exchange(blocks, along_outer):
+    def exchange(blocks, along_outer, work=None, held=(), parts=()):
         diagonal, near, second, own = blocks
+        if work is not None:
+            held, diagonal = lax.optimization_barrier((held, diagonal))
         first = shift(diagonal, along_outer, 0)
         near = shift(near, along_outer, 0)
-        return own, near, shift(onward(second, first), along_outer, 1)
-
-    def exchange_beside(blocks, held):
-        diagonal, near, second, own = blocks
-        held, diagonal = lax.optimization_barrier((held, diagonal))
-        first = shift(diagonal, False, 0)
-        near = shift(near, False, 0)
-        *routes, w_diag, w_near, w_far, w_own = call(
-            plan_kernel,
-            [jax.ShapeDtypeStruct((owners, LANES), F32)] * 3 + blocks_of(cols, outer_rows),
+        parts = tuple(shift(part, True, turn) for part, turn in zip(parts, (0, 1, None)))
+        done = ()
+        if work is not None:
+            done = tuple(work(held))
+            first, done, parts = lax.optimization_barrier((first, done, parts))
+        return (own, near, shift(onward(second, first), along_outer, 1)), done, parts
+
+    state = [jax.ShapeDtypeStruct((owners, CAP), F32)] * 3
+    state += [jax.ShapeDtypeStruct((owners, MAIN), F32)]
+    chunks = cold_owner.shape[0] // 512
+
+    def plan(begin, end, out_shape, scratch=()):
+        return lambda held: call(
+            functools.partial(plan_kernel, begin, end),
+            out_shape,
             held,
-            smem=(outer_place,),
-            flops=2 * 10**9,
-            moved=10**7,
+            scratch=scratch,
+            flops=5 * 10**8,
+            moved=0,
         )
-        first, routes, parts = lax.optimization_barrier((first, routes, (w_near, w_far, w_diag)))
-        far = onward(second, first)
-        far, parts = lax.optimization_barrier((far, parts))
-        far = shift(far, False, 1)
-        near, parts = lax.optimization_barrier((near, parts))
-        parts = tuple(shift(part, True, turn) for part, turn in zip(parts, (0, 1, None)))
-        far, parts = lax.optimization_barrier((far, parts))
-        return (own, near, far), routes, (w_own, *parts)
-
+
+    routing = [jax.ShapeDtypeStruct((owners, LANES), F32)] * 3
+    slots_in = (cold_owner.T, cold_rows.T, hot_flag.T, bag_sizes[None, :])
     live = lax.broadcasted_iota(jnp.int32, hot_rows.shape, 1) < bag_sizes[:, None]
     hot_index = (
         jnp.where(live & (hot_flag == 1), hot_rows, -1)
@@ -336,9 +344,9 @@
     def stage_two(terms):
         return call(
             mid_kernel,
-            blocks_of(cols, samples),
-            terms,
-            smem=(inner_place,),
+            blocks_of(cols, samples) + blocks_of(cols, outer_rows),
+            terms + (cross_weight,),
+            smem=(inner_place, outer_place),
             scratch=[pltpu.VMEM((outer_rows, samples), BF16)],
             flops=4 * outer_rows * samples,
             moved=10 * outer_rows * samples,
@@ -347,15 +355,17 @@
     blocks = call(
         hidden_kernel,
         blocks_of(outer_rows, samples),
-        (hidden_weight, pre_hidden, upstream[:, None], out_weight[None, :]),
+        (hidden_weight, pre_hidden, upstream[None, :], out_weight[None, :]),
         smem=(outer_place,),
         flops=2 * total_cols * samples * pre_hidden.shape[1],
         moved=4 * total_cols * samples,
     )
-    terms, routes, weights = exchange_beside(
-        stage_two(exchange(blocks, True)),
-        (cold_owner.T, cold_rows.T, hot_flag.T, bag_sizes[None, :], cross_weight),
-    )
+    terms, _, _ = exchange(blocks, True)
+    *blocks, w_diag, w_near, w_far, w_own = stage_two(terms)
+    terms, planned, parts = exchange(
+        blocks, False, plan(0, chunks // 2, state), slots_in, (w_near, w_far, w_diag)
+    )
+    weights = (w_own, *parts)
     back_one, gated = call(
         gate_kernel,
         [jax.ShapeDtypeStruct((cols, samples), F32), jax.ShapeDtypeStruct((cols, samples), BF16)],
@@ -375,7 +385,9 @@
         flops=2 * total_cols * samples * cols,
         moved=4 * outer_rows * samples,
     )
-    terms = exchange(blocks, False)
+    terms, routes, _ = exchange(
+        blocks, False, plan(chunks // 2, chunks, routing, [pltpu.VMEM(x.shape, F32) for x in state]), slots_in + planned
+    )
     message = call(
         send_kernel,
         jax.ShapeDtypeStruct((owners, MSG_ROWS, MAIN), BF16),

time: 219 us -> 210 us (0.959)
  blocking collectives: 54.6 us -> 35.3 us
  starting transfers between devices: 83.3 us -> 92.2 us
    all_to_all x1, blocking collectives: 54.6 us -> 35.3 us  [local(): got = lax.all_to_all(message, 'dp', split_axis=0, concat_axis=0, tiled=True)]
    ppermute x15, starting transfers between devices: 83.3 us -> 92.2 us  [shift(): return lax.ppermute(x, ('dp', 'col'), pairs)]
    unnamed x22 -> x24, local copies, waits for them, and re-layouts: 1.27 us -> 3.47 us
    pallas_call x7 -> x8, Pallas kernels: 23.2 us -> 21.6 us  [call(): pl.pallas_call(kernel, out_shape=out_shape, in_specs=[scalar] * len(smem)...]
  transfers between devices with their start and end apart: 15 -> 15, of which waited for: 11 -> 8; matrix products, arithmetic and copies ran while one was open for 0% -> 0% of each run, Pallas kernels for 4% -> 4%
where the time goes in v4:
time: 210 us; the launch traced here: 207 us
  starting transfers between devices  92.2 us (44%)
  waiting for transfers between devices  50.9 us (24%)
  blocking collectives  35.3 us (17%)
  Pallas kernels  21.6 us (10%)
  local copies, waits for them, and re-layouts  5.12 us (2%)
    ppermute x15, starting transfers between devices, shift(): return lax.ppermute(x, ('dp', 'col'), pairs)  92.2 us
    ppermute x15, waiting for transfers between devices, shift(): return lax.ppermute(x, ('dp', 'col'), pairs)  50.9 us
    all_to_all x1, blocking collectives, local(): got = lax.all_to_all(message, 'dp', split_axis=0, concat_axis=0, tiled=True)  35.3 us
    pallas_call x8, Pallas kernels, call(): pl.pallas_call(kernel, out_shape=out_shape, in_specs=[scalar] * len(smem)...  21.6 us
  transfers between devices with their start and end apart: 15, of which 8 were waited for; matrix products, arithmetic and copies ran while one was open for 0% of the time, Pallas kernels for 4%

profile of v4, /device:TPU:1, one launch (start us, length us, event | category | flops | bytes accessed | tf_op | source)
XLA Modules:
  0.0 207.1 jit_solution(6833919268192843229)
XLA Ops:
  2.0 1.2 copy-done.4
  4.2 1.5 shard_map.131
  5.7 5.2 %collective-permute-start.1 = (bf16[512,512]{1,0:T(8,128)(2,1)S(1)}, bf16[512,512]{1,0:T(8,128)(2,1)S(1)}, u32[]{:S(2)}, u32[]{:S(2)}) collective-permute-start(bf16[512,512]{1,0:T(8,128)(2,1)S(1)} %get-tuple-element.58), channel_id=1, source_target_pairs={{0,4},{1,5},{2,6},{3,7},{4,0},{5,1},{6,2},{7,3},{8,12},{9,13},{10,... | collective-permute-start | bytes 1572872 | tf_op jit(solution)/shard_map/ppermute | solution.py:302
  10.9 1.9 collective-permute-start
  12.9 4.6 %collective-permute-done.1 = bf16[512,512]{1,0:T(8,128)(2,1)S(1)} collective-permute-done((bf16[512,512]{1,0:T(8,128)(2,1)S(1)}, bf16[512,512]{1,0:T(8,128)(2,1)S(1)}, u32[]{:S(2)}, u32[]{:S(2)}) %collective-permute-start.1) | collective-permute-done | bytes 524320 | tf_op jit(solution)/shard_map/ppermute | solution.py:302
  17.6 2.2 %collective-permute-start.2 = (bf16[512,512]{1,0:T(8,128)(2,1)S(1)}, bf16[512,512]{1,0:T(8,128)(2,1)S(1)}, u32[]{:S(2)}, u32[]{:S(2)}) collective-permute-start(bf16[512,512]{1,0:T(8,128)(2,1)S(1)} %add_convert_fusion), channel_id=1, source_target_pairs={{0,12},{1,13},{2,14},{3,15},{4,8},{5,9},{6,10},{7,11},{8,4},{9,5},... | collective-permute-start | bytes 1572872 | tf_op jit(solution)/shard_map/ppermute | solution.py:302
  20.0 3.2 %collective-permute-done.near = bf16[512,512]{1,0:T(8,128)(2,1)S(1)} collective-permute-done((bf16[512,512]{1,0:T(8,128)(2,1)S(1)}, bf16[512,512]{1,0:T(8,128)(2,1)S(1)}, u32[]{:S(2)}, u32[]{:S(2)}) %collective-permute-start) | collective-permute-done | bytes 524320 | tf_op jit(solution)/shard_map/ppermute | solution.py:302
  23.1 7.9 %collective-permute-done.2.far = bf16[512,512]{1,0:T(8,128)(2,1)S(1)} collective-permute-done((bf16[512,512]{1,0:T(8,128)(2,1)S(1)}, bf16[512,512]{1,0:T(8,128)(2,1)S(1)}, u32[]{:S(2)}, u32[]{:S(2)}) %collective-permute-start.2) | collective-permute-done | bytes 524320 | tf_op jit(solution)/shard_map/ppermute | solution.py:302
  31.0 1.0 shard_map.132
  32.0 20.9 %collective-permute-start.3 = (bf16[128,512]{1,0:T(8,128)(2,1)S(1)}, bf16[128,512]{1,0:T(8,128)(2,1)S(1)}, u32[]{:S(2)}, u32[]{:S(2)}) collective-permute-start(bf16[128,512]{1,0:T(8,128)(2,1)S(1)} %get-tuple-element.61), channel_id=1, source_target_pairs={{0,1},{1,0},{2,3},{3,2},{4,5},{5,4},{6,7},{7,6},{8,9},{9,8},{10,11... | collective-permute-start | bytes 393224 | tf_op jit(solution)/shard_map/ppermute | solution.py:302
  52.9 4.4 %collective-permute-start.4 = (bf16[128,512]{1,0:T(8,128)(2,1)S(1)}, bf16[128,512]{1,0:T(8,128)(2,1)S(1)}, u32[]{:S(2)}, u32[]{:S(2)}) collective-permute-start(bf16[128,512]{1,0:T(8,128)(2,1)S(1)} %get-tuple-element.70), channel_id=1, source_target_pairs={{0,4},{1,5},{2,6},{3,7},{4,0},{5,1},{6,2},{7,3},{8,12},{9,13},{10,... | collective-permute-start | bytes 393224 | tf_op jit(solution)/shard_map/ppermute | solution.py:302
  57.3 1.9 collective-permute-start.5
  59.2 3.3 %collective-permute-start.6 = (bf16[128,512]{1,0:T(8,128)(2,1)S(1)}, bf16[128,512]{1,0:T(8,128)(2,1)S(1)}, u32[]{:S(2)}, u32[]{:S(2)}) collective-permute-start(bf16[128,512]{1,0:T(8,128)(2,1)S(1)} %get-tuple-element.72), channel_id=1, source_target_pairs={{0,8},{1,9},{2,10},{3,11},{4,12},{5,13},{6,14},{7,15},{8,0},{9,1},... | collective-permute-start | bytes 393224 | tf_op jit(solution)/shard_map/ppermute | solution.py:302
  62.5 1.9 collective-permute-start.7
  64.4 3.6 %shard_map.133 = (f32[64,160]{1,0:T(8,128)S(1)}, f32[64,160]{1,0:T(8,128)S(1)}, f32[64,160]{1,0:T(8,128)S(1)}, f32[64,128]{1,0:T(8,128)S(1)}) custom-call(s32[2,4096]{1,0:T(2,128)S(1)} %bitcast.18, s32[2,4096]{1,0:T(2,128)S(1)} %bitcast.20, s32[2,4096]{1,0:T(2,128)S(1)} %bitcast.13, s32[1,4096]{1,0:T(1,128)S(1)} %bitcast.16), custom_call_target="tpu_custom_call" | custom-call | flops 500000000 | tf_op jit(solution)/shard_map/pallas_call | solution.py:42
  68.1 8.2 %collective-permute-start.8 = (bf16[128,512]{1,0:T(8,128)(2,1)S(1)}, bf16[128,512]{1,0:T(8,128)(2,1)S(1)}, u32[]{:S(2)}, u32[]{:S(2)}) collective-permute-start(bf16[128,512]{1,0:T(8,128)(2,1)S(1)} %add_convert_fusion.2), channel_id=1, source_target_pairs={{0,3},{1,2},{2,1},{3,0},{4,7},{5,6},{6,5},{7,4},{8,11},{9,10},{10,... | collective-permute-start | bytes 393224 | tf_op jit(solution)/shard_map/ppermute | solution.py:302
  76.3 1.0 collective-permute-done.7.near
  77.3 16.0 %collective-permute-done.8.far = bf16[128,512]{1,0:T(8,128)(2,1)S(1)} collective-permute-done((bf16[128,512]{1,0:T(8,128)(2,1)S(1)}, bf16[128,512]{1,0:T(8,128)(2,1)S(1)}, u32[]{:S(2)}, u32[]{:S(2)}) %collective-permute-start.8) | collective-permute-done | bytes 131104 | tf_op jit(solution)/shard_map/ppermute | solution.py:302
  93.5 2.9 %collective-permute-start.9 = (bf16[128,512]{1,0:T(8,128)(2,1)S(1)}, bf16[128,512]{1,0:T(8,128)(2,1)S(1)}, u32[]{:S(2)}, u32[]{:S(2)}) collective-permute-start(bf16[128,512]{1,0:T(8,128)(2,1)S(1)} %get-tuple-element.80.g_own), channel_id=1, source_target_pairs={{0,4},{1,5},{2,6},{3,7},{4,0},{5,1},{6,2},{7,3},{8,12},{9,13},{10,... | collective-permute-start | bytes 393224 | tf_op jit(solution)/shard_map/ppermute | solution.py:302
  96.4 1.9 collective-permute-start.10
  98.3 2.1 collective-permute-done.9.g_near
  100.4 1.9 collective-permute-start.11
  102.3 3.8 %collective-permute-done.11.g_diag = bf16[128,512]{1,0:T(8,128)(2,1)S(1)} collective-permute-done((bf16[128,512]{1,0:T(8,128)(2,1)S(1)}, bf16[128,512]{1,0:T(8,128)(2,1)S(1)}, u32[]{:S(2)}, u32[]{:S(2)}) %collective-permute-start.11) | collective-permute-done | bytes 131104 | tf_op jit(solution)/shard_map/ppermute | solution.py:302
  106.1 1.3 shard_map.135
  107.4 9.4 %collective-permute-start.13 = (bf16[128,512]{1,0:T(8,128)(2,1)S(1)}, bf16[128,512]{1,0:T(8,128)(2,1)S(1)}, u32[]{:S(2)}, u32[]{:S(2)}) collective-permute-start(bf16[128,512]{1,0:T(8,128)(2,1)S(1)} %get-tuple-element.89), channel_id=1, source_target_pairs={{0,1},{1,0},{2,3},{3,2},{4,5},{5,4},{6,7},{7,6},{8,9},{9,8},{10,11... | collective-permute-start | bytes 393224 | tf_op jit(solution)/shard_map/ppermute | solution.py:302
  116.8 4.6 %collective-permute-start.12 = (bf16[128,512]{1,0:T(8,128)(2,1)S(1)}, bf16[128,512]{1,0:T(8,128)(2,1)S(1)}, u32[]{:S(2)}, u32[]{:S(2)}) collective-permute-start(bf16[128,512]{1,0:T(8,128)(2,1)S(1)} %get-tuple-element.82), channel_id=1, source_target_pairs={{0,1},{1,0},{2,3},{3,2},{4,5},{5,4},{6,7},{7,6},{8,9},{9,8},{10,11... | collective-permute-start | bytes 393224 | tf_op jit(solution)/shard_map/ppermute | solution.py:302
  121.4 3.7 %shard_map.136 = (f32[64,256]{1,0:T(8,128)S(1)}, f32[64,256]{1,0:T(8,128)S(1)}, f32[64,256]{1,0:T(8,128)S(1)}) custom-call(s32[2,4096]{1,0:T(2,128)S(1)} %bitcast.19, s32[2,4096]{1,0:T(2,128)S(1)} %bitcast.21, s32[2,4096]{1,0:T(2,128)S(1)} %bitcast.14, s32[1,4096]{1,0:T(1,128)S(1)} %bitcast.17, f32[64,160]{1,0:T(8,128)S(1)} %get-tuple-element.94.refs_0_, ...), custom_call_target="tpu_custom_call" | custom-call | flops 500000000 | tf_op jit(solution)/shard_map/pallas_call | solution.py:42
  125.2 21.5 %collective-permute-start.14 = (bf16[128,512]{1,0:T(8,128)(2,1)S(1)}, bf16[128,512]{1,0:T(8,128)(2,1)S(1)}, u32[]{:S(2)}, u32[]{:S(2)}) collective-permute-start(bf16[128,512]{1,0:T(8,128)(2,1)S(1)} %add_convert_fusion.1), channel_id=1, source_target_pairs={{0,3},{1,2},{2,1},{3,0},{4,7},{5,6},{6,5},{7,4},{8,11},{9,10},{10,... | collective-permute-start | bytes 393224 | tf_op jit(solution)/shard_map/ppermute | solution.py:302
  147.2 12.3 %collective-permute-done.14.far = bf16[128,512]{1,0:T(8,128)(2,1)S(1)} collective-permute-done((bf16[128,512]{1,0:T(8,128)(2,1)S(1)}, bf16[128,512]{1,0:T(8,128)(2,1)S(1)}, u32[]{:S(2)}, u32[]{:S(2)}) %collective-permute-start.14) | collective-permute-done | bytes 131104 | tf_op jit(solution)/shard_map/ppermute | solution.py:302
  159.6 5.9 %shard_map.137 = bf16[64,24,128]{2,1,0:T(8,128)(2,1)S(1)} custom-call(bf16[128,512]{1,0:T(8,128)(2,1)S(1)} %get-tuple-element.81.own, bf16[128,512]{1,0:T(8,128)(2,1)S(1)} %collective-permute-done.12.near, bf16[128,512]{1,0:T(8,128)(2,1)S(1)} %collective-permute-done.14.far, f32[128,512]{1,0:T(8,128)S(1)} %get-tuple-element.102.back_one, ...), custom_call_target="tpu_custom_call" | custom-call | flops 2000000000 | bytes 10000000 | tf_op jit(solution)/shard_map/pallas_call | solution.py:42
  165.5 35.3 %all_to_all.5.got = bf16[64,24,128]{2,1,0:T(8,128)(2,1)S(1)} all-to-all(bf16[64,24,128]{2,1,0:T(8,128)(2,1)S(1)} %shard_map.137), channel_id=1, replica_groups=mesh['dp'=64,'col'=16] {'dp'}, dimensions={0} | all-to-all | bytes 786432 | tf_op jit(solution)/shard_map/all_to_all | solution.py:399
  200.8 4.5 %shard_map.138 = (f32[16,512]{1,0:T(8,128)}, f32[1,128]{1,0:T(1,128)S(1)}) custom-call(bf16[64,24,128]{2,1,0:T(8,128)(2,1)S(1)} %all_to_all.5.got), custom_call_target="tpu_custom_call" | custom-call | flops 2000000000 | bytes 10000000 | tf_op jit(solution)/shard_map/pallas_call | solution.py:42
  (43 shorter events, 5.1 us)
Async XLA Ops:
  0.6 0.7 copy-start.11
  1.3 0.7 copy-start.9
  2.0 1.2 copy-start.4
  3.2 0.9 copy-start.5
  5.7 11.8 %collective-permute-start.1 = (bf16[512,512]{1,0:T(8,128)(2,1)S(1)}, bf16[512,512]{1,0:T(8,128)(2,1)S(1)}, u32[]{:S(2)}, u32[]{:S(2)}) collective-permute-start(bf16[512,512]{1,0:T(8,128)(2,1)S(1)} %get-tuple-element.58), channel_id=1, source_target_pairs={{0,4},{1,5},{2,6},{3,7},{4,0},{5,1},{6,2},{7,3},{8,12},{9,13},{10,... | collective-permute-start | bytes 1572872 | tf_op jit(solution)/shard_map/ppermute | solution.py:302
  10.9 12.2 %collective-permute-start = (bf16[512,512]{1,0:T(8,128)(2,1)S(1)}, bf16[512,512]{1,0:T(8,128)(2,1)S(1)}, u32[]{:S(2)}, u32[]{:S(2)}) collective-permute-start(bf16[512,512]{1,0:T(8,128)(2,1)S(1)} %get-tuple-element.56), channel_id=1, source_target_pairs={{0,4},{1,5},{2,6},{3,7},{4,0},{5,1},{6,2},{7,3},{8,12},{9,13},{10,... | collective-permute-start | bytes 1572872 | tf_op jit(solution)/shard_map/ppermute | solution.py:302
  17.5 13.5 %copy-start = (bf16[128,2048]{1,0:T(8,128)(2,1)S(1)}, bf16[128,2048]{1,0:T(8,128)(2,1)}, u32[]{:S(2)}) copy-start(bf16[128,2048]{1,0:T(8,128)(2,1)} %weight.3) | copy-start | bytes 1572868
  17.6 13.3 %collective-permute-start.2 = (bf16[512,512]{1,0:T(8,128)(2,1)S(1)}, bf16[512,512]{1,0:T(8,128)(2,1)S(1)}, u32[]{:S(2)}, u32[]{:S(2)}) collective-permute-start(bf16[512,512]{1,0:T(8,128)(2,1)S(1)} %add_convert_fusion), channel_id=1, source_target_pairs={{0,12},{1,13},{2,14},{3,15},{4,8},{5,9},{6,10},{7,11},{8,4},{9,5},... | collective-permute-start | bytes 1572872 | tf_op jit(solution)/shard_map/ppermute | solution.py:302
  31.0 33.4 %copy-start.2 = (s32[4096,2]{0,1:T(2,128)S(1)}, s32[4096,2]{0,1:T(2,128)}, u32[]{:S(2)}) copy-start(s32[4096,2]{0,1:T(2,128)} %param.22) | copy-start | bytes 98308
  31.0 33.4 %copy-start.7 = (s32[4096,2]{0,1:T(2,128)S(1)}, s32[4096,2]{0,1:T(2,128)}, u32[]{:S(2)}) copy-start(s32[4096,2]{0,1:T(2,128)} %param.20) | copy-start | bytes 98308
  31.0 33.4 %copy-start.8 = (s32[4096,2]{0,1:T(2,128)S(1)}, s32[4096,2]{0,1:T(2,128)}, u32[]{:S(2)}) copy-start(s32[4096,2]{0,1:T(2,128)} %param.21) | copy-start | bytes 98308
  32.0 32.5 %copy-start.3 = (s32[4096]{0:T(1024)S(1)}, s32[4096]{0:T(1024)}, u32[]{:S(2)}) copy-start(s32[4096]{0:T(1024)} %param.23) | copy-start | bytes 49156
  32.0 36.0 %collective-permute-start.3 = (bf16[128,512]{1,0:T(8,128)(2,1)S(1)}, bf16[128,512]{1,0:T(8,128)(2,1)S(1)}, u32[]{:S(2)}, u32[]{:S(2)}) collective-permute-start(bf16[128,512]{1,0:T(8,128)(2,1)S(1)} %get-tuple-element.61), channel_id=1, source_target_pairs={{0,1},{1,0},{2,3},{3,2},{4,5},{5,4},{6,7},{7,6},{8,9},{9,8},{10,11... | collective-permute-start | bytes 393224 | tf_op jit(solution)/shard_map/ppermute | solution.py:302
  52.9 15.2 %collective-permute-start.4 = (bf16[128,512]{1,0:T(8,128)(2,1)S(1)}, bf16[128,512]{1,0:T(8,128)(2,1)S(1)}, u32[]{:S(2)}, u32[]{:S(2)}) collective-permute-start(bf16[128,512]{1,0:T(8,128)(2,1)S(1)} %get-tuple-element.70), channel_id=1, source_target_pairs={{0,4},{1,5},{2,6},{3,7},{4,0},{5,1},{6,2},{7,3},{8,12},{9,13},{10,... | collective-permute-start | bytes 393224 | tf_op jit(solution)/shard_map/ppermute | solution.py:302
  57.3 10.8 %collective-permute-start.5 = (bf16[128,512]{1,0:T(8,128)(2,1)S(1)}, bf16[128,512]{1,0:T(8,128)(2,1)S(1)}, u32[]{:S(2)}, u32[]{:S(2)}) collective-permute-start(bf16[128,512]{1,0:T(8,128)(2,1)S(1)} %get-tuple-element.71), channel_id=1, source_target_pairs={{0,12},{1,13},{2,14},{3,15},{4,8},{5,9},{6,10},{7,11},{8,4},{9,5},... | collective-permute-start | bytes 393224 | tf_op jit(solution)/shard_map/ppermute | solution.py:302
  59.2 8.9 %collective-permute-start.6 = (bf16[128,512]{1,0:T(8,128)(2,1)S(1)}, bf16[128,512]{1,0:T(8,128)(2,1)S(1)}, u32[]{:S(2)}, u32[]{:S(2)}) collective-permute-start(bf16[128,512]{1,0:T(8,128)(2,1)S(1)} %get-tuple-element.72), channel_id=1, source_target_pairs={{0,8},{1,9},{2,10},{3,11},{4,12},{5,13},{6,14},{7,15},{8,0},{9,1},... | collective-permute-start | bytes 393224 | tf_op jit(solution)/shard_map/ppermute | solution.py:302
  62.5 14.8 %collective-permute-start.7 = (bf16[128,512]{1,0:T(8,128)(2,1)S(1)}, bf16[128,512]{1,0:T(8,128)(2,1)S(1)}, u32[]{:S(2)}, u32[]{:S(2)}) collective-permute-start(bf16[128,512]{1,0:T(8,128)(2,1)S(1)} %get-tuple-element.77), channel_id=1, source_target_pairs={{0,1},{1,0},{2,3},{3,2},{4,5},{5,4},{6,7},{7,6},{8,9},{9,8},{10,11... | collective-permute-start | bytes 393224 | tf_op jit(solution)/shard_map/ppermute | solution.py:302
  68.1 25.3 %copy-start.1 = (bf16[512,128]{1,0:T(8,128)(2,1)S(1)}, bf16[512,128]{1,0:T(8,128)(2,1)}, u32[]{:S(2)}) copy-start(bf16[512,128]{1,0:T(8,128)(2,1)} %embedded.1) | copy-start | bytes 393220
  68.1 25.2 %collective-permute-start.8 = (bf16[128,512]{1,0:T(8,128)(2,1)S(1)}, bf16[128,512]{1,0:T(8,128)(2,1)S(1)}, u32[]{:S(2)}, u32[]{:S(2)}) collective-permute-start(bf16[128,512]{1,0:T(8,128)(2,1)S(1)} %add_convert_fusion.2), channel_id=1, source_target_pairs={{0,3},{1,2},{2,1},{3,0},{4,7},{5,6},{6,5},{7,4},{8,11},{9,10},{10,... | collective-permute-start | bytes 393224 | tf_op jit(solution)/shard_map/ppermute | solution.py:302
  93.5 6.9 %collective-permute-start.9 = (bf16[128,512]{1,0:T(8,128)(2,1)S(1)}, bf16[128,512]{1,0:T(8,128)(2,1)S(1)}, u32[]{:S(2)}, u32[]{:S(2)}) collective-permute-start(bf16[128,512]{1,0:T(8,128)(2,1)S(1)} %get-tuple-element.80.g_own), channel_id=1, source_target_pairs={{0,4},{1,5},{2,6},{3,7},{4,0},{5,1},{6,2},{7,3},{8,12},{9,13},{10,... | collective-permute-start | bytes 393224 | tf_op jit(solution)/shard_map/ppermute | solution.py:302
  96.4 5.9 %collective-permute-start.10 = (bf16[128,512]{1,0:T(8,128)(2,1)S(1)}, bf16[128,512]{1,0:T(8,128)(2,1)S(1)}, u32[]{:S(2)}, u32[]{:S(2)}) collective-permute-start(bf16[128,512]{1,0:T(8,128)(2,1)S(1)} %get-tuple-element.80.g_own), channel_id=1, source_target_pairs={{0,12},{1,13},{2,14},{3,15},{4,8},{5,9},{6,10},{7,11},{8,4},{9,5},... | collective-permute-start | bytes 393224 | tf_op jit(solution)/shard_map/ppermute | solution.py:302
  100.4 5.7 %collective-permute-start.11 = (bf16[128,512]{1,0:T(8,128)(2,1)S(1)}, bf16[128,512]{1,0:T(8,128)(2,1)S(1)}, u32[]{:S(2)}, u32[]{:S(2)}) collective-permute-start(bf16[128,512]{1,0:T(8,128)(2,1)S(1)} %collective-permute-done.9.g_near), channel_id=1, source_target_pairs={{0,12},{1,13},{2,14},{3,15},{4,8},{5,9},{6,10},{7,11},{8,4},{9,5},... | collective-permute-start | bytes 393224 | tf_op jit(solution)/shard_map/ppermute | solution.py:302
  107.4 17.7 %collective-permute-start.13 = (bf16[128,512]{1,0:T(8,128)(2,1)S(1)}, bf16[128,512]{1,0:T(8,128)(2,1)S(1)}, u32[]{:S(2)}, u32[]{:S(2)}) collective-permute-start(bf16[128,512]{1,0:T(8,128)(2,1)S(1)} %get-tuple-element.89), channel_id=1, source_target_pairs={{0,1},{1,0},{2,3},{3,2},{4,5},{5,4},{6,7},{7,6},{8,9},{9,8},{10,11... | collective-permute-start | bytes 393224 | tf_op jit(solution)/shard_map/ppermute | solution.py:302
  116.8 30.5 %collective-permute-start.12 = (bf16[128,512]{1,0:T(8,128)(2,1)S(1)}, bf16[128,512]{1,0:T(8,128)(2,1)S(1)}, u32[]{:S(2)}, u32[]{:S(2)}) collective-permute-start(bf16[128,512]{1,0:T(8,128)(2,1)S(1)} %get-tuple-element.82), channel_id=1, source_target_pairs={{0,1},{1,0},{2,3},{3,2},{4,5},{5,4},{6,7},{7,6},{8,9},{9,8},{10,11... | collective-permute-start | bytes 393224 | tf_op jit(solution)/shard_map/ppermute | solution.py:302
  125.1 21.6 %copy-start.10 = (s32[4096,2]{0,1:T(2,128)S(1)}, s32[4096,2]{0,1:T(2,128)}, u32[]{:S(2)}) copy-start(s32[4096,2]{0,1:T(2,128)} %param.19) | copy-start | bytes 98308
  125.2 34.4 %collective-permute-start.14 = (bf16[128,512]{1,0:T(8,128)(2,1)S(1)}, bf16[128,512]{1,0:T(8,128)(2,1)S(1)}, u32[]{:S(2)}, u32[]{:S(2)}) collective-permute-start(bf16[128,512]{1,0:T(8,128)(2,1)S(1)} %add_convert_fusion.1), channel_id=1, source_target_pairs={{0,3},{1,2},{2,1},{3,0},{4,7},{5,6},{6,5},{7,4},{8,11},{9,10},{10,... | collective-permute-start | bytes 393224 | tf_op jit(solution)/shard_map/ppermute | solution.py:302
  147.1 12.5 %copy-start.6 = (bf16[512,128]{1,0:T(8,128)(2,1)S(1)}, bf16[512,128]{1,0:T(8,128)(2,1)}, u32[]{:S(2)}) copy-start(bf16[512,128]{1,0:T(8,128)(2,1)} %gate.1) | copy-start | bytes 393220

commit v5 on v4

--- a/solution.py
+++ b/solution.py
@@ -111,7 +111,7 @@
     gated[...] = (total * embedded[...].astype(F32).T).astype(BF16)
 
 
-def cross_kernel(place, w_own, w_near, w_far, w_diag, g_own, g_near, g_far, g_diag, *refs):
+def cross_kernel(place, w_own, w_diag, w_near, w_far, g_own, g_diag, g_near, g_far, *refs):
     total = refs[4]
     product = mxu(w_own[...], g_own[...], TN)
     for weight, gated in ((w_near, g_near), (w_far, g_far), (w_diag, g_diag)):
@@ -216,7 +216,7 @@
         out[o] = jnp.concatenate([value[:, :MAIN], last], axis=0).astype(BF16)
         return carry
 
-    lax.fori_loop(0, owners, step, 0, unroll=4)
+    lax.fori_loop(0, owners, step, 0, unroll=8)
 
 
 def gather_kernel(got, cold, hot):
@@ -251,7 +251,7 @@
         owners,
         step,
         (jnp.zeros((MAIN, parts * wide), F32), jnp.zeros((8, MAIN), F32)),
-        unroll=4,
+        unroll=8,
     )
     total = total.T
     for p in range(parts):
@@ -310,12 +310,21 @@
             held, diagonal = lax.optimization_barrier((held, diagonal))
         first = shift(diagonal, along_outer, 0)
         near = shift(near, along_outer, 0)
-        parts = tuple(shift(part, True, turn) for part, turn in zip(parts, (0, 1, None)))
         done = ()
         if work is not None:
             done = tuple(work(held))
-            first, done, parts = lax.optimization_barrier((first, done, parts))
-        return (own, near, shift(onward(second, first), along_outer, 1)), done, parts
+            first, done = lax.optimization_barrier((first, done))
+        far = onward(second, first)
+        if not parts:
+            return (own, near, shift(far, along_outer, 1)), done, parts
+        far, parts = lax.optimization_barrier((far, parts))
+        far = shift(far, along_outer, 1)
+        w_near, w_far, w_diag = parts
+        w_diag = shift(w_diag, True, None)
+        near, w_near, w_far = lax.optimization_barrier((near, w_near, w_far))
+        parts = w_diag, shift(w_near, True, 0), shift(w_far, True, 1)
+        far, parts = lax.optimization_barrier((far, parts))
+        return (own, near, far), done, parts
 
     state = [jax.ShapeDtypeStruct((owners, CAP), F32)] * 3
     state += [jax.ShapeDtypeStruct((owners, MAIN), F32)]
@@ -373,13 +382,13 @@
         flops=4 * cols * samples,
         moved=16 * cols * samples,
     )
+    diagonal = shift(gated, True, None)
     near = shift(gated, True, 0)
     far = shift(gated, True, 1)
-    diagonal = shift(near, True, 1)
     blocks = call(
         cross_kernel,
         blocks_of(cols, samples),
-        weights + (gated, near, far, diagonal),
+        weights + (gated, diagonal, near, far),
         smem=(inner_place,),
         scratch=[pltpu.VMEM((outer_rows, samples), BF16)],
         flops=2 * total_cols * samples * cols,

time: 210 us -> 216 us (1.029); the launches traced: 207 us -> 215 us
  blocking collectives: 35.3 us -> 56.3 us
  waiting for transfers between devices: 50.9 us -> 42.9 us
  Pallas kernels: 21.6 us -> 18.9 us
    all_to_all x1, blocking collectives: 35.3 us -> 56.3 us  [local(): got = lax.all_to_all(message, 'dp', split_axis=0, concat_axis=0, tiled=True)]
    ppermute x15, waiting for transfers between devices: 50.9 us -> 42.9 us  [shift(): return lax.ppermute(x, ('dp', 'col'), pairs)]
    pallas_call x8, Pallas kernels: 21.6 us -> 18.9 us  [call(): pl.pallas_call(kernel, out_shape=out_shape, in_specs=[scalar] * len(smem)...]
  transfers between devices with their start and end apart: 15 -> 15, of which waited for: 8 -> 11; matrix products, arithmetic and copies ran while one was open for 0% -> 0% of each run, Pallas kernels for 4% -> 3%
where the time goes in v5:
time: 216 us; the launch traced here: 215 us
  starting transfers between devices  90.1 us (42%)
  blocking collectives  56.3 us (26%)
  waiting for transfers between devices  42.9 us (20%)
  Pallas kernels  18.9 us (9%)
  local copies, waits for them, and re-layouts  5.12 us (2%)
    ppermute x15, starting transfers between devices, shift(): return lax.ppermute(x, ('dp', 'col'), pairs)  90.1 us
    all_to_all x1, blocking collectives, local(): got = lax.all_to_all(message, 'dp', split_axis=0, concat_axis=0, tiled=True)  56.3 us
    ppermute x15, waiting for transfers between devices, shift(): return lax.ppermute(x, ('dp', 'col'), pairs)  42.9 us
    pallas_call x8, Pallas kernels, call(): pl.pallas_call(kernel, out_shape=out_shape, in_specs=[scalar] * len(smem)...  18.9 us
  transfers between devices with their start and end apart: 15, of which 11 were waited for; matrix products, arithmetic and copies ran while one was open for 0% of the time, Pallas kernels for 3%

profile of v5, /device:TPU:1, one launch (start us, length us, event | category | flops | bytes accessed | tf_op | source)
XLA Modules:
  0.0 215.4 jit_solution(9424485091436506244)
XLA Ops:
  2.0 1.2 copy-done.4
  4.2 1.5 shard_map.131
  5.7 5.2 %collective-permute-start.1 = (bf16[512,512]{1,0:T(8,128)(2,1)S(1)}, bf16[512,512]{1,0:T(8,128)(2,1)S(1)}, u32[]{:S(2)}, u32[]{:S(2)}) collective-permute-start(bf16[512,512]{1,0:T(8,128)(2,1)S(1)} %get-tuple-element.66), channel_id=1, source_target_pairs={{0,4},{1,5},{2,6},{3,7},{4,0},{5,1},{6,2},{7,3},{8,12},{9,13},{10,... | collective-permute-start | bytes 1572872 | tf_op jit(solution)/shard_map/ppermute | solution.py:302
  10.9 1.9 collective-permute-start
  12.9 4.6 %collective-permute-done.1 = bf16[512,512]{1,0:T(8,128)(2,1)S(1)} collective-permute-done((bf16[512,512]{1,0:T(8,128)(2,1)S(1)}, bf16[512,512]{1,0:T(8,128)(2,1)S(1)}, u32[]{:S(2)}, u32[]{:S(2)}) %collective-permute-start.1) | collective-permute-done | bytes 524320 | tf_op jit(solution)/shard_map/ppermute | solution.py:302
  17.6 2.2 %collective-permute-start.2 = (bf16[512,512]{1,0:T(8,128)(2,1)S(1)}, bf16[512,512]{1,0:T(8,128)(2,1)S(1)}, u32[]{:S(2)}, u32[]{:S(2)}) collective-permute-start(bf16[512,512]{1,0:T(8,128)(2,1)S(1)} %add_convert_fusion), channel_id=1, source_target_pairs={{0,12},{1,13},{2,14},{3,15},{4,8},{5,9},{6,10},{7,11},{8,4},{9,5},... | collective-permute-start | bytes 1572872 | tf_op jit(solution)/shard_map/ppermute | solution.py:302
  20.0 3.2 %collective-permute-done.near = bf16[512,512]{1,0:T(8,128)(2,1)S(1)} collective-permute-done((bf16[512,512]{1,0:T(8,128)(2,1)S(1)}, bf16[512,512]{1,0:T(8,128)(2,1)S(1)}, u32[]{:S(2)}, u32[]{:S(2)}) %collective-permute-start) | collective-permute-done | bytes 524320 | tf_op jit(solution)/shard_map/ppermute | solution.py:302
  23.1 7.9 %collective-permute-done.2.far = bf16[512,512]{1,0:T(8,128)(2,1)S(1)} collective-permute-done((bf16[512,512]{1,0:T(8,128)(2,1)S(1)}, bf16[512,512]{1,0:T(8,128)(2,1)S(1)}, u32[]{:S(2)}, u32[]{:S(2)}) %collective-permute-start.2) | collective-permute-done | bytes 524320 | tf_op jit(solution)/shard_map/ppermute | solution.py:302
  32.0 20.9 %collective-permute-start.3 = (bf16[128,512]{1,0:T(8,128)(2,1)S(1)}, bf16[128,512]{1,0:T(8,128)(2,1)S(1)}, u32[]{:S(2)}, u32[]{:S(2)}) collective-permute-start(bf16[128,512]{1,0:T(8,128)(2,1)S(1)} %get-tuple-element.70), channel_id=1, source_target_pairs={{0,1},{1,0},{2,3},{3,2},{4,5},{5,4},{6,7},{7,6},{8,9},{9,8},{10,11... | collective-permute-start | bytes 393224 | tf_op jit(solution)/shard_map/ppermute | solution.py:302
  52.9 1.9 collective-permute-start.6
  54.8 3.6 %shard_map.133 = (f32[64,160]{1,0:T(8,128)S(1)}, f32[64,160]{1,0:T(8,128)S(1)}, f32[64,160]{1,0:T(8,128)S(1)}, f32[64,128]{1,0:T(8,128)S(1)}) custom-call(s32[2,4096]{1,0:T(2,128)S(1)} %bitcast.18, s32[2,4096]{1,0:T(2,128)S(1)} %bitcast.20, s32[2,4096]{1,0:T(2,128)S(1)} %bitcast.13, s32[1,4096]{1,0:T(1,128)S(1)} %bitcast.16), custom_call_target="tpu_custom_call" | custom-call | flops 500000000 | tf_op jit(solution)/shard_map/pallas_call | solution.py:42
  58.4 3.4 %collective-permute-done.3 = bf16[128,512]{1,0:T(8,128)(2,1)S(1)} collective-permute-done((bf16[128,512]{1,0:T(8,128)(2,1)S(1)}, bf16[128,512]{1,0:T(8,128)(2,1)S(1)}, u32[]{:S(2)}, u32[]{:S(2)}) %collective-permute-start.3) | collective-permute-done | bytes 131104 | tf_op jit(solution)/shard_map/ppermute | solution.py:302
  61.9 11.6 %collective-permute-start.4 = (bf16[128,512]{1,0:T(8,128)(2,1)S(1)}, bf16[128,512]{1,0:T(8,128)(2,1)S(1)}, u32[]{:S(2)}, u32[]{:S(2)}) collective-permute-start(bf16[128,512]{1,0:T(8,128)(2,1)S(1)} %add_convert_fusion.2), channel_id=1, source_target_pairs={{0,3},{1,2},{2,1},{3,0},{4,7},{5,6},{6,5},{7,4},{8,11},{9,10},{10,... | collective-permute-start | bytes 393224 | tf_op jit(solution)/shard_map/ppermute | solution.py:302
  73.4 12.0 %collective-permute-start.5 = (bf16[128,512]{1,0:T(8,128)(2,1)S(1)}, bf16[128,512]{1,0:T(8,128)(2,1)S(1)}, u32[]{:S(2)}, u32[]{:S(2)}) collective-permute-start(bf16[128,512]{1,0:T(8,128)(2,1)S(1)} %get-tuple-element.84), channel_id=1, source_target_pairs={{0,8},{1,9},{2,10},{3,11},{4,12},{5,13},{6,14},{7,15},{8,0},{9,1},... | collective-permute-start | bytes 393224 | tf_op jit(solution)/shard_map/ppermute | solution.py:302
  85.5 2.7 %collective-permute-start.7 = (bf16[128,512]{1,0:T(8,128)(2,1)S(1)}, bf16[128,512]{1,0:T(8,128)(2,1)S(1)}, u32[]{:S(2)}, u32[]{:S(2)}) collective-permute-start(bf16[128,512]{1,0:T(8,128)(2,1)S(1)} %get-tuple-element.88), channel_id=1, source_target_pairs={{0,4},{1,5},{2,6},{3,7},{4,0},{5,1},{6,2},{7,3},{8,12},{9,13},{10,... | collective-permute-start | bytes 393224 | tf_op jit(solution)/shard_map/ppermute | solution.py:302
  88.2 1.9 collective-permute-start.8
  90.1 3.2 %collective-permute-done.7.w_near = bf16[128,512]{1,0:T(8,128)(2,1)S(1)} collective-permute-done((bf16[128,512]{1,0:T(8,128)(2,1)S(1)}, bf16[128,512]{1,0:T(8,128)(2,1)S(1)}, u32[]{:S(2)}, u32[]{:S(2)}) %collective-permute-start.7) | collective-permute-done | bytes 131104 | tf_op jit(solution)/shard_map/ppermute | solution.py:302
  94.0 4.8 %collective-permute-start.9 = (bf16[128,512]{1,0:T(8,128)(2,1)S(1)}, bf16[128,512]{1,0:T(8,128)(2,1)S(1)}, u32[]{:S(2)}, u32[]{:S(2)}) collective-permute-start(bf16[128,512]{1,0:T(8,128)(2,1)S(1)} %get-tuple-element.96.g_own), channel_id=1, source_target_pairs={{0,8},{1,9},{2,10},{3,11},{4,12},{5,13},{6,14},{7,15},{8,0},{9,1},... | collective-permute-start | bytes 393224 | tf_op jit(solution)/shard_map/ppermute | solution.py:302
  98.8 3.1 %collective-permute-start.10 = (bf16[128,512]{1,0:T(8,128)(2,1)S(1)}, bf16[128,512]{1,0:T(8,128)(2,1)S(1)}, u32[]{:S(2)}, u32[]{:S(2)}) collective-permute-start(bf16[128,512]{1,0:T(8,128)(2,1)S(1)} %get-tuple-element.96.g_own), channel_id=1, source_target_pairs={{0,4},{1,5},{2,6},{3,7},{4,0},{5,1},{6,2},{7,3},{8,12},{9,13},{10,... | collective-permute-start | bytes 393224 | tf_op jit(solution)/shard_map/ppermute | solution.py:302
  102.0 1.9 collective-permute-start.11
  103.9 1.8 collective-permute-done.10.g_near
  105.7 2.2 %collective-permute-done.11.g_far = bf16[128,512]{1,0:T(8,128)(2,1)S(1)} collective-permute-done((bf16[128,512]{1,0:T(8,128)(2,1)S(1)}, bf16[128,512]{1,0:T(8,128)(2,1)S(1)}, u32[]{:S(2)}, u32[]{:S(2)}) %collective-permute-start.11) | collective-permute-done | bytes 131104 | tf_op jit(solution)/shard_map/ppermute | solution.py:302
  107.9 1.3 shard_map.135
  109.2 10.9 %collective-permute-start.13 = (bf16[128,512]{1,0:T(8,128)(2,1)S(1)}, bf16[128,512]{1,0:T(8,128)(2,1)S(1)}, u32[]{:S(2)}, u32[]{:S(2)}) collective-permute-start(bf16[128,512]{1,0:T(8,128)(2,1)S(1)} %get-tuple-element.105), channel_id=1, source_target_pairs={{0,1},{1,0},{2,3},{3,2},{4,5},{5,4},{6,7},{7,6},{8,9},{9,8},{10,11... | collective-permute-start | bytes 393224 | tf_op jit(solution)/shard_map/ppermute | solution.py:302
  120.1 3.1 %collective-permute-start.12 = (bf16[128,512]{1,0:T(8,128)(2,1)S(1)}, bf16[128,512]{1,0:T(8,128)(2,1)S(1)}, u32[]{:S(2)}, u32[]{:S(2)}) collective-permute-start(bf16[128,512]{1,0:T(8,128)(2,1)S(1)} %get-tuple-element.98), channel_id=1, source_target_pairs={{0,1},{1,0},{2,3},{3,2},{4,5},{5,4},{6,7},{7,6},{8,9},{9,8},{10,11... | collective-permute-start | bytes 393224 | tf_op jit(solution)/shard_map/ppermute | solution.py:302
  123.2 3.7 %shard_map.136 = (f32[64,256]{1,0:T(8,128)S(1)}, f32[64,256]{1,0:T(8,128)S(1)}, f32[64,256]{1,0:T(8,128)S(1)}) custom-call(s32[2,4096]{1,0:T(2,128)S(1)} %bitcast.19, s32[2,4096]{1,0:T(2,128)S(1)} %bitcast.21, s32[2,4096]{1,0:T(2,128)S(1)} %bitcast.14, s32[1,4096]{1,0:T(1,128)S(1)} %bitcast.17, f32[64,160]{1,0:T(8,128)S(1)} %get-tuple-element.110.refs_0_, ...), custom_call_target="tpu_custom_call" | custom-call | flops 500000000 | tf_op jit(solution)/shard_map/pallas_call | solution.py:42
  126.9 5.7 %collective-permute-done.13 = bf16[128,512]{1,0:T(8,128)(2,1)S(1)} collective-permute-done((bf16[128,512]{1,0:T(8,128)(2,1)S(1)}, bf16[128,512]{1,0:T(8,128)(2,1)S(1)}, u32[]{:S(2)}, u32[]{:S(2)}) %collective-permute-start.13) | collective-permute-done | bytes 131104 | tf_op jit(solution)/shard_map/ppermute | solution.py:302
  132.7 5.9 %collective-permute-start.14 = (bf16[128,512]{1,0:T(8,128)(2,1)S(1)}, bf16[128,512]{1,0:T(8,128)(2,1)S(1)}, u32[]{:S(2)}, u32[]{:S(2)}) collective-permute-start(bf16[128,512]{1,0:T(8,128)(2,1)S(1)} %add_convert_fusion.1), channel_id=1, source_target_pairs={{0,3},{1,2},{2,1},{3,0},{4,7},{5,6},{6,5},{7,4},{8,11},{9,10},{10,... | collective-permute-start | bytes 393224 | tf_op jit(solution)/shard_map/ppermute | solution.py:302
  139.5 10.0 %collective-permute-done.14.far = bf16[128,512]{1,0:T(8,128)(2,1)S(1)} collective-permute-done((bf16[128,512]{1,0:T(8,128)(2,1)S(1)}, bf16[128,512]{1,0:T(8,128)(2,1)S(1)}, u32[]{:S(2)}, u32[]{:S(2)}) %collective-permute-start.14) | collective-permute-done | bytes 131104 | tf_op jit(solution)/shard_map/ppermute | solution.py:302
  149.5 4.6 %shard_map.137 = bf16[64,24,128]{2,1,0:T(8,128)(2,1)S(1)} custom-call(bf16[128,512]{1,0:T(8,128)(2,1)S(1)} %get-tuple-element.97.own, bf16[128,512]{1,0:T(8,128)(2,1)S(1)} %collective-permute-done.12.near, bf16[128,512]{1,0:T(8,128)(2,1)S(1)} %collective-permute-done.14.far, f32[128,512]{1,0:T(8,128)S(1)} %get-tuple-element.118.back_one, ...), custom_call_target="tpu_custom_call" | custom-call | flops 2000000000 | bytes 10000000 | tf_op jit(solution)/shard_map/pallas_call | solution.py:42
  154.1 56.3 %all_to_all.5.got = bf16[64,24,128]{2,1,0:T(8,128)(2,1)S(1)} all-to-all(bf16[64,24,128]{2,1,0:T(8,128)(2,1)S(1)} %shard_map.137), channel_id=1, replica_groups=mesh['dp'=64,'col'=16] {'dp'}, dimensions={0} | all-to-all | bytes 786432 | tf_op jit(solution)/shard_map/all_to_all | solution.py:408
  210.4 3.2 %shard_map.138 = (f32[16,512]{1,0:T(8,128)}, f32[1,128]{1,0:T(1,128)S(1)}) custom-call(bf16[64,24,128]{2,1,0:T(8,128)(2,1)S(1)} %all_to_all.5.got), custom_call_target="tpu_custom_call" | custom-call | flops 2000000000 | bytes 10000000 | tf_op jit(solution)/shard_map/pallas_call | solution.py:42
  (43 shorter events, 6.9 us)
Async XLA Ops:
  0.6 0.7 copy-start.11
  1.3 0.7 copy-start.9
  2.0 1.2 copy-start.4
  3.2 0.9 copy-start.5
  5.7 11.8 %collective-permute-start.1 = (bf16[512,512]{1,0:T(8,128)(2,1)S(1)}, bf16[512,512]{1,0:T(8,128)(2,1)S(1)}, u32[]{:S(2)}, u32[]{:S(2)}) collective-permute-start(bf16[512,512]{1,0:T(8,128)(2,1)S(1)} %get-tuple-element.66), channel_id=1, source_target_pairs={{0,4},{1,5},{2,6},{3,7},{4,0},{5,1},{6,2},{7,3},{8,12},{9,13},{10,... | collective-permute-start | bytes 1572872 | tf_op jit(solution)/shard_map/ppermute | solution.py:302
  10.9 12.2 %collective-permute-start = (bf16[512,512]{1,0:T(8,128)(2,1)S(1)}, bf16[512,512]{1,0:T(8,128)(2,1)S(1)}, u32[]{:S(2)}, u32[]{:S(2)}) collective-permute-start(bf16[512,512]{1,0:T(8,128)(2,1)S(1)} %get-tuple-element.64), channel_id=1, source_target_pairs={{0,4},{1,5},{2,6},{3,7},{4,0},{5,1},{6,2},{7,3},{8,12},{9,13},{10,... | collective-permute-start | bytes 1572872 | tf_op jit(solution)/shard_map/ppermute | solution.py:302
  17.5 13.5 %copy-start = (bf16[128,2048]{1,0:T(8,128)(2,1)S(1)}, bf16[128,2048]{1,0:T(8,128)(2,1)}, u32[]{:S(2)}) copy-start(bf16[128,2048]{1,0:T(8,128)(2,1)} %weight.3) | copy-start | bytes 1572868
  17.6 13.3 %collective-permute-start.2 = (bf16[512,512]{1,0:T(8,128)(2,1)S(1)}, bf16[512,512]{1,0:T(8,128)(2,1)S(1)}, u32[]{:S(2)}, u32[]{:S(2)}) collective-permute-start(bf16[512,512]{1,0:T(8,128)(2,1)S(1)} %add_convert_fusion), channel_id=1, source_target_pairs={{0,12},{1,13},{2,14},{3,15},{4,8},{5,9},{6,10},{7,11},{8,4},{9,5},... | collective-permute-start | bytes 1572872 | tf_op jit(solution)/shard_map/ppermute | solution.py:302
  31.0 23.8 %copy-start.2 = (s32[4096,2]{0,1:T(2,128)S(1)}, s32[4096,2]{0,1:T(2,128)}, u32[]{:S(2)}) copy-start(s32[4096,2]{0,1:T(2,128)} %param.22) | copy-start | bytes 98308
  31.0 23.8 %copy-start.3 = (s32[4096]{0:T(1024)S(1)}, s32[4096]{0:T(1024)}, u32[]{:S(2)}) copy-start(s32[4096]{0:T(1024)} %param.23) | copy-start | bytes 49156
  31.0 23.8 %copy-start.7 = (s32[4096,2]{0,1:T(2,128)S(1)}, s32[4096,2]{0,1:T(2,128)}, u32[]{:S(2)}) copy-start(s32[4096,2]{0,1:T(2,128)} %param.20) | copy-start | bytes 98308
  31.0 23.8 %copy-start.8 = (s32[4096,2]{0,1:T(2,128)S(1)}, s32[4096,2]{0,1:T(2,128)}, u32[]{:S(2)}) copy-start(s32[4096,2]{0,1:T(2,128)} %param.21) | copy-start | bytes 98308
  32.0 29.8 %collective-permute-start.3 = (bf16[128,512]{1,0:T(8,128)(2,1)S(1)}, bf16[128,512]{1,0:T(8,128)(2,1)S(1)}, u32[]{:S(2)}, u32[]{:S(2)}) collective-permute-start(bf16[128,512]{1,0:T(8,128)(2,1)S(1)} %get-tuple-element.70), channel_id=1, source_target_pairs={{0,1},{1,0},{2,3},{3,2},{4,5},{5,4},{6,7},{7,6},{8,9},{9,8},{10,11... | collective-permute-start | bytes 393224 | tf_op jit(solution)/shard_map/ppermute | solution.py:302
  52.9 32.6 %collective-permute-start.6 = (bf16[128,512]{1,0:T(8,128)(2,1)S(1)}, bf16[128,512]{1,0:T(8,128)(2,1)S(1)}, u32[]{:S(2)}, u32[]{:S(2)}) collective-permute-start(bf16[128,512]{1,0:T(8,128)(2,1)S(1)} %get-tuple-element.85), channel_id=1, source_target_pairs={{0,1},{1,0},{2,3},{3,2},{4,5},{5,4},{6,7},{7,6},{8,9},{9,8},{10,11... | collective-permute-start | bytes 393224 | tf_op jit(solution)/shard_map/ppermute | solution.py:302
  61.8 32.1 %copy-start.1 = (bf16[512,128]{1,0:T(8,128)(2,1)S(1)}, bf16[512,128]{1,0:T(8,128)(2,1)}, u32[]{:S(2)}) copy-start(bf16[512,128]{1,0:T(8,128)(2,1)} %embedded.1) | copy-start | bytes 393220
  61.9 28.3 %collective-permute-start.4 = (bf16[128,512]{1,0:T(8,128)(2,1)S(1)}, bf16[128,512]{1,0:T(8,128)(2,1)S(1)}, u32[]{:S(2)}, u32[]{:S(2)}) collective-permute-start(bf16[128,512]{1,0:T(8,128)(2,1)S(1)} %add_convert_fusion.2), channel_id=1, source_target_pairs={{0,3},{1,2},{2,1},{3,0},{4,7},{5,6},{6,5},{7,4},{8,11},{9,10},{10,... | collective-permute-start | bytes 393224 | tf_op jit(solution)/shard_map/ppermute | solution.py:302
  73.4 16.7 %collective-permute-start.5 = (bf16[128,512]{1,0:T(8,128)(2,1)S(1)}, bf16[128,512]{1,0:T(8,128)(2,1)S(1)}, u32[]{:S(2)}, u32[]{:S(2)}) collective-permute-start(bf16[128,512]{1,0:T(8,128)(2,1)S(1)} %get-tuple-element.84), channel_id=1, source_target_pairs={{0,8},{1,9},{2,10},{3,11},{4,12},{5,13},{6,14},{7,15},{8,0},{9,1},... | collective-permute-start | bytes 393224 | tf_op jit(solution)/shard_map/ppermute | solution.py:302
  85.5 7.9 %collective-permute-start.7 = (bf16[128,512]{1,0:T(8,128)(2,1)S(1)}, bf16[128,512]{1,0:T(8,128)(2,1)S(1)}, u32[]{:S(2)}, u32[]{:S(2)}) collective-permute-start(bf16[128,512]{1,0:T(8,128)(2,1)S(1)} %get-tuple-element.88), channel_id=1, source_target_pairs={{0,4},{1,5},{2,6},{3,7},{4,0},{5,1},{6,2},{7,3},{8,12},{9,13},{10,... | collective-permute-start | bytes 393224 | tf_op jit(solution)/shard_map/ppermute | solution.py:302
  88.2 5.7 %collective-permute-start.8 = (bf16[128,512]{1,0:T(8,128)(2,1)S(1)}, bf16[128,512]{1,0:T(8,128)(2,1)S(1)}, u32[]{:S(2)}, u32[]{:S(2)}) collective-permute-start(bf16[128,512]{1,0:T(8,128)(2,1)S(1)} %get-tuple-element.89), channel_id=1, source_target_pairs={{0,12},{1,13},{2,14},{3,15},{4,8},{5,9},{6,10},{7,11},{8,4},{9,5},... | collective-permute-start | bytes 393224 | tf_op jit(solution)/shard_map/ppermute | solution.py:302
  94.0 9.9 %collective-permute-start.9 = (bf16[128,512]{1,0:T(8,128)(2,1)S(1)}, bf16[128,512]{1,0:T(8,128)(2,1)S(1)}, u32[]{:S(2)}, u32[]{:S(2)}) collective-permute-start(bf16[128,512]{1,0:T(8,128)(2,1)S(1)} %get-tuple-element.96.g_own), channel_id=1, source_target_pairs={{0,8},{1,9},{2,10},{3,11},{4,12},{5,13},{6,14},{7,15},{8,0},{9,1},... | collective-permute-start | bytes 393224 | tf_op jit(solution)/shard_map/ppermute | solution.py:302
  98.8 6.9 %collective-permute-start.10 = (bf16[128,512]{1,0:T(8,128)(2,1)S(1)}, bf16[128,512]{1,0:T(8,128)(2,1)S(1)}, u32[]{:S(2)}, u32[]{:S(2)}) collective-permute-start(bf16[128,512]{1,0:T(8,128)(2,1)S(1)} %get-tuple-element.96.g_own), channel_id=1, source_target_pairs={{0,4},{1,5},{2,6},{3,7},{4,0},{5,1},{6,2},{7,3},{8,12},{9,13},{10,... | collective-permute-start | bytes 393224 | tf_op jit(solution)/shard_map/ppermute | solution.py:302
  102.0 6.0 %collective-permute-start.11 = (bf16[128,512]{1,0:T(8,128)(2,1)S(1)}, bf16[128,512]{1,0:T(8,128)(2,1)S(1)}, u32[]{:S(2)}, u32[]{:S(2)}) collective-permute-start(bf16[128,512]{1,0:T(8,128)(2,1)S(1)} %get-tuple-element.96.g_own), channel_id=1, source_target_pairs={{0,12},{1,13},{2,14},{3,15},{4,8},{5,9},{6,10},{7,11},{8,4},{9,5},... | collective-permute-start | bytes 393224 | tf_op jit(solution)/shard_map/ppermute | solution.py:302
  109.2 23.4 %collective-permute-start.13 = (bf16[128,512]{1,0:T(8,128)(2,1)S(1)}, bf16[128,512]{1,0:T(8,128)(2,1)S(1)}, u32[]{:S(2)}, u32[]{:S(2)}) collective-permute-start(bf16[128,512]{1,0:T(8,128)(2,1)S(1)} %get-tuple-element.105), channel_id=1, source_target_pairs={{0,1},{1,0},{2,3},{3,2},{4,5},{5,4},{6,7},{7,6},{8,9},{9,8},{10,11... | collective-permute-start | bytes 393224 | tf_op jit(solution)/shard_map/ppermute | solution.py:302
  120.1 19.4 %collective-permute-start.12 = (bf16[128,512]{1,0:T(8,128)(2,1)S(1)}, bf16[128,512]{1,0:T(8,128)(2,1)S(1)}, u32[]{:S(2)}, u32[]{:S(2)}) collective-permute-start(bf16[128,512]{1,0:T(8,128)(2,1)S(1)} %get-tuple-element.98), channel_id=1, source_target_pairs={{0,1},{1,0},{2,3},{3,2},{4,5},{5,4},{6,7},{7,6},{8,9},{9,8},{10,11... | collective-permute-start | bytes 393224 | tf_op jit(solution)/shard_map/ppermute | solution.py:302
  132.7 6.0 %copy-start.10 = (s32[4096,2]{0,1:T(2,128)S(1)}, s32[4096,2]{0,1:T(2,128)}, u32[]{:S(2)}) copy-start(s32[4096,2]{0,1:T(2,128)} %param.19) | copy-start | bytes 98308
  132.7 16.8 %collective-permute-start.14 = (bf16[128,512]{1,0:T(8,128)(2,1)S(1)}, bf16[128,512]{1,0:T(8,128)(2,1)S(1)}, u32[]{:S(2)}, u32[]{:S(2)}) collective-permute-start(bf16[128,512]{1,0:T(8,128)(2,1)S(1)} %add_convert_fusion.1), channel_id=1, source_target_pairs={{0,3},{1,2},{2,1},{3,0},{4,7},{5,6},{6,5},{7,4},{8,11},{9,10},{10,... | collective-permute-start | bytes 393224 | tf_op jit(solution)/shard_map/ppermute | solution.py:302
  139.0 10.5 %copy-start.6 = (bf16[512,128]{1,0:T(8,128)(2,1)S(1)}, bf16[512,128]{1,0:T(8,128)(2,1)}, u32[]{:S(2)}) copy-start(bf16[512,128]{1,0:T(8,128)(2,1)} %gate.1) | copy-start | bytes 393220
